TPU v7x, 256 devices: a whole 4x4x8 slice. The times are simulated.
256 devices in a mesh: layer: 8 (over z_lo, x), dp: 32 (over z_hi, y, core).
Axes of the slice: x: 4, y: 4, z: 8 (z_hi: 4, z_lo: 2; z = z_hi * 2 + z_lo), core: 2. Of those that a mesh axis runs over, the one named last changes fastest.
Arguments:
- layer_inputs: bfloat16 [8, 8192, 5120], P('layer', 'dp'), may hold values from -6 to 6
- output_grads: bfloat16 [8, 8192, 13824], P('layer', 'dp'), may hold values from -6 to 6
- left_factors: bfloat16 [8, 32, 16, 13824], P('layer', 'dp'), may hold values from -0.0546875 to 0.0546875
- right_factors: bfloat16 [8, 32, 16, 5120], P('layer', 'dp'), may hold values from -0.078125 to 0.078125
- strengths: bfloat16 [8, 32, 16], P('layer', 'dp'), may hold values from 0.25 to 4
- train_ids: int32 [8192], P('dp'), may hold values from 0 to 100351
- query_ids: int32 [32, 64], replicated, may hold values from 0 to 100351
Outputs:
- token_scores: float32 [32, 8192], P('layer', 'dp')
- intersection: float32 [32, 4], P('layer')
All inputs are finite; a program needn't handle non-finite values.
Results may differ from a plain program's by a relative error of at most 0.0003.
Values may be sent and summed in bfloat16 or wider, within the bound.
No kernel may reach another device: no remote copies, remote signals or barrier semaphores. Data moves between devices by JAX's collectives and lax.ppermute only.
A program may use at most 128 MiB of HBM per device.

v0:
```python
import math

import jax
import jax.numpy as jnp
from jax import lax
from jax.sharding import PartitionSpec as P

SEQ_LEN = 2048


def local(layer_inputs, output_grads, left_factors, right_factors, strengths, train_ids, query_ids):
    activations = layer_inputs[0]
    gradients = output_grads[0]
    token_count = activations.shape[0]
    local_queries = left_factors.shape[1]
    rank_count = left_factors.shape[2]
    layer_count = lax.axis_size("layer")
    shard_count = lax.axis_size("dp")
    query_count = local_queries * shard_count
    scaling = 1.0 / math.sqrt(rank_count * layer_count)

    def project(source, factors):
        flattened = factors[0].reshape(factors.shape[1] * rank_count, factors.shape[3])
        return lax.dot_general(
            source, flattened, (((1,), (1,)), ((), ())), preferred_element_type=jnp.float32
        )

    left_all, right_all, strength_all = (
        lax.all_gather(left_factors, "dp", axis=1, tiled=True),
        lax.all_gather(right_factors, "dp", axis=1, tiled=True),
        lax.all_gather(strengths, "dp", axis=1, tiled=True),
    )
    weights_row = strength_all[0].reshape(1, query_count * rank_count).astype(jnp.float32)
    weighted = project(gradients, left_all) * project(activations, right_all) * weights_row
    layer_scores = weighted.reshape(token_count, query_count, rank_count).sum(axis=2).T * scaling
    own_scores = lax.psum_scatter(layer_scores, "layer", scatter_dimension=0, tiled=True)
    own_rows = query_count // layer_count
    layer_index = lax.axis_index("layer")
    seq_count = token_count * shard_count // SEQ_LEN
    seq_index = lax.axis_index("dp") * token_count // SEQ_LEN
    columns = (jnp.arange(seq_count, dtype=jnp.int32) == seq_index).astype(jnp.float32)
    norm_factor = 1.0 / math.sqrt(SEQ_LEN)
    own_ids = lax.dynamic_slice_in_dim(query_ids, layer_index * own_rows, own_rows, 0)
    matches = jnp.any(own_ids[:, :, None] == train_ids[None, None, :], axis=1).astype(jnp.float32)
    seq_part = jnp.sum(own_scores * matches, axis=1) * norm_factor
    intersection = lax.psum(seq_part[:, None] * columns[None, :], "dp")
    return (own_scores, intersection)


def solution(mesh):
    return jax.shard_map(
        local,
        mesh=mesh,
        in_specs=(
            P("layer", "dp", None),
            P("layer", "dp", None),
            P("layer", "dp", None, None),
            P("layer", "dp", None, None),
            P("layer", "dp", None),
            P("dp"),
            P(),
        ),
        out_specs=(P("layer", "dp"), P("layer", None)),
        check_vma=False,
    )
```

profile of v0, /device:TPU:1, one launch (start us, length us, event | category | flops | bytes accessed | tf_op | source)
XLA Modules:
  0.0 311.0 jit_solution(14287703911180811215)
XLA Ops:
  7.2 0.0 copy-start
  7.2 0.0 all-gather.5.cloned.1.call-start
  7.2 0.7 all-gather.5.cloned.1.call-update
  7.9 0.0 all-gather.3.cloned.1.call-start
  8.0 0.7 all-gather.3.cloned.1.call-update
  8.7 49.1 %all_gather.11 = bf16[1,32,16]{2,0,1:T(2,128)(2,1)S(1)} all-gather(bf16[1,1,16]{2,0,1:T(2,128)(2,1)} %bitcast.24), channel_id=1, replica_groups=mesh['layer'=8,'dp'=32] {'dp'}, dimensions={1}, use_global_device_ids=true | all-gather | bytes 1056 | tf_op jit(solution)/shard_map/all_gather | solution.py:31
  57.8 0.1 convert_reduce_fusion
  57.8 0.1 reshape.27
  57.9 1.3 dynamic-slice
  59.8 0.7 constant_dynamic-slice_fusion.1
  60.5 0.8 compare_reduce_fusion
  61.3 18.0 %all-gather.5.cloned.1.call-done = bf16[1,32,16,5120]{3,2,0,1:T(8,128)(2,1)} async-done(((bf16[1,1,16,5120]{3,2,0,1:T(8,128)(2,1)}), bf16[1,32,16,5120]{3,2,0,1:T(8,128)(2,1)}) %all-gather.5.cloned.1.call-update) | async-done | bytes 5242896 | tf_op jit(solution)/shard_map/all_gather | solution.py:30
  79.3 0.0 copy-done
  79.3 4.0 %fusion.2 = f32[256,512]{1,0:T(8,128)S(1)} fusion(bf16[512,5120]{1,0:T(8,128)(2,1)} %bitcast.26, bf16[1,256,5120]{2,1,0:T(8,128)(2,1)S(1)} %copy-done), kind=kOutput, calls=%fused_computation.2 | convolution fusion | flops 1342177280 | bytes 8388608 | tf_op jit(solution)/shard_map/dot_general | solution.py:24
  83.4 93.0 %all-gather.3.cloned.1.call-done = bf16[1,32,16,13824]{3,2,0,1:T(8,128)(2,1)} async-done(((bf16[1,1,16,13824]{3,2,0,1:T(8,128)(2,1)}), bf16[1,32,16,13824]{3,2,0,1:T(8,128)(2,1)}) %all-gather.3.cloned.1.call-update) | async-done | bytes 14155792 | tf_op jit(solution)/shard_map/all_gather | solution.py:29
  176.4 11.7 %fusion.7 = f32[256,512]{1,0:T(8,128)} fusion(f32[256,512]{1,0:T(8,128)S(1)} %fusion.2, bf16[512,13824]{1,0:T(8,128)(2,1)} %bitcast.25, bf16[1,256,13824]{2,1,0:T(8,128)(2,1)} %param.8, f32[512]{0:T(512)S(1)} %reshape.27), kind=kOutput, calls=%fused_computation.5 | convolution fusion | flops 3624140800 | bytes 22284288 | tf_op jit(solution)/shard_map/dot_general | solution.py:24
  188.0 1.2 copy.17
  189.3 0.1 bitcast_reduce_fusion
  189.4 37.0 %all-reduce = f32[32,256]{1,0:T(8,128)S(1)} all-reduce(f32[32,256]{1,0:T(8,128)S(1)} %multiply_bitcast_fusion), channel_id=2, replica_groups=mesh['layer'=8,'dp'=32] {'layer'}, use_global_device_ids=true, to_apply=%region_1.0.clone | all-reduce | flops 8192 | bytes 65536
  226.4 0.7 select_reduce_fusion
  227.1 0.1 broadcast_multiply_fusion
  227.2 77.0 %psum.7 = f32[4,4]{1,0:T(4,128)} all-reduce(f32[4,4]{1,0:T(4,128)S(1)} %broadcast_multiply_fusion), channel_id=1, replica_groups=mesh['layer'=8,'dp'=32] {'dp'}, use_global_device_ids=true, to_apply=%region_4.5 | all-reduce | flops 16 | bytes 128 | tf_op jit(solution)/shard_map/psum | solution.py:46
  (3 shorter events, 0.0 us)
Async XLA Ops:
  7.2 72.2 %copy-start = (bf16[1,256,5120]{2,1,0:T(8,128)(2,1)S(1)}, bf16[1,256,5120]{2,1,0:T(8,128)(2,1)}, u32[]{:S(2)}) copy-start(bf16[1,256,5120]{2,1,0:T(8,128)(2,1)} %param.7) | copy-start | bytes 7864324
  7.2 72.1 %all-gather.5.cloned.1.call-start = ((), (), s32[]{:S(2)}) async-start(), calls=%async_computation.1 | async-start | bytes 5406720 | tf_op jit(solution)/shard_map/all_gather | solution.py:30
  7.9 168.4 %all-gather.3.cloned.1.call-start = ((), (), s32[]{:S(2)}) async-start(), calls=%async_computation | async-start | bytes 14598144 | tf_op jit(solution)/shard_map/all_gather | solution.py:29
Sparse Core Ops, SparseCore 0:
  10.6 68.7 all-gather.4
  81.9 94.4 all-gather.2
where the time goes:
time: 311 us
  blocking collectives  163 us (52%)
  waiting for transfers between devices  112 us (36%)
  matrix products  15.7 us (5%)
  between operations  14.8 us (5%)
  local copies, waits for them, and re-layouts  3.29 us (1%)
    all_gather x1, waiting for transfers between devices, local(): lax.all_gather(left_factors, 'dp', axis=1, tiled=True)  93 us
    psum x1, blocking collectives, local(): intersection = lax.psum(seq_part[:, None] * columns[None, :], 'dp')  77 us
    all_gather x1, blocking collectives, local(): lax.all_gather(strengths, 'dp', axis=1, tiled=True)  49.1 us
    unnamed x1, blocking collectives  37 us
    all_gather x1, waiting for transfers between devices, local(): lax.all_gather(right_factors, 'dp', axis=1, tiled=True)  18 us
    dot_general x2, matrix products, project(): lax.dot_general(source, flattened, (((1,), (1,)), ((), ())), preferred_el...  15.7 us
  transfers between devices with their start and end apart: 2, of which 2 were waited for; matrix products, arithmetic and copies ran while one was open for 2% of the time, Pallas kernels for 0%

commit v1 on v0

v1 whole, which is shorter than its diff:
```python
import math

import jax
import jax.numpy as jnp
from jax import lax
from jax.sharding import Mesh, PartitionSpec as P

SEQ_LEN = 2048
NZ, NY, NC = 4, 4, 2
RING = ("z", "y", "c")


def ring_pairs(along_z):
    pairs = []
    for z in range(NZ):
        for y in range(NY):
            for c in range(NC):
                step = 1 - 2 * c
                to_z = (z + step) % NZ if along_z else z
                to_y = y if along_z else (y + step) % NY
                pairs.append(((z * NY + y) * NC + c, (to_z * NY + to_y) * NC + c))
    return pairs


def hop_y(x):
    return lax.ppermute(x, RING, ring_pairs(False))


def hop_z(x):
    return lax.ppermute(x, RING, ring_pairs(True))


def ring(x, hop, count):
    blocks = [x]
    for _ in range(count - 1):
        blocks.append(hop(blocks[-1]))
    return blocks


def swap(x):
    return lax.ppermute(x, "c", [(0, 1), (1, 0)])


def dot(factors, source):
    return lax.dot_general(
        factors, source, (((1,), (1,)), ((), ())), preferred_element_type=jnp.float32
    )


def local(layer_inputs, output_grads, left_factors, right_factors, strengths, train_ids, query_ids):
    acts, grads = layer_inputs[0], output_grads[0]
    left, right = left_factors[0, 0], right_factors[0, 0]
    rank, width = right.shape
    tokens = acts.shape[0]
    layers = lax.axis_size("layer")
    queries = query_ids.shape[0]
    z0, y0, c0 = lax.axis_index("z"), lax.axis_index("y"), lax.axis_index("c")
    layer_index = lax.axis_index("layer")

    right = jnp.concatenate(
        [right, jnp.broadcast_to(strengths[0, 0][:, None], (rank, 128))], axis=1
    )
    other_acts, other_grads = swap(acts), swap(grads)
    other_ids = swap(train_ids)

    right_y = ring(right, hop_y, NY)
    left_z = ring(left, hop_z, NZ)
    left_zy = [ring(block, hop_y, NY) for block in left_z]
    right_z = ring(jnp.concatenate(right_y, axis=0), hop_z, NZ)

    parts = []
    for i in range(NZ):
        left_rows = jnp.concatenate(left_zy[i], axis=0)
        right_rows = right_z[i][:, :width]
        weight = right_z[i][:, width : width + 1].astype(jnp.float32)
        halves = [
            dot(left_rows, g) * dot(right_rows, a) * weight
            for g, a in ((grads, acts), (other_grads, other_acts))
        ]
        both = jnp.concatenate(halves, axis=1)
        parts.append(both.reshape(NY, rank, 2 * tokens).sum(axis=1))
    scores = jnp.stack(parts) * (1.0 / math.sqrt(rank * layers))
    sign = 1 - 2 * c0
    zs, ys = jnp.arange(NZ), jnp.arange(NY)
    pick_z = (z0 - sign * zs) % NZ == zs[:, None]
    pick_y = (y0 - sign * ys) % NY == ys[:, None]
    scores = jnp.where(pick_z[:, :, None, None], scores[None], 0.0).sum(axis=1)
    scores = jnp.where(pick_y[None, :, :, None], scores[:, None], 0.0).sum(axis=2)
    scores = scores.reshape(layers, 2, 2, tokens)
    scores = jnp.where(c0 == 0, scores, scores[:, :, ::-1])
    sent = scores.transpose(0, 2, 1, 3).reshape(layers * NC, 2, tokens)
    got = lax.all_to_all(sent, ("layer", "c"), 0, 0, tiled=True)
    own_scores = got.reshape(layers, NC, 2, tokens).sum(axis=0)
    own_scores = own_scores.transpose(1, 0, 2).reshape(2 * NC, tokens)

    own_rows = queries // layers
    own_ids = lax.dynamic_slice_in_dim(query_ids, layer_index * own_rows, own_rows, 0)
    matches = jnp.any(own_ids[:, :, None] == train_ids[None, None, :], axis=1).astype(jnp.float32)
    seq_part = jnp.sum(own_scores * matches, axis=1) * (1.0 / math.sqrt(SEQ_LEN))
    sums = jnp.broadcast_to(seq_part[None, :, None], (NZ * NY * NC, own_rows, 128))
    sums = lax.all_to_all(sums, RING, 0, 0, tiled=True)[:, :, 0]
    intersection = sums.reshape(NZ, NY * NC, own_rows).sum(axis=1).T
    return (own_scores, intersection)


def solution(mesh):
    cut = Mesh(mesh.devices.reshape(-1, NZ, NY, NC), ("layer",) + RING)
    return jax.shard_map(
        local,
        mesh=cut,
        in_specs=(
            P("layer", RING, None),
            P("layer", RING, None),
            P("layer", RING, None, None),
            P("layer", RING, None, None),
            P("layer", RING, None),
            P(RING),
            P(),
        ),
        out_specs=(P("layer", RING), P("layer", None)),
        check_vma=False,
    )
```

time: 311 us -> 182 us (0.59)
  blocking collectives: 163 us -> 0 us
  starting transfers between devices: 0.08 us -> 54.7 us
  waiting for transfers between devices: 112 us -> 73.3 us
  matrix products: 15.7 us -> 45.5 us
  between operations: 14.8 us -> 0.99 us
    all_gather x2 -> x0, waiting for transfers between devices: 111 us -> none  [the longest x1 93 us: local(): lax.all_gather(left_factors, 'dp', axis=1, tiled=True)]
    psum x1 -> x0, blocking collectives: 77 us -> none  [local(): intersection = lax.psum(seq_part[:, None] * columns[None, :], 'dp')]
    ppermute x0 -> x23, waiting for transfers between devices: none -> 58.4 us  [the longest x6 37.9 us: hop_z(): return lax.ppermute(x, RING, ring_pairs(True))]
    all_gather x1 -> x0, blocking collectives: 49.1 us -> none  [local(): lax.all_gather(strengths, 'dp', axis=1, tiled=True)]
    unnamed x1 -> x0, blocking collectives: 37 us -> none
    ppermute x0 -> x23, starting transfers between devices: none -> 35.8 us  [the longest x6 17.8 us: hop_z(): return lax.ppermute(x, RING, ring_pairs(True))]
    dot_general x2 -> x16, matrix products: 15.7 us -> 45.5 us  [dot(): lax.dot_general(factors, source, (((1,), (1,)), ((), ())), preferred_elem...]
    all_to_all x0 -> x2, starting transfers between devices: none -> 18.9 us  [the longest x1 10.5 us: local(): sums = lax.all_to_all(sums, RING, 0, 0, tiled=True)[:, :, 0]]
  transfers between devices with their start and end apart: 2 -> 25, of which waited for: 2 -> 14; matrix products, arithmetic and copies ran while one was open for 2% -> 16% of each run, Pallas kernels for 0% -> 0%
where the time goes in v1:
time: 182 us
  waiting for transfers between devices  73.3 us (40%)
  starting transfers between devices  54.7 us (30%)
  matrix products  45.5 us (25%)
  other arithmetic  3.68 us (2%)
  local copies, waits for them, and re-layouts  3.61 us (2%)
    dot_general x16, matrix products, dot(): lax.dot_general(factors, source, (((1,), (1,)), ((), ())), preferred_elem...  45.5 us
    ppermute x6, waiting for transfers between devices, hop_z(): return lax.ppermute(x, RING, ring_pairs(True))  37.9 us
    ppermute x15, waiting for transfers between devices, hop_y(): return lax.ppermute(x, RING, ring_pairs(False))  20.5 us
    ppermute x6, starting transfers between devices, hop_z(): return lax.ppermute(x, RING, ring_pairs(True))  17.8 us
    ppermute x15, starting transfers between devices, hop_y(): return lax.ppermute(x, RING, ring_pairs(False))  17.4 us
    all_to_all x1, starting transfers between devices, local(): sums = lax.all_to_all(sums, RING, 0, 0, tiled=True)[:, :, 0]  10.5 us
    all_to_all x1, waiting for transfers between devices, local(): sums = lax.all_to_all(sums, RING, 0, 0, tiled=True)[:, :, 0]  9.19 us
    all_to_all x1, starting transfers between devices, local(): got = lax.all_to_all(sent, ('layer', 'c'), 0, 0, tiled=True)  8.39 us
  transfers between devices with their start and end apart: 25, of which 14 were waited for; matrix products, arithmetic and copies ran while one was open for 16% of the time, Pallas kernels for 0%

profile of v1, /device:TPU:1, one launch (start us, length us, event | category | flops | bytes accessed | tf_op | source)
XLA Modules:
  0.0 181.8 jit_solution(9106068071397707898)
XLA Ops:
  0.7 6.9 %collective-permute-start.8 = (bf16[16,13824]{1,0:T(8,128)(2,1)}, bf16[16,13824]{1,0:T(8,128)(2,1)S(1)}, u32[]{:S(2)}, u32[]{:S(2)}) collective-permute-start(bf16[16,13824]{1,0:T(8,128)(2,1)} %bitcast.70), channel_id=1, source_target_pairs={{0,8},{1,25},{2,10},{3,27},{4,12},{5,29},{6,14},{7,31},{8,16},{9,1... | collective-permute-start | bytes 1327112 | tf_op jit(solution)/shard_map/ppermute | solution.py:30
  7.6 2.7 %collective-permute-start = (bf16[16,13824]{1,0:T(8,128)(2,1)}, bf16[16,13824]{1,0:T(8,128)(2,1)}, u32[]{:S(2)}, u32[]{:S(2)}) collective-permute-start(bf16[16,13824]{1,0:T(8,128)(2,1)} %bitcast.71), channel_id=1, source_target_pairs={{0,2},{1,7},{2,4},{3,1},{4,6},{5,3},{6,0},{7,5},{8,10},{9,15},{10,... | collective-permute-start | bytes 1327112 | tf_op jit(solution)/shard_map/ppermute | solution.py:26
  13.1 4.5 %collective-permute-done.3 = bf16[16,5248]{1,0:T(8,128)(2,1)S(1)} collective-permute-done((bf16[16,5248]{1,0:T(8,128)(2,1)S(1)}, bf16[16,5248]{1,0:T(8,128)(2,1)S(1)}, u32[]{:S(2)}, u32[]{:S(2)}) %collective-permute-start.3) | collective-permute-done | bytes 167968 | tf_op jit(solution)/shard_map/ppermute | solution.py:26
  17.6 3.1 %collective-permute-start.4 = (bf16[16,5248]{1,0:T(8,128)(2,1)S(1)}, bf16[16,5248]{1,0:T(8,128)(2,1)S(1)}, u32[]{:S(2)}, u32[]{:S(2)}) collective-permute-start(bf16[16,5248]{1,0:T(8,128)(2,1)S(1)} %collective-permute-done.3), channel_id=1, source_target_pairs={{0,2},{1,7},{2,4},{3,1},{4,6},{5,3},{6,0},{7,5},{8,10},{9,15},{10,... | collective-permute-start | bytes 503816 | tf_op jit(solution)/shard_map/ppermute | solution.py:26
  23.0 3.1 %collective-permute-start.5 = (bf16[16,5248]{1,0:T(8,128)(2,1)S(1)}, bf16[16,5248]{1,0:T(8,128)(2,1)S(1)}, u32[]{:S(2)}, u32[]{:S(2)}) collective-permute-start(bf16[16,5248]{1,0:T(8,128)(2,1)S(1)} %collective-permute-done.4), channel_id=1, source_target_pairs={{0,2},{1,7},{2,4},{3,1},{4,6},{5,3},{6,0},{7,5},{8,10},{9,15},{10,... | collective-permute-start | bytes 503816 | tf_op jit(solution)/shard_map/ppermute | solution.py:26
  28.4 3.1 %collective-permute-start.1 = (bf16[16,13824]{1,0:T(8,128)(2,1)}, bf16[16,13824]{1,0:T(8,128)(2,1)S(1)}, u32[]{:S(2)}, u32[]{:S(2)}) collective-permute-start(bf16[16,13824]{1,0:T(8,128)(2,1)} %collective-permute-done), channel_id=1, source_target_pairs={{0,2},{1,7},{2,4},{3,1},{4,6},{5,3},{6,0},{7,5},{8,10},{9,15},{10,... | collective-permute-start | bytes 1327112 | tf_op jit(solution)/shard_map/ppermute | solution.py:26
  33.5 4.5 %collective-permute-done.13 = bf16[16,13824]{1,0:T(8,128)(2,1)S(1)} collective-permute-done((bf16[16,13824]{1,0:T(8,128)(2,1)S(1)}, bf16[16,13824]{1,0:T(8,128)(2,1)S(1)}, u32[]{:S(2)}, u32[]{:S(2)}) %collective-permute-start.13) | collective-permute-done | bytes 442400 | tf_op jit(solution)/shard_map/ppermute | solution.py:30
  40.9 14.9 %collective-permute-done.12 = bf16[64,5248]{1,0:T(8,128)(2,1)S(1)} collective-permute-done((bf16[64,5248]{1,0:T(8,128)(2,1)S(1)}, bf16[64,5248]{1,0:T(8,128)(2,1)S(1)}, u32[]{:S(2)}, u32[]{:S(2)}) %collective-permute-start.12) | collective-permute-done | bytes 671776 | tf_op jit(solution)/shard_map/ppermute | solution.py:30
  57.0 8.7 %collective-permute-done.18 = bf16[16,13824]{1,0:T(8,128)(2,1)S(1)} collective-permute-done((bf16[16,13824]{1,0:T(8,128)(2,1)S(1)}, bf16[16,13824]{1,0:T(8,128)(2,1)S(1)}, u32[]{:S(2)}, u32[]{:S(2)}) %collective-permute-start.18) | collective-permute-done | bytes 442400 | tf_op jit(solution)/shard_map/ppermute | solution.py:30
  65.7 3.4 %collective-permute-start.17 = (bf16[64,5248]{1,0:T(8,128)(2,1)S(1)}, bf16[64,5248]{1,0:T(8,128)(2,1)S(1)}, u32[]{:S(2)}, u32[]{:S(2)}) collective-permute-start(bf16[64,5248]{1,0:T(8,128)(2,1)S(1)} %collective-permute-done.12), channel_id=1, source_target_pairs={{0,8},{1,25},{2,10},{3,27},{4,12},{5,29},{6,14},{7,31},{8,16},{9,1... | collective-permute-start | bytes 2015240 | tf_op jit(solution)/shard_map/ppermute | solution.py:30
  69.3 3.8 %collective-permute-done.2 = bf16[16,13824]{1,0:T(8,128)(2,1)S(1)} collective-permute-done((bf16[16,13824]{1,0:T(8,128)(2,1)S(1)}, bf16[16,13824]{1,0:T(8,128)(2,1)S(1)}, u32[]{:S(2)}, u32[]{:S(2)}) %collective-permute-start.2) | collective-permute-done | bytes 442400 | tf_op jit(solution)/shard_map/ppermute | solution.py:26
  74.4 3.3 %fusion.7 = f32[64,256]{1,0:T(8,128)S(1)} fusion(f32[64,256]{1,0:T(8,128)S(1)} %fusion.22, bf16[16,13824]{1,0:T(8,128)(2,1)S(1)} %collective-permute-done.2, bf16[16,13824]{1,0:T(8,128)(2,1)S(1)} %collective-permute-done.1, bf16[16,13824]{1,0:T(8,128)(2,1)} %collective-permute-done, bf16[16,13824]{1,0:T(8,128)(2,1)S(1)} %bitcast.72, ...), kind=kOutput, calls=%fused_computation.16 | convolution fusion | flops 460095488 | bytes 8978688 | tf_op jit(solution)/shard_map/dot_general | solution.py:45
  79.1 3.5 %collective-permute-done.15 = bf16[16,13824]{1,0:T(8,128)(2,1)S(1)} collective-permute-done((bf16[16,13824]{1,0:T(8,128)(2,1)S(1)}, bf16[16,13824]{1,0:T(8,128)(2,1)S(1)}, u32[]{:S(2)}, u32[]{:S(2)}) %collective-permute-start.15) | collective-permute-done | bytes 442400 | tf_op jit(solution)/shard_map/ppermute | solution.py:26
  83.6 3.8 %collective-permute-done.11 = bf16[16,13824]{1,0:T(8,128)(2,1)S(1)} collective-permute-done((bf16[16,13824]{1,0:T(8,128)(2,1)S(1)}, bf16[16,13824]{1,0:T(8,128)(2,1)S(1)}, u32[]{:S(2)}, u32[]{:S(2)}) %collective-permute-start.11) | collective-permute-done | bytes 442400 | tf_op jit(solution)/shard_map/ppermute | solution.py:26
  90.6 3.4 %collective-permute-start.22 = (bf16[64,5248]{1,0:T(8,128)(2,1)S(1)}, bf16[64,5248]{1,0:T(8,128)(2,1)S(1)}, u32[]{:S(2)}, u32[]{:S(2)}) collective-permute-start(bf16[64,5248]{1,0:T(8,128)(2,1)S(1)} %collective-permute-done.17), channel_id=1, source_target_pairs={{0,8},{1,25},{2,10},{3,27},{4,12},{5,29},{6,14},{7,31},{8,16},{9,1... | collective-permute-start | bytes 2015240 | tf_op jit(solution)/shard_map/ppermute | solution.py:30
  99.1 9.7 %collective-permute-done.22 = bf16[64,5248]{1,0:T(8,128)(2,1)S(1)} collective-permute-done((bf16[64,5248]{1,0:T(8,128)(2,1)S(1)}, bf16[64,5248]{1,0:T(8,128)(2,1)S(1)}, u32[]{:S(2)}, u32[]{:S(2)}) %collective-permute-start.22) | collective-permute-done | bytes 671776 | tf_op jit(solution)/shard_map/ppermute | solution.py:30
  122.9 5.4 %fusion.6 = f32[64,256]{1,0:T(8,128)S(1)} fusion(f32[64,256]{1,0:T(8,128)S(1)} %fusion.20, bf16[256,13824]{1,0:T(8,128)(2,1)} %collective-permute-done.6, bf16[16,13824]{1,0:T(8,128)(2,1)S(1)} %collective-permute-done.2, bf16[16,13824]{1,0:T(8,128)(2,1)S(1)} %collective-permute-done.1, bf16[16,13824]{1,0:T(8,128)(2,1)} %collective-permute-done, ...), kind=kOutput, calls=%fused_computation.14 | convolution fusion | flops 460095488 | bytes 8978688 | tf_op jit(solution)/shard_map/dot_general | solution.py:45
  128.3 5.2 %fusion.4 = f32[64,256]{1,0:T(8,128)S(1)} fusion(f32[64,256]{1,0:T(8,128)S(1)} %fusion.16, bf16[64,13824]{1,0:T(8,128)(2,1)S(1)} %constant_dynamic-update-slice_fusion, bf16[256,13824]{1,0:T(8,128)(2,1)} %collective-permute-done.6, f32[64]{0:T(128)S(1)} %convert_reduce_fusion.2), kind=kOutput, calls=%fused_computation.10 | convolution fusion | flops 453017600 | bytes 8978688 | tf_op jit(solution)/shard_map/dot_general | solution.py:45
  133.6 5.3 %fusion.2 = f32[64,256]{1,0:T(8,128)S(1)} fusion(f32[64,256]{1,0:T(8,128)S(1)} %fusion.12, bf16[64,13824]{1,0:T(8,128)(2,1)S(1)} %constant_dynamic-update-slice_fusion.4, bf16[256,13824]{1,0:T(8,128)(2,1)} %collective-permute-done.6, f32[64]{0:T(128)S(1)} %convert_reduce_fusion.1), kind=kOutput, calls=%fused_computation.6 | convolution fusion | flops 453017600 | bytes 8978688 | tf_op jit(solution)/shard_map/dot_general | solution.py:45
  138.9 5.3 %fusion = f32[64,256]{1,0:T(8,128)S(1)} fusion(f32[64,256]{1,0:T(8,128)S(1)} %fusion.8, bf16[64,13824]{1,0:T(8,128)(2,1)S(1)} %constant_dynamic-update-slice_fusion.8, bf16[256,13824]{1,0:T(8,128)(2,1)} %collective-permute-done.6, f32[64]{0:T(128)S(1)} %convert_reduce_fusion), kind=kOutput, calls=%fused_computation.2 | convolution fusion | flops 453017600 | bytes 8978688 | tf_op jit(solution)/shard_map/dot_general | solution.py:45
  145.4 8.4 %all-to-all-start = ((f32[16,2,256]{2,1,0:T(2,128)}), f32[16,2,256]{2,1,0:T(2,128)S(1)}, u32[]{:S(2)}, u32[]{:S(2)}) async-start(f32[16,2,256]{2,1,0:T(2,128)} %bitcast.14), calls=%async_computation | async-start | bytes 65536 | tf_op jit(solution)/shard_map/all_to_all | solution.py:92
  153.9 5.7 %all-to-all-done = f32[16,2,256]{2,1,0:T(2,128)S(1)} async-done(((f32[16,2,256]{2,1,0:T(2,128)}), f32[16,2,256]{2,1,0:T(2,128)S(1)}, u32[]{:S(2)}, u32[]{:S(2)}) %all-to-all-start) | async-done | bytes 32800 | tf_op jit(solution)/shard_map/all_to_all | solution.py:92
  160.6 10.5 %all-to-all-start.1 = ((f32[32,4,128]{2,1,0:T(4,128)}), f32[32,4,128]{2,1,0:T(4,128)S(1)}, u32[]{:S(2)}, u32[]{:S(2)}) async-start(f32[32,4,128]{2,1,0:T(4,128)} %broadcast_in_dim.68), calls=%async_computation.1 | async-start | bytes 131072 | tf_op jit(solution)/shard_map/all_to_all | solution.py:101
  171.7 9.2 %all-to-all-done.1 = f32[32,4,128]{2,1,0:T(4,128)S(1)} async-done(((f32[32,4,128]{2,1,0:T(4,128)}), f32[32,4,128]{2,1,0:T(4,128)S(1)}, u32[]{:S(2)}, u32[]{:S(2)}) %all-to-all-start.1) | async-done | bytes 65568 | tf_op jit(solution)/shard_map/all_to_all | solution.py:101
  (99 shorter events, 43.3 us)
Async XLA Ops:
  0.7 25.5 %collective-permute-start.8 = (bf16[16,13824]{1,0:T(8,128)(2,1)}, bf16[16,13824]{1,0:T(8,128)(2,1)S(1)}, u32[]{:S(2)}, u32[]{:S(2)}) collective-permute-start(bf16[16,13824]{1,0:T(8,128)(2,1)} %bitcast.70), channel_id=1, source_target_pairs={{0,8},{1,25},{2,10},{3,27},{4,12},{5,29},{6,14},{7,31},{8,16},{9,1... | collective-permute-start | bytes 1327112 | tf_op jit(solution)/shard_map/ppermute | solution.py:30
  7.6 19.9 %collective-permute-start = (bf16[16,13824]{1,0:T(8,128)(2,1)}, bf16[16,13824]{1,0:T(8,128)(2,1)}, u32[]{:S(2)}, u32[]{:S(2)}) collective-permute-start(bf16[16,13824]{1,0:T(8,128)(2,1)} %bitcast.71), channel_id=1, source_target_pairs={{0,2},{1,7},{2,4},{3,1},{4,6},{5,3},{6,0},{7,5},{8,10},{9,15},{10,... | collective-permute-start | bytes 1327112 | tf_op jit(solution)/shard_map/ppermute | solution.py:26
  12.0 5.6 %collective-permute-start.3 = (bf16[16,5248]{1,0:T(8,128)(2,1)S(1)}, bf16[16,5248]{1,0:T(8,128)(2,1)S(1)}, u32[]{:S(2)}, u32[]{:S(2)}) collective-permute-start(bf16[16,5248]{1,0:T(8,128)(2,1)S(1)} %pad_maximum_fusion.4), channel_id=1, source_target_pairs={{0,2},{1,7},{2,4},{3,1},{4,6},{5,3},{6,0},{7,5},{8,10},{9,15},{10,... | collective-permute-start | bytes 503816 | tf_op jit(solution)/shard_map/ppermute | solution.py:26
  12.5 97.4 %collective-permute-start.7 = (bf16[256,5120]{1,0:T(8,128)(2,1)}, bf16[256,5120]{1,0:T(8,128)(2,1)}, u32[]{:S(2)}, u32[]{:S(2)}) collective-permute-start(bf16[256,5120]{1,0:T(8,128)(2,1)} %bitcast.58), channel_id=1, source_target_pairs={{0,1},{1,0},{2,3},{3,2},{4,5},{5,4},{6,7},{7,6},{8,9},{9,8},{10,11... | collective-permute-start | bytes 7864328 | tf_op jit(solution)/shard_map/ppermute | solution.py:41
  12.5 110.4 %collective-permute-start.6 = (bf16[256,13824]{1,0:T(8,128)(2,1)}, bf16[256,13824]{1,0:T(8,128)(2,1)}, u32[]{:S(2)}, u32[]{:S(2)}) collective-permute-start(bf16[256,13824]{1,0:T(8,128)(2,1)} %bitcast.57), channel_id=1, source_target_pairs={{0,1},{1,0},{2,3},{3,2},{4,5},{5,4},{6,7},{7,6},{8,9},{9,8},{10,11... | collective-permute-start | bytes 21233672 | tf_op jit(solution)/shard_map/ppermute | solution.py:41
  23.0 5.4 %collective-permute-start.5 = (bf16[16,5248]{1,0:T(8,128)(2,1)S(1)}, bf16[16,5248]{1,0:T(8,128)(2,1)S(1)}, u32[]{:S(2)}, u32[]{:S(2)}) collective-permute-start(bf16[16,5248]{1,0:T(8,128)(2,1)S(1)} %collective-permute-done.4), channel_id=1, source_target_pairs={{0,2},{1,7},{2,4},{3,1},{4,6},{5,3},{6,0},{7,5},{8,10},{9,15},{10,... | collective-permute-start | bytes 503816 | tf_op jit(solution)/shard_map/ppermute | solution.py:26
  26.1 11.9 %collective-permute-start.13 = (bf16[16,13824]{1,0:T(8,128)(2,1)S(1)}, bf16[16,13824]{1,0:T(8,128)(2,1)S(1)}, u32[]{:S(2)}, u32[]{:S(2)}) collective-permute-start(bf16[16,13824]{1,0:T(8,128)(2,1)S(1)} %collective-permute-done.8), channel_id=1, source_target_pairs={{0,8},{1,25},{2,10},{3,27},{4,12},{5,29},{6,14},{7,31},{8,16},{9,1... | collective-permute-start | bytes 1327112 | tf_op jit(solution)/shard_map/ppermute | solution.py:30
  27.5 13.2 %collective-permute-start.9 = (bf16[16,13824]{1,0:T(8,128)(2,1)S(1)}, bf16[16,13824]{1,0:T(8,128)(2,1)S(1)}, u32[]{:S(2)}, u32[]{:S(2)}) collective-permute-start(bf16[16,13824]{1,0:T(8,128)(2,1)S(1)} %collective-permute-done.8), channel_id=1, source_target_pairs={{0,2},{1,7},{2,4},{3,1},{4,6},{5,3},{6,0},{7,5},{8,10},{9,15},{10,... | collective-permute-start | bytes 1327112 | tf_op jit(solution)/shard_map/ppermute | solution.py:26
  28.4 28.4 %collective-permute-start.1 = (bf16[16,13824]{1,0:T(8,128)(2,1)}, bf16[16,13824]{1,0:T(8,128)(2,1)S(1)}, u32[]{:S(2)}, u32[]{:S(2)}) collective-permute-start(bf16[16,13824]{1,0:T(8,128)(2,1)} %collective-permute-done), channel_id=1, source_target_pairs={{0,2},{1,7},{2,4},{3,1},{4,6},{5,3},{6,0},{7,5},{8,10},{9,15},{10,... | collective-permute-start | bytes 1327112 | tf_op jit(solution)/shard_map/ppermute | solution.py:26
  38.1 17.7 %collective-permute-start.12 = (bf16[64,5248]{1,0:T(8,128)(2,1)S(1)}, bf16[64,5248]{1,0:T(8,128)(2,1)S(1)}, u32[]{:S(2)}, u32[]{:S(2)}) collective-permute-start(bf16[64,5248]{1,0:T(8,128)(2,1)S(1)} %pad_maximum_fusion.1), channel_id=1, source_target_pairs={{0,8},{1,25},{2,10},{3,27},{4,12},{5,29},{6,14},{7,31},{8,16},{9,1... | collective-permute-start | bytes 2015240 | tf_op jit(solution)/shard_map/ppermute | solution.py:30
  40.7 25.0 %collective-permute-start.18 = (bf16[16,13824]{1,0:T(8,128)(2,1)S(1)}, bf16[16,13824]{1,0:T(8,128)(2,1)S(1)}, u32[]{:S(2)}, u32[]{:S(2)}) collective-permute-start(bf16[16,13824]{1,0:T(8,128)(2,1)S(1)} %collective-permute-done.13), channel_id=1, source_target_pairs={{0,8},{1,25},{2,10},{3,27},{4,12},{5,29},{6,14},{7,31},{8,16},{9,1... | collective-permute-start | bytes 1327112 | tf_op jit(solution)/shard_map/ppermute | solution.py:30
  55.8 9.9 %collective-permute-start.14 = (bf16[16,13824]{1,0:T(8,128)(2,1)S(1)}, bf16[16,13824]{1,0:T(8,128)(2,1)S(1)}, u32[]{:S(2)}, u32[]{:S(2)}) collective-permute-start(bf16[16,13824]{1,0:T(8,128)(2,1)S(1)} %collective-permute-done.13), channel_id=1, source_target_pairs={{0,2},{1,7},{2,4},{3,1},{4,6},{5,3},{6,0},{7,5},{8,10},{9,15},{10,... | collective-permute-start | bytes 1327112 | tf_op jit(solution)/shard_map/ppermute | solution.py:26
  56.9 12.3 %collective-permute-start.10 = (bf16[16,13824]{1,0:T(8,128)(2,1)S(1)}, bf16[16,13824]{1,0:T(8,128)(2,1)S(1)}, u32[]{:S(2)}, u32[]{:S(2)}) collective-permute-start(bf16[16,13824]{1,0:T(8,128)(2,1)S(1)} %collective-permute-done.9), channel_id=1, source_target_pairs={{0,2},{1,7},{2,4},{3,1},{4,6},{5,3},{6,0},{7,5},{8,10},{9,15},{10,... | collective-permute-start | bytes 1327112 | tf_op jit(solution)/shard_map/ppermute | solution.py:26
  65.7 7.4 %collective-permute-start.2 = (bf16[16,13824]{1,0:T(8,128)(2,1)S(1)}, bf16[16,13824]{1,0:T(8,128)(2,1)S(1)}, u32[]{:S(2)}, u32[]{:S(2)}) collective-permute-start(bf16[16,13824]{1,0:T(8,128)(2,1)S(1)} %collective-permute-done.1), channel_id=1, source_target_pairs={{0,2},{1,7},{2,4},{3,1},{4,6},{5,3},{6,0},{7,5},{8,10},{9,15},{10,... | collective-permute-start | bytes 1327112 | tf_op jit(solution)/shard_map/ppermute | solution.py:26
  65.7 24.8 %collective-permute-start.17 = (bf16[64,5248]{1,0:T(8,128)(2,1)S(1)}, bf16[64,5248]{1,0:T(8,128)(2,1)S(1)}, u32[]{:S(2)}, u32[]{:S(2)}) collective-permute-start(bf16[64,5248]{1,0:T(8,128)(2,1)S(1)} %collective-permute-done.12), channel_id=1, source_target_pairs={{0,8},{1,25},{2,10},{3,27},{4,12},{5,29},{6,14},{7,31},{8,16},{9,1... | collective-permute-start | bytes 2015240 | tf_op jit(solution)/shard_map/ppermute | solution.py:30
  69.2 8.7 %collective-permute-start.19 = (bf16[16,13824]{1,0:T(8,128)(2,1)S(1)}, bf16[16,13824]{1,0:T(8,128)(2,1)S(1)}, u32[]{:S(2)}, u32[]{:S(2)}) collective-permute-start(bf16[16,13824]{1,0:T(8,128)(2,1)S(1)} %collective-permute-done.18), channel_id=1, source_target_pairs={{0,2},{1,7},{2,4},{3,1},{4,6},{5,3},{6,0},{7,5},{8,10},{9,15},{10,... | collective-permute-start | bytes 1327112 | tf_op jit(solution)/shard_map/ppermute | solution.py:26
  73.1 9.5 %collective-permute-start.15 = (bf16[16,13824]{1,0:T(8,128)(2,1)S(1)}, bf16[16,13824]{1,0:T(8,128)(2,1)S(1)}, u32[]{:S(2)}, u32[]{:S(2)}) collective-permute-start(bf16[16,13824]{1,0:T(8,128)(2,1)S(1)} %collective-permute-done.14), channel_id=1, source_target_pairs={{0,2},{1,7},{2,4},{3,1},{4,6},{5,3},{6,0},{7,5},{8,10},{9,15},{10,... | collective-permute-start | bytes 1327112 | tf_op jit(solution)/shard_map/ppermute | solution.py:26
  77.9 9.5 %collective-permute-start.11 = (bf16[16,13824]{1,0:T(8,128)(2,1)S(1)}, bf16[16,13824]{1,0:T(8,128)(2,1)S(1)}, u32[]{:S(2)}, u32[]{:S(2)}) collective-permute-start(bf16[16,13824]{1,0:T(8,128)(2,1)S(1)} %collective-permute-done.10), channel_id=1, source_target_pairs={{0,2},{1,7},{2,4},{3,1},{4,6},{5,3},{6,0},{7,5},{8,10},{9,15},{10,... | collective-permute-start | bytes 1327112 | tf_op jit(solution)/shard_map/ppermute | solution.py:26
  82.6 12.4 %collective-permute-start.20 = (bf16[16,13824]{1,0:T(8,128)(2,1)S(1)}, bf16[16,13824]{1,0:T(8,128)(2,1)S(1)}, u32[]{:S(2)}, u32[]{:S(2)}) collective-permute-start(bf16[16,13824]{1,0:T(8,128)(2,1)S(1)} %collective-permute-done.19), channel_id=1, source_target_pairs={{0,2},{1,7},{2,4},{3,1},{4,6},{5,3},{6,0},{7,5},{8,10},{9,15},{10,... | collective-permute-start | bytes 1327112 | tf_op jit(solution)/shard_map/ppermute | solution.py:26
  87.4 9.5 %collective-permute-start.16 = (bf16[16,13824]{1,0:T(8,128)(2,1)S(1)}, bf16[16,13824]{1,0:T(8,128)(2,1)S(1)}, u32[]{:S(2)}, u32[]{:S(2)}) collective-permute-start(bf16[16,13824]{1,0:T(8,128)(2,1)S(1)} %collective-permute-done.15), channel_id=1, source_target_pairs={{0,2},{1,7},{2,4},{3,1},{4,6},{5,3},{6,0},{7,5},{8,10},{9,15},{10,... | collective-permute-start | bytes 1327112 | tf_op jit(solution)/shard_map/ppermute | solution.py:26
  90.6 18.3 %collective-permute-start.22 = (bf16[64,5248]{1,0:T(8,128)(2,1)S(1)}, bf16[64,5248]{1,0:T(8,128)(2,1)S(1)}, u32[]{:S(2)}, u32[]{:S(2)}) collective-permute-start(bf16[64,5248]{1,0:T(8,128)(2,1)S(1)} %collective-permute-done.17), channel_id=1, source_target_pairs={{0,8},{1,25},{2,10},{3,27},{4,12},{5,29},{6,14},{7,31},{8,16},{9,1... | collective-permute-start | bytes 2015240 | tf_op jit(solution)/shard_map/ppermute | solution.py:30
  95.0 25.6 %collective-permute-start.21 = (bf16[16,13824]{1,0:T(8,128)(2,1)S(1)}, bf16[16,13824]{1,0:T(8,128)(2,1)S(1)}, u32[]{:S(2)}, u32[]{:S(2)}) collective-permute-start(bf16[16,13824]{1,0:T(8,128)(2,1)S(1)} %collective-permute-done.20), channel_id=1, source_target_pairs={{0,2},{1,7},{2,4},{3,1},{4,6},{5,3},{6,0},{7,5},{8,10},{9,15},{10,... | collective-permute-start | bytes 1327112 | tf_op jit(solution)/shard_map/ppermute | solution.py:26
  145.4 14.2 %all-to-all-start = ((f32[16,2,256]{2,1,0:T(2,128)}), f32[16,2,256]{2,1,0:T(2,128)S(1)}, u32[]{:S(2)}, u32[]{:S(2)}) async-start(f32[16,2,256]{2,1,0:T(2,128)} %bitcast.14), calls=%async_computation | async-start | bytes 65536 | tf_op jit(solution)/shard_map/all_to_all | solution.py:92
  160.6 20.3 %all-to-all-start.1 = ((f32[32,4,128]{2,1,0:T(4,128)}), f32[32,4,128]{2,1,0:T(4,128)S(1)}, u32[]{:S(2)}, u32[]{:S(2)}) async-start(f32[32,4,128]{2,1,0:T(4,128)} %broadcast_in_dim.68), calls=%async_computation.1 | async-start | bytes 131072 | tf_op jit(solution)/shard_map/all_to_all | solution.py:101
  (6 other events, 123.6 us)

commit v2 on v1

v2 whole, which is shorter than its diff:
```python
import math

import jax
import jax.numpy as jnp
from jax import lax
from jax.experimental import pallas as pl
from jax.experimental.pallas import tpu as pltpu
from jax.sharding import Mesh, PartitionSpec as P

SEQ_LEN = 2048
NZ, NY, NC = 4, 4, 2
RING = ("z", "y", "c")
VMEM = 12 << 20
PLAN = (
    "y01", "ga", "p1", "z1", "y02", "gg", "p3", "p2", "z2", "y12", "y03", "z3", "y21", "y31",
    "b1", "y23", "y32", "y22", "y11", "y13", "y33", "C0", "b2", "b3", "C1",
)
STEPS = (0, 1, -1, 2)


SOURCE = ("", "0", "0", "1")
WAY = (0, 1, -1, 1)


def pairs(along_z, way):
    out = []
    for z in range(NZ):
        for y in range(NY):
            for c in range(NC):
                step = way * (1 - 2 * c)
                to_z = (z + step) % NZ if along_z else z
                to_y = y if along_z else (y + step) % NY
                out.append(((z * NY + y) * NC + c, (to_z * NY + to_y) * NC + c))
    return out


def hop(x, along_z, way):
    return lax.ppermute(x, RING, pairs(along_z, way))


def swap(x):
    return lax.ppermute(x, "c", [(0, 1), (1, 0)])


def pack(right, strengths):
    rank, width = right.shape

    def kernel(right_ref, strength_ref, short_ref):
        short_ref[:, :width] = right_ref[...]
        row = jnp.broadcast_to(strength_ref[...].astype(jnp.float32), (rank, rank))
        eye = lax.broadcasted_iota(jnp.int32, (rank, rank), 0) == lax.broadcasted_iota(
            jnp.int32, (rank, rank), 1
        )
        column = jnp.sum(jnp.where(eye, row, 0.0), axis=1, keepdims=True)
        short_ref[:, width:] = jnp.broadcast_to(column, (rank, 128)).astype(right.dtype)

    return pl.pallas_call(
        kernel,
        out_shape=jax.ShapeDtypeStruct((rank, width + 128), right.dtype),
        name="pack",
    )(right, strengths)


def grad_part(blocks, sources):
    tokens, depth = sources[0].shape
    rows = sum(x.shape[0] for x in blocks)
    step = depth // 9

    def kernel(*refs):
        block_refs, rest = refs[: len(blocks)], refs[len(blocks) :]
        for s, out_ref in enumerate(rest[len(sources) :]):
            total = None
            for k in range(0, depth, step):
                factors = jnp.concatenate([r[:, k : k + step] for r in block_refs], axis=0)
                part = contract(rest[s][:, k : k + step], factors)
                total = part if total is None else total + part
            out_ref[...] = total

    return pl.pallas_call(
        kernel,
        out_shape=(jax.ShapeDtypeStruct((tokens, rows), jnp.float32),) * len(sources),
        name="grad_part",
        compiler_params=pltpu.CompilerParams(vmem_limit_bytes=VMEM),
    )(*blocks, *sources)


def score_part(bundles, sources, grad_parts, rank):
    tokens, depth = sources[0].shape
    rows = sum(x.shape[0] for x in bundles)
    step = depth // 4

    def kernel(*refs):
        bundle_refs, rest = refs[: len(bundles)], refs[len(bundles) : -1]
        out_ref = refs[-1]
        weight = jnp.concatenate([r[:, depth:] for r in bundle_refs], axis=0)
        weight = weight.astype(jnp.float32)[:, :1]
        for s in range(len(sources)):
            total = None
            for k in range(0, depth, step):
                factors = jnp.concatenate([r[:, k : k + step] for r in bundle_refs], axis=0)
                part = contract(rest[s][:, k : k + step], factors)
                total = part if total is None else total + part
            weighted = (total * rest[len(sources) + s][...]).T * weight
            mine = slice(s * tokens, (s + 1) * tokens)
            out_ref[:, mine] = weighted.reshape(rows // rank, rank, tokens).sum(axis=1)

    return pl.pallas_call(
        kernel,
        out_shape=jax.ShapeDtypeStruct((rows // rank, len(sources) * tokens), jnp.float32),
        name="score_part",
        compiler_params=pltpu.CompilerParams(vmem_limit_bytes=VMEM),
    )(*bundles, *sources, *grad_parts)


def contract(a, b):
    return lax.dot_general(a, b, (((1,), (1,)), ((), ())), preferred_element_type=jnp.float32)


def local(layer_inputs, output_grads, left_factors, right_factors, strengths, train_ids, query_ids):
    acts, grads = layer_inputs[0], output_grads[0]
    rank, high = left_factors.shape[2:]
    tokens = acts.shape[0]
    layers = lax.axis_size("layer")
    queries = query_ids.shape[0]
    z0, y0, c0 = lax.axis_index("z"), lax.axis_index("y"), lax.axis_index("c")
    layer_index = lax.axis_index("layer")

    long, short = left_factors[0, 0], pack(right_factors[0, 0], strengths[0])
    held = {"z0": long, "p0": short, "y00": long}
    last = None

    def start(task):
        if task[0] == "g":
            return swap(acts if task == "ga" else grads)
        count = int(task[-1])
        from_task = task[:-1] + SOURCE[count]
        if from_task not in held and task[0] == "b":
            held["b0"] = jnp.concatenate([held[f"p{j}"] for j in range(NY)], axis=0)
        return hop(held[from_task], task[0] in "zb", WAY[count])

    def compute(task):
        if task == "C0":
            blocks = [held[f"y{i}{j}"] for i in range(NZ) for j in range(NY)]
            return grad_part(blocks, [grads, held["gg"]])
        bundles = [held[f"b{i}"] for i in range(NZ)]
        return score_part(bundles, [acts, held["ga"]], held["C0"], rank)

    def after(x):
        return x if last is None else lax.optimization_barrier((x, last))[0]

    for task in PLAN:
        held[task] = last = compute(task) if task[0] == "C" else after(start(task))
        if task[0] == "z":
            held[f"y{task[1]}0"] = last
    scores = held["C1"].reshape(NZ, NY, -1)

    steps = jnp.array(STEPS, jnp.int32)
    way = 1 - 2 * c0
    pick_z = (z0 - way * steps) % NZ == jnp.arange(NZ)[:, None]
    pick_y = (y0 - way * steps) % NY == jnp.arange(NY)[:, None]
    scores = jnp.where(pick_z[:, :, None, None], scores[None], 0.0).sum(axis=1)
    scores = jnp.where(pick_y[None, :, :, None], scores[:, None], 0.0).sum(axis=2)
    scores = scores.reshape(layers, 2, NC, tokens) * (1.0 / math.sqrt(rank * layers))
    scores = jnp.where(c0 == 0, scores, scores[:, :, ::-1])
    sent = scores.transpose(0, 2, 1, 3).reshape(layers * NC, 2, tokens)
    got = lax.all_to_all(sent, ("layer", "c"), 0, 0, tiled=True)
    own_scores = got.reshape(layers, NC, 2, tokens).sum(axis=0)
    own_scores = own_scores.transpose(1, 0, 2).reshape(2 * NC, tokens)

    own_rows = queries // layers
    own_ids = lax.dynamic_slice_in_dim(query_ids, layer_index * own_rows, own_rows, 0)
    matches = jnp.any(own_ids[:, :, None] == train_ids[None, None, :], axis=1).astype(jnp.float32)
    seq_part = jnp.sum(own_scores * matches, axis=1) * (1.0 / math.sqrt(SEQ_LEN))
    sums = jnp.broadcast_to(seq_part[None, :, None], (NZ * NY * NC, own_rows, 128))
    sums = lax.all_to_all(sums, RING, 0, 0, tiled=True)[:, :, 0]
    intersection = sums.reshape(NZ, NY * NC, own_rows).sum(axis=1).T
    return (own_scores, intersection)


def solution(mesh):
    cut = Mesh(mesh.devices.reshape(-1, NZ, NY, NC), ("layer",) + RING)
    return jax.shard_map(
        local,
        mesh=cut,
        in_specs=(
            P("layer", RING, None),
            P("layer", RING, None),
            P("layer", RING, None, None),
            P("layer", RING, None, None),
            P("layer", RING, None),
            P(RING),
            P(),
        ),
        out_specs=(P("layer", RING), P("layer", None)),
        check_vma=False,
    )
```

time: 182 us -> 144 us (0.79)
  matrix products: 45.5 us -> 0 us
  waiting for transfers between devices: 73.3 us -> 45.9 us
  local copies, waits for them, and re-layouts: 3.61 us -> 16.6 us
  Pallas kernels: 0 us -> 12.8 us
  starting transfers between devices: 54.7 us -> 65.4 us
    dot_general x16 -> x0, matrix products: 45.5 us -> none  [dot(): lax.dot_general(factors, source, (((1,), (1,)), ((), ())), preferred_elem...]
    ppermute x21, waiting for transfers between devices: 58.4 us -> 29 us  [hop(): return lax.ppermute(x, RING, pairs(along_z, way))]
    unnamed x19 -> x36, local copies, waits for them, and re-layouts: 0.3 us -> 14 us
    pallas_call x0 -> x3, Pallas kernels: none -> 12.8 us  [the longest x1 7.92 us: grad_part(): pl.pallas_call(kernel, out_shape=(jax.ShapeDtypeStruct((tokens, rows), jn...]
    ppermute x21, starting transfers between devices: 35.3 us -> 47.5 us  [hop(): return lax.ppermute(x, RING, pairs(along_z, way))]
    all_to_all x1, starting transfers between devices: 10.5 us -> 4.84 us  [local(): sums = lax.all_to_all(sums, RING, 0, 0, tiled=True)[:, :, 0]]
    ppermute x2, starting transfers between devices: 0.51 us -> 3.43 us  [swap(): return lax.ppermute(x, 'c', [(0, 1), (1, 0)])]
    ppermute x2, waiting for transfers between devices: 0.01 us -> 2.07 us  [swap(): return lax.ppermute(x, 'c', [(0, 1), (1, 0)])]
  transfers between devices with their start and end apart: 25 -> 25, of which waited for: 14 -> 9; matrix products, arithmetic and copies ran while one was open for 16% -> 1% of each run, Pallas kernels for 0% -> 7%
where the time goes in v2:
time: 144 us
  starting transfers between devices  65.4 us (45%)
  waiting for transfers between devices  45.9 us (32%)
  local copies, waits for them, and re-layouts  16.6 us (12%)
  Pallas kernels  12.8 us (9%)
  other arithmetic  2.2 us (2%)
    ppermute x21, starting transfers between devices, hop(): return lax.ppermute(x, RING, pairs(along_z, way))  47.5 us
    ppermute x21, waiting for transfers between devices, hop(): return lax.ppermute(x, RING, pairs(along_z, way))  29 us
    unnamed x36, local copies, waits for them, and re-layouts  14 us
    all_to_all x1, starting transfers between devices, local(): got = lax.all_to_all(sent, ('layer', 'c'), 0, 0, tiled=True)  9.57 us
    all_to_all x1, waiting for transfers between devices, local(): sums = lax.all_to_all(sums, RING, 0, 0, tiled=True)[:, :, 0]  9.19 us
    pallas_call x1, Pallas kernels, grad_part(): pl.pallas_call(kernel, out_shape=(jax.ShapeDtypeStruct((tokens, rows), jn...  7.92 us
    all_to_all x1, waiting for transfers between devices, local(): got = lax.all_to_all(sent, ('layer', 'c'), 0, 0, tiled=True)  5.66 us
    all_to_all x1, starting transfers between devices, local(): sums = lax.all_to_all(sums, RING, 0, 0, tiled=True)[:, :, 0]  4.84 us
  transfers between devices with their start and end apart: 25, of which 9 were waited for; matrix products, arithmetic and copies ran while one was open for 1% of the time, Pallas kernels for 7%

profile of v2, /device:TPU:1, one launch (start us, length us, event | category | flops | bytes accessed | tf_op | source)
XLA Modules:
  0.0 143.6 jit_solution(2043755441822836773)
XLA Ops:
  0.7 3.3 %collective-permute-start.5 = (bf16[256,13824]{1,0:T(8,128)(2,1)}, bf16[256,13824]{1,0:T(8,128)(2,1)}, u32[]{:S(2)}, u32[]{:S(2)}) collective-permute-start(bf16[256,13824]{1,0:T(8,128)(2,1)} %bitcast.15), channel_id=1, source_target_pairs={{0,1},{1,0},{2,3},{3,2},{4,5},{5,4},{6,7},{7,6},{8,9},{9,8},{10,11... | collective-permute-start | bytes 21233672 | tf_op jit(solution)/shard_map/ppermute | solution.py:42
  5.1 6.0 %collective-permute-start.7 = (bf16[16,13824]{1,0:T(8,128)(2,1)}, bf16[16,13824]{1,0:T(8,128)(2,1)}, u32[]{:S(2)}, u32[]{:S(2)}) collective-permute-start(bf16[16,13824]{1,0:T(8,128)(2,1)} %bitcast.20), channel_id=1, source_target_pairs={{0,8},{1,25},{2,10},{3,27},{4,12},{5,29},{6,14},{7,31},{8,16},{9,1... | collective-permute-start | bytes 1327112 | tf_op jit(solution)/shard_map/ppermute | solution.py:38
  13.6 1.7 %pack.1 = bf16[16,5248]{1,0:T(8,128)(2,1)} custom-call(bf16[16,5120]{1,0:T(8,128)(2,1)} %bitcast.25, bf16[1,16]{1,0:T(2,128)(2,1)} %bitcast.29), custom_call_target="tpu_custom_call" | custom-call | tf_op jit(solution)/shard_map/pack/pallas_call | solution.py:57
  15.3 2.1 %collective-permute-done.1.refs_5_ = bf16[256,5120]{1,0:T(8,128)(2,1)S(1)} collective-permute-done((bf16[256,5120]{1,0:T(8,128)(2,1)}, bf16[256,5120]{1,0:T(8,128)(2,1)S(1)}, u32[]{:S(2)}, u32[]{:S(2)}) %collective-permute-start.1) | collective-permute-done | bytes 2621472 | tf_op jit(solution)/shard_map/ppermute | solution.py:42
  18.6 3.6 %collective-permute-done = bf16[16,5248]{1,0:T(8,128)(2,1)S(1)} collective-permute-done((bf16[16,5248]{1,0:T(8,128)(2,1)}, bf16[16,5248]{1,0:T(8,128)(2,1)S(1)}, u32[]{:S(2)}, u32[]{:S(2)}) %collective-permute-start) | collective-permute-done | bytes 167968 | tf_op jit(solution)/shard_map/ppermute | solution.py:38
  22.2 2.2 %collective-permute-start.4 = (bf16[16,5248]{1,0:T(8,128)(2,1)S(1)}, bf16[16,5248]{1,0:T(8,128)(2,1)S(1)}, u32[]{:S(2)}, u32[]{:S(2)}) collective-permute-start(bf16[16,5248]{1,0:T(8,128)(2,1)S(1)} %collective-permute-done), channel_id=1, source_target_pairs={{0,2},{1,7},{2,4},{3,1},{4,6},{5,3},{6,0},{7,5},{8,10},{9,15},{10,... | collective-permute-start | bytes 503816 | tf_op jit(solution)/shard_map/ppermute | solution.py:38
  25.2 2.7 %collective-permute-start.10 = (bf16[16,13824]{1,0:T(8,128)(2,1)}, bf16[16,13824]{1,0:T(8,128)(2,1)S(1)}, u32[]{:S(2)}, u32[]{:S(2)}) collective-permute-start(bf16[16,13824]{1,0:T(8,128)(2,1)} %collective-permute-done.2.refs_1_), channel_id=1, source_target_pairs={{0,2},{1,7},{2,4},{3,1},{4,6},{5,3},{6,0},{7,5},{8,10},{9,15},{10,... | collective-permute-start | bytes 1327112 | tf_op jit(solution)/shard_map/ppermute | solution.py:38
  27.9 7.0 %collective-permute-start.9 = (bf16[16,13824]{1,0:T(8,128)(2,1)}, bf16[16,13824]{1,0:T(8,128)(2,1)}, u32[]{:S(2)}, u32[]{:S(2)}) collective-permute-start(bf16[16,13824]{1,0:T(8,128)(2,1)} %collective-permute-done.7.refs_4_), channel_id=1, source_target_pairs={{0,8},{1,25},{2,10},{3,27},{4,12},{5,29},{6,14},{7,31},{8,16},{9,1... | collective-permute-start | bytes 1327112 | tf_op jit(solution)/shard_map/ppermute | solution.py:38
  34.9 2.6 %collective-permute-start.14 = (bf16[16,13824]{1,0:T(8,128)(2,1)}, bf16[16,13824]{1,0:T(8,128)(2,1)S(1)}, u32[]{:S(2)}, u32[]{:S(2)}) collective-permute-start(bf16[16,13824]{1,0:T(8,128)(2,1)} %collective-permute-done.12.refs_8_), channel_id=1, source_target_pairs={{0,2},{1,7},{2,4},{3,1},{4,6},{5,3},{6,0},{7,5},{8,10},{9,15},{10,... | collective-permute-start | bytes 1327112 | tf_op jit(solution)/shard_map/ppermute | solution.py:38
  38.5 2.3 %collective-permute-start.8 = (bf16[64,5248]{1,0:T(8,128)(2,1)S(1)}, bf16[64,5248]{1,0:T(8,128)(2,1)}, u32[]{:S(2)}, u32[]{:S(2)}) collective-permute-start(bf16[64,5248]{1,0:T(8,128)(2,1)S(1)} %pad_maximum_fusion.refs_0_), channel_id=1, source_target_pairs={{0,8},{1,25},{2,10},{3,27},{4,12},{5,29},{6,14},{7,31},{8,16},{9,1... | collective-permute-start | bytes 2015240 | tf_op jit(solution)/shard_map/ppermute | solution.py:38
  42.4 8.3 %collective-permute-done.9.refs_12_ = bf16[16,13824]{1,0:T(8,128)(2,1)} collective-permute-done((bf16[16,13824]{1,0:T(8,128)(2,1)}, bf16[16,13824]{1,0:T(8,128)(2,1)}, u32[]{:S(2)}, u32[]{:S(2)}) %collective-permute-start.9) | collective-permute-done | bytes 442400 | tf_op jit(solution)/shard_map/ppermute | solution.py:38
  50.7 4.1 %collective-permute-start.19 = (bf16[16,13824]{1,0:T(8,128)(2,1)S(1)}, bf16[16,13824]{1,0:T(8,128)(2,1)S(1)}, u32[]{:S(2)}, u32[]{:S(2)}) collective-permute-start(bf16[16,13824]{1,0:T(8,128)(2,1)S(1)} %collective-permute-done.14.refs_9_), channel_id=1, source_target_pairs={{0,2},{1,7},{2,4},{3,1},{4,6},{5,3},{6,0},{7,5},{8,10},{9,15},{10,... | collective-permute-start | bytes 1327112 | tf_op jit(solution)/shard_map/ppermute | solution.py:38
  55.5 3.6 %collective-permute-done.13.refs_13_ = bf16[16,13824]{1,0:T(8,128)(2,1)S(1)} collective-permute-done((bf16[16,13824]{1,0:T(8,128)(2,1)}, bf16[16,13824]{1,0:T(8,128)(2,1)S(1)}, u32[]{:S(2)}, u32[]{:S(2)}) %collective-permute-start.13) | collective-permute-done | bytes 442400 | tf_op jit(solution)/shard_map/ppermute | solution.py:38
  60.5 8.1 %collective-permute-start.15 = (bf16[64,5248]{1,0:T(8,128)(2,1)S(1)}, bf16[64,5248]{1,0:T(8,128)(2,1)}, u32[]{:S(2)}, u32[]{:S(2)}) collective-permute-start(bf16[64,5248]{1,0:T(8,128)(2,1)S(1)} %pad_maximum_fusion.refs_0_), channel_id=1, source_target_pairs={{0,24},{1,9},{2,26},{3,11},{4,28},{5,13},{6,30},{7,15},{8,0},{9,17... | collective-permute-start | bytes 2015240 | tf_op jit(solution)/shard_map/ppermute | solution.py:38
  69.4 7.3 %collective-permute-start.22 = (bf16[64,5248]{1,0:T(8,128)(2,1)}, bf16[64,5248]{1,0:T(8,128)(2,1)}, u32[]{:S(2)}, u32[]{:S(2)}) collective-permute-start(bf16[64,5248]{1,0:T(8,128)(2,1)} %collective-permute-done.8.refs_1_), channel_id=1, source_target_pairs={{0,8},{1,25},{2,10},{3,27},{4,12},{5,29},{6,14},{7,31},{8,16},{9,1... | collective-permute-start | bytes 2015240 | tf_op jit(solution)/shard_map/ppermute | solution.py:38
  76.8 2.0 %collective-permute-done.17.refs_10_ = bf16[16,13824]{1,0:T(8,128)(2,1)} collective-permute-done((bf16[16,13824]{1,0:T(8,128)(2,1)}, bf16[16,13824]{1,0:T(8,128)(2,1)}, u32[]{:S(2)}, u32[]{:S(2)}) %collective-permute-start.17) | collective-permute-done | bytes 442400 | tf_op jit(solution)/shard_map/ppermute | solution.py:38
  79.3 10.0 %collective-permute-done.20.refs_7_ = bf16[16,13824]{1,0:T(8,128)(2,1)S(1)} collective-permute-done((bf16[16,13824]{1,0:T(8,128)(2,1)}, bf16[16,13824]{1,0:T(8,128)(2,1)S(1)}, u32[]{:S(2)}, u32[]{:S(2)}) %collective-permute-start.20) | collective-permute-done | bytes 442400 | tf_op jit(solution)/shard_map/ppermute | solution.py:38
  89.3 3.0 %copy-done.1 = bf16[1,256,13824]{2,1,0:T(8,128)(2,1)S(1)} copy-done((bf16[1,256,13824]{2,1,0:T(8,128)(2,1)S(1)}, bf16[1,256,13824]{2,1,0:T(8,128)(2,1)}, u32[]{:S(2)}) %copy-start.1) | copy-done | bytes 7077912
  99.4 7.9 %grad_part.1 = (f32[256,256]{1,0:T(8,128)S(1)}, f32[256,256]{1,0:T(8,128)S(1)}) custom-call(bf16[16,13824]{1,0:T(8,128)(2,1)S(1)} %bitcast.23, bf16[16,13824]{1,0:T(8,128)(2,1)} %collective-permute-done.2.refs_1_, bf16[16,13824]{1,0:T(8,128)(2,1)S(1)} %copy-done.5, bf16[16,13824]{1,0:T(8,128)(2,1)S(1)} %copy-done.7, ...), custom_call_target="tpu_custom_call" | custom-call | tf_op jit(solution)/shard_map/grad_part/pallas_call | solution.py:79
  107.4 3.2 %score_part.1 = f32[16,512]{1,0:T(8,128)S(1)} custom-call(bf16[64,5248]{1,0:T(8,128)(2,1)S(1)} %pad_maximum_fusion.refs_0_, bf16[64,5248]{1,0:T(8,128)(2,1)} %collective-permute-done.8.refs_1_, bf16[64,5248]{1,0:T(8,128)(2,1)} %collective-permute-done.15.refs_2_, bf16[64,5248]{1,0:T(8,128)(2,1)} %collective-permute-done.22.refs_3_, ...), custom_call_target="tpu_custom_call" | custom-call | tf_op jit(solution)/shard_map/score_part/pallas_call | solution.py:107
  111.7 9.6 %all-to-all-start = ((f32[16,2,256]{2,1,0:T(2,128)}), f32[16,2,256]{2,1,0:T(2,128)S(1)}, u32[]{:S(2)}, u32[]{:S(2)}) async-start(f32[16,2,256]{2,1,0:T(2,128)} %bitcast.6), calls=%async_computation | async-start | bytes 65536 | tf_op jit(solution)/shard_map/all_to_all | solution.py:166
  121.4 5.7 %all-to-all-done = f32[16,2,256]{2,1,0:T(2,128)S(1)} async-done(((f32[16,2,256]{2,1,0:T(2,128)}), f32[16,2,256]{2,1,0:T(2,128)S(1)}, u32[]{:S(2)}, u32[]{:S(2)}) %all-to-all-start) | async-done | bytes 32800 | tf_op jit(solution)/shard_map/all_to_all | solution.py:166
  128.1 4.8 %all-to-all-start.1 = ((f32[32,4,128]{2,1,0:T(4,128)}), f32[32,4,128]{2,1,0:T(4,128)S(1)}, u32[]{:S(2)}, u32[]{:S(2)}) async-start(f32[32,4,128]{2,1,0:T(4,128)} %broadcast_in_dim.61), calls=%async_computation.1 | async-start | bytes 131072 | tf_op jit(solution)/shard_map/all_to_all | solution.py:175
  133.6 9.2 %all-to-all-done.1 = f32[32,4,128]{2,1,0:T(4,128)S(1)} async-done(((f32[32,4,128]{2,1,0:T(4,128)}), f32[32,4,128]{2,1,0:T(4,128)S(1)}, u32[]{:S(2)}, u32[]{:S(2)}) %all-to-all-start.1) | async-done | bytes 65568 | tf_op jit(solution)/shard_map/all_to_all | solution.py:175
  (89 shorter events, 22.6 us)
Async XLA Ops:
  0.7 27.2 %collective-permute-start.5 = (bf16[256,13824]{1,0:T(8,128)(2,1)}, bf16[256,13824]{1,0:T(8,128)(2,1)}, u32[]{:S(2)}, u32[]{:S(2)}) collective-permute-start(bf16[256,13824]{1,0:T(8,128)(2,1)} %bitcast.15), channel_id=1, source_target_pairs={{0,1},{1,0},{2,3},{3,2},{4,5},{5,4},{6,7},{7,6},{8,9},{9,8},{10,11... | collective-permute-start | bytes 21233672 | tf_op jit(solution)/shard_map/ppermute | solution.py:42
  4.0 13.4 %collective-permute-start.1 = (bf16[256,5120]{1,0:T(8,128)(2,1)}, bf16[256,5120]{1,0:T(8,128)(2,1)S(1)}, u32[]{:S(2)}, u32[]{:S(2)}) collective-permute-start(bf16[256,5120]{1,0:T(8,128)(2,1)} %bitcast.17), channel_id=1, source_target_pairs={{0,1},{1,0},{2,3},{3,2},{4,5},{5,4},{6,7},{7,6},{8,9},{9,8},{10,11... | collective-permute-start | bytes 7864328 | tf_op jit(solution)/shard_map/ppermute | solution.py:42
  4.1 8.5 %collective-permute-start.2 = (bf16[16,13824]{1,0:T(8,128)(2,1)}, bf16[16,13824]{1,0:T(8,128)(2,1)}, u32[]{:S(2)}, u32[]{:S(2)}) collective-permute-start(bf16[16,13824]{1,0:T(8,128)(2,1)} %bitcast.19), channel_id=1, source_target_pairs={{0,2},{1,7},{2,4},{3,1},{4,6},{5,3},{6,0},{7,5},{8,10},{9,15},{10,... | collective-permute-start | bytes 1327112 | tf_op jit(solution)/shard_map/ppermute | solution.py:38
  5.1 19.3 %collective-permute-start.7 = (bf16[16,13824]{1,0:T(8,128)(2,1)}, bf16[16,13824]{1,0:T(8,128)(2,1)}, u32[]{:S(2)}, u32[]{:S(2)}) collective-permute-start(bf16[16,13824]{1,0:T(8,128)(2,1)} %bitcast.20), channel_id=1, source_target_pairs={{0,8},{1,25},{2,10},{3,27},{4,12},{5,29},{6,14},{7,31},{8,16},{9,1... | collective-permute-start | bytes 1327112 | tf_op jit(solution)/shard_map/ppermute | solution.py:38
  11.1 13.3 %collective-permute-start.6 = (bf16[16,13824]{1,0:T(8,128)(2,1)}, bf16[16,13824]{1,0:T(8,128)(2,1)S(1)}, u32[]{:S(2)}, u32[]{:S(2)}) collective-permute-start(bf16[16,13824]{1,0:T(8,128)(2,1)} %bitcast.21), channel_id=1, source_target_pairs={{0,6},{1,3},{2,0},{3,5},{4,2},{5,7},{6,4},{7,1},{8,14},{9,11},{10,... | collective-permute-start | bytes 1327112 | tf_op jit(solution)/shard_map/ppermute | solution.py:38
  12.5 22.3 %collective-permute-start.12 = (bf16[16,13824]{1,0:T(8,128)(2,1)}, bf16[16,13824]{1,0:T(8,128)(2,1)}, u32[]{:S(2)}, u32[]{:S(2)}) collective-permute-start(bf16[16,13824]{1,0:T(8,128)(2,1)} %bitcast.22), channel_id=1, source_target_pairs={{0,24},{1,9},{2,26},{3,11},{4,28},{5,13},{6,30},{7,15},{8,0},{9,17... | collective-permute-start | bytes 1327112 | tf_op jit(solution)/shard_map/ppermute | solution.py:38
  22.2 5.7 %collective-permute-start.4 = (bf16[16,5248]{1,0:T(8,128)(2,1)S(1)}, bf16[16,5248]{1,0:T(8,128)(2,1)S(1)}, u32[]{:S(2)}, u32[]{:S(2)}) collective-permute-start(bf16[16,5248]{1,0:T(8,128)(2,1)S(1)} %collective-permute-done), channel_id=1, source_target_pairs={{0,2},{1,7},{2,4},{3,1},{4,6},{5,3},{6,0},{7,5},{8,10},{9,15},{10,... | collective-permute-start | bytes 503816 | tf_op jit(solution)/shard_map/ppermute | solution.py:38
  24.4 10.5 %collective-permute-start.3 = (bf16[16,5248]{1,0:T(8,128)(2,1)}, bf16[16,5248]{1,0:T(8,128)(2,1)S(1)}, u32[]{:S(2)}, u32[]{:S(2)}) collective-permute-start(bf16[16,5248]{1,0:T(8,128)(2,1)} %pack.1), channel_id=1, source_target_pairs={{0,6},{1,3},{2,0},{3,5},{4,2},{5,7},{6,4},{7,1},{8,14},{9,11},{10,... | collective-permute-start | bytes 503816 | tf_op jit(solution)/shard_map/ppermute | solution.py:38
  25.2 16.4 %collective-permute-start.10 = (bf16[16,13824]{1,0:T(8,128)(2,1)}, bf16[16,13824]{1,0:T(8,128)(2,1)S(1)}, u32[]{:S(2)}, u32[]{:S(2)}) collective-permute-start(bf16[16,13824]{1,0:T(8,128)(2,1)} %collective-permute-done.2.refs_1_), channel_id=1, source_target_pairs={{0,2},{1,7},{2,4},{3,1},{4,6},{5,3},{6,0},{7,5},{8,10},{9,15},{10,... | collective-permute-start | bytes 1327112 | tf_op jit(solution)/shard_map/ppermute | solution.py:38
  27.9 12.9 %collective-permute-start.11 = (bf16[16,13824]{1,0:T(8,128)(2,1)}, bf16[16,13824]{1,0:T(8,128)(2,1)S(1)}, u32[]{:S(2)}, u32[]{:S(2)}) collective-permute-start(bf16[16,13824]{1,0:T(8,128)(2,1)} %collective-permute-done.7.refs_4_), channel_id=1, source_target_pairs={{0,6},{1,3},{2,0},{3,5},{4,2},{5,7},{6,4},{7,1},{8,14},{9,11},{10,... | collective-permute-start | bytes 1327112 | tf_op jit(solution)/shard_map/ppermute | solution.py:38
  27.9 22.8 %collective-permute-start.9 = (bf16[16,13824]{1,0:T(8,128)(2,1)}, bf16[16,13824]{1,0:T(8,128)(2,1)}, u32[]{:S(2)}, u32[]{:S(2)}) collective-permute-start(bf16[16,13824]{1,0:T(8,128)(2,1)} %collective-permute-done.7.refs_4_), channel_id=1, source_target_pairs={{0,8},{1,25},{2,10},{3,27},{4,12},{5,29},{6,14},{7,31},{8,16},{9,1... | collective-permute-start | bytes 1327112 | tf_op jit(solution)/shard_map/ppermute | solution.py:38
  34.9 15.8 %collective-permute-start.14 = (bf16[16,13824]{1,0:T(8,128)(2,1)}, bf16[16,13824]{1,0:T(8,128)(2,1)S(1)}, u32[]{:S(2)}, u32[]{:S(2)}) collective-permute-start(bf16[16,13824]{1,0:T(8,128)(2,1)} %collective-permute-done.12.refs_8_), channel_id=1, source_target_pairs={{0,2},{1,7},{2,4},{3,1},{4,6},{5,3},{6,0},{7,5},{8,10},{9,15},{10,... | collective-permute-start | bytes 1327112 | tf_op jit(solution)/shard_map/ppermute | solution.py:38
  38.5 22.1 %collective-permute-start.8 = (bf16[64,5248]{1,0:T(8,128)(2,1)S(1)}, bf16[64,5248]{1,0:T(8,128)(2,1)}, u32[]{:S(2)}, u32[]{:S(2)}) collective-permute-start(bf16[64,5248]{1,0:T(8,128)(2,1)S(1)} %pad_maximum_fusion.refs_0_), channel_id=1, source_target_pairs={{0,8},{1,25},{2,10},{3,27},{4,12},{5,29},{6,14},{7,31},{8,16},{9,1... | collective-permute-start | bytes 2015240 | tf_op jit(solution)/shard_map/ppermute | solution.py:38
  50.7 8.5 %collective-permute-start.13 = (bf16[16,13824]{1,0:T(8,128)(2,1)}, bf16[16,13824]{1,0:T(8,128)(2,1)S(1)}, u32[]{:S(2)}, u32[]{:S(2)}) collective-permute-start(bf16[16,13824]{1,0:T(8,128)(2,1)} %collective-permute-done.9.refs_12_), channel_id=1, source_target_pairs={{0,2},{1,7},{2,4},{3,1},{4,6},{5,3},{6,0},{7,5},{8,10},{9,15},{10,... | collective-permute-start | bytes 1327112 | tf_op jit(solution)/shard_map/ppermute | solution.py:38
  50.7 17.9 %collective-permute-start.19 = (bf16[16,13824]{1,0:T(8,128)(2,1)S(1)}, bf16[16,13824]{1,0:T(8,128)(2,1)S(1)}, u32[]{:S(2)}, u32[]{:S(2)}) collective-permute-start(bf16[16,13824]{1,0:T(8,128)(2,1)S(1)} %collective-permute-done.14.refs_9_), channel_id=1, source_target_pairs={{0,2},{1,7},{2,4},{3,1},{4,6},{5,3},{6,0},{7,5},{8,10},{9,15},{10,... | collective-permute-start | bytes 1327112 | tf_op jit(solution)/shard_map/ppermute | solution.py:38
  55.5 21.2 %collective-permute-start.18 = (bf16[16,13824]{1,0:T(8,128)(2,1)}, bf16[16,13824]{1,0:T(8,128)(2,1)}, u32[]{:S(2)}, u32[]{:S(2)}) collective-permute-start(bf16[16,13824]{1,0:T(8,128)(2,1)} %collective-permute-done.9.refs_12_), channel_id=1, source_target_pairs={{0,6},{1,3},{2,0},{3,5},{4,2},{5,7},{6,4},{7,1},{8,14},{9,11},{10,... | collective-permute-start | bytes 1327112 | tf_op jit(solution)/shard_map/ppermute | solution.py:38
  55.5 23.3 %collective-permute-start.17 = (bf16[16,13824]{1,0:T(8,128)(2,1)}, bf16[16,13824]{1,0:T(8,128)(2,1)}, u32[]{:S(2)}, u32[]{:S(2)}) collective-permute-start(bf16[16,13824]{1,0:T(8,128)(2,1)} %collective-permute-done.12.refs_8_), channel_id=1, source_target_pairs={{0,6},{1,3},{2,0},{3,5},{4,2},{5,7},{6,4},{7,1},{8,14},{9,11},{10,... | collective-permute-start | bytes 1327112 | tf_op jit(solution)/shard_map/ppermute | solution.py:38
  59.2 19.6 %collective-permute-start.16 = (bf16[16,13824]{1,0:T(8,128)(2,1)}, bf16[16,13824]{1,0:T(8,128)(2,1)}, u32[]{:S(2)}, u32[]{:S(2)}) collective-permute-start(bf16[16,13824]{1,0:T(8,128)(2,1)} %collective-permute-done.7.refs_4_), channel_id=1, source_target_pairs={{0,2},{1,7},{2,4},{3,1},{4,6},{5,3},{6,0},{7,5},{8,10},{9,15},{10,... | collective-permute-start | bytes 1327112 | tf_op jit(solution)/shard_map/ppermute | solution.py:38
  60.5 46.8 %collective-permute-start.15 = (bf16[64,5248]{1,0:T(8,128)(2,1)S(1)}, bf16[64,5248]{1,0:T(8,128)(2,1)}, u32[]{:S(2)}, u32[]{:S(2)}) collective-permute-start(bf16[64,5248]{1,0:T(8,128)(2,1)S(1)} %pad_maximum_fusion.refs_0_), channel_id=1, source_target_pairs={{0,24},{1,9},{2,26},{3,11},{4,28},{5,13},{6,30},{7,15},{8,0},{9,17... | collective-permute-start | bytes 2015240 | tf_op jit(solution)/shard_map/ppermute | solution.py:38
  69.4 37.9 %collective-permute-start.22 = (bf16[64,5248]{1,0:T(8,128)(2,1)}, bf16[64,5248]{1,0:T(8,128)(2,1)}, u32[]{:S(2)}, u32[]{:S(2)}) collective-permute-start(bf16[64,5248]{1,0:T(8,128)(2,1)} %collective-permute-done.8.refs_1_), channel_id=1, source_target_pairs={{0,8},{1,25},{2,10},{3,27},{4,12},{5,29},{6,14},{7,31},{8,16},{9,1... | collective-permute-start | bytes 2015240 | tf_op jit(solution)/shard_map/ppermute | solution.py:38
  76.7 12.6 %collective-permute-start.21 = (bf16[16,13824]{1,0:T(8,128)(2,1)}, bf16[16,13824]{1,0:T(8,128)(2,1)S(1)}, u32[]{:S(2)}, u32[]{:S(2)}) collective-permute-start(bf16[16,13824]{1,0:T(8,128)(2,1)} %copy-done.12), channel_id=1, source_target_pairs={{0,2},{1,7},{2,4},{3,1},{4,6},{5,3},{6,0},{7,5},{8,10},{9,15},{10,... | collective-permute-start | bytes 1327112 | tf_op jit(solution)/shard_map/ppermute | solution.py:38
  78.8 10.5 %collective-permute-start.20 = (bf16[16,13824]{1,0:T(8,128)(2,1)}, bf16[16,13824]{1,0:T(8,128)(2,1)S(1)}, u32[]{:S(2)}, u32[]{:S(2)}) collective-permute-start(bf16[16,13824]{1,0:T(8,128)(2,1)} %collective-permute-done.16.refs_5_), channel_id=1, source_target_pairs={{0,2},{1,7},{2,4},{3,1},{4,6},{5,3},{6,0},{7,5},{8,10},{9,15},{10,... | collective-permute-start | bytes 1327112 | tf_op jit(solution)/shard_map/ppermute | solution.py:38
  111.7 15.4 %all-to-all-start = ((f32[16,2,256]{2,1,0:T(2,128)}), f32[16,2,256]{2,1,0:T(2,128)S(1)}, u32[]{:S(2)}, u32[]{:S(2)}) async-start(f32[16,2,256]{2,1,0:T(2,128)} %bitcast.6), calls=%async_computation | async-start | bytes 65536 | tf_op jit(solution)/shard_map/all_to_all | solution.py:166
  128.1 14.7 %all-to-all-start.1 = ((f32[32,4,128]{2,1,0:T(4,128)}), f32[32,4,128]{2,1,0:T(4,128)S(1)}, u32[]{:S(2)}, u32[]{:S(2)}) async-start(f32[32,4,128]{2,1,0:T(4,128)} %broadcast_in_dim.61), calls=%async_computation.1 | async-start | bytes 131072 | tf_op jit(solution)/shard_map/all_to_all | solution.py:175
  (19 other events, 205.0 us)

commit v3 on v2

--- a/solution.py
+++ b/solution.py
@@ -58,6 +58,7 @@
         kernel,
         out_shape=jax.ShapeDtypeStruct((rank, width + 128), right.dtype),
         name="pack",
+        compiler_params=pltpu.CompilerParams(vmem_limit_bytes=4 << 20),
     )(right, strengths)
 
 
@@ -125,7 +126,11 @@
     z0, y0, c0 = lax.axis_index("z"), lax.axis_index("y"), lax.axis_index("c")
     layer_index = lax.axis_index("layer")
 
-    long, short = left_factors[0, 0], pack(right_factors[0, 0], strengths[0])
+    places = (z0, y0, c0, layer_index)
+    arrays = (left_factors[0, 0], right_factors[0, 0], strengths[0], acts, grads)
+    arrays, places = lax.optimization_barrier((arrays, places))
+    long, right, own_strengths, acts, grads = arrays
+    short = pack(right, own_strengths)
     held = {"z0": long, "p0": short, "y00": long}
     last = None
 
@@ -152,7 +157,8 @@
         held[task] = last = compute(task) if task[0] == "C" else after(start(task))
         if task[0] == "z":
             held[f"y{task[1]}0"] = last
-    scores = held["C1"].reshape(NZ, NY, -1)
+    scores, z0, y0, c0, layer_index = lax.optimization_barrier((held["C1"], *places))
+    scores = scores.reshape(NZ, NY, -1)
 
     steps = jnp.array(STEPS, jnp.int32)
     way = 1 - 2 * c0

time: 144 us -> 134 us (0.931)
  local copies, waits for them, and re-layouts: 16.6 us -> 7.13 us
  waiting for transfers between devices: 45.9 us -> 54.9 us
  Pallas kernels: 12.8 us -> 5.62 us
    unnamed x36 -> x16, local copies, waits for them, and re-layouts: 14 us -> 4.61 us
    ppermute x21, waiting for transfers between devices: 29 us -> 36.5 us  [hop(): return lax.ppermute(x, RING, pairs(along_z, way))]
    pallas_call x1, Pallas kernels: 7.92 us -> 3.83 us  [grad_part(): pl.pallas_call(kernel, out_shape=(jax.ShapeDtypeStruct((tokens, rows), jn...]
    ppermute x21, starting transfers between devices: 47.5 us -> 44.5 us  [hop(): return lax.ppermute(x, RING, pairs(along_z, way))]
    pallas_call x1, Pallas kernels: 1.65 us -> 0.08 us  [pack(): pl.pallas_call(kernel, out_shape=jax.ShapeDtypeStruct((rank, width + 128)...]
    ppermute x2, waiting for transfers between devices: 2.07 us -> 3.56 us  [swap(): return lax.ppermute(x, 'c', [(0, 1), (1, 0)])]
    pallas_call x1, Pallas kernels: 3.19 us -> 1.71 us  [score_part(): pl.pallas_call(kernel, out_shape=jax.ShapeDtypeStruct((rows // rank, len(...]
  transfers between devices with their start and end apart: 25 -> 25, of which waited for: 9 -> 10; matrix products, arithmetic and copies ran while one was open for 1% -> 1% of each run, Pallas kernels for 7% -> 3%
where the time goes in v3:
time: 134 us
  starting transfers between devices  64.4 us (48%)
  waiting for transfers between devices  54.9 us (41%)
  local copies, waits for them, and re-layouts  7.13 us (5%)
  Pallas kernels  5.62 us (4%)
    ppermute x21, starting transfers between devices, hop(): return lax.ppermute(x, RING, pairs(along_z, way))  44.5 us
    ppermute x21, waiting for transfers between devices, hop(): return lax.ppermute(x, RING, pairs(along_z, way))  36.5 us
    all_to_all x1, starting transfers between devices, local(): got = lax.all_to_all(sent, ('layer', 'c'), 0, 0, tiled=True)  10.7 us
    all_to_all x1, waiting for transfers between devices, local(): sums = lax.all_to_all(sums, RING, 0, 0, tiled=True)[:, :, 0]  9.19 us
    all_to_all x1, starting transfers between devices, local(): sums = lax.all_to_all(sums, RING, 0, 0, tiled=True)[:, :, 0]  5.76 us
    all_to_all x1, waiting for transfers between devices, local(): got = lax.all_to_all(sent, ('layer', 'c'), 0, 0, tiled=True)  5.63 us
    unnamed x16, local copies, waits for them, and re-layouts  4.61 us
    pallas_call x1, Pallas kernels, grad_part(): pl.pallas_call(kernel, out_shape=(jax.ShapeDtypeStruct((tokens, rows), jn...  3.83 us
  transfers between devices with their start and end apart: 25, of which 10 were waited for; matrix products, arithmetic and copies ran while one was open for 1% of the time, Pallas kernels for 3%

profile of v3, /device:TPU:1, one launch (start us, length us, event | category | flops | bytes accessed | tf_op | source)
XLA Modules:
  0.0 134.1 jit_solution(5273361049306306760)
XLA Ops:
  0.7 3.3 %collective-permute-start.5 = (bf16[256,13824]{1,0:T(8,128)(2,1)}, bf16[256,13824]{1,0:T(8,128)(2,1)S(1)}, u32[]{:S(2)}, u32[]{:S(2)}) collective-permute-start(bf16[256,13824]{1,0:T(8,128)(2,1)} %bitcast.15), channel_id=1, source_target_pairs={{0,1},{1,0},{2,3},{3,2},{4,5},{5,4},{6,7},{7,6},{8,9},{9,8},{10,11... | collective-permute-start | bytes 21233672 | tf_op jit(solution)/shard_map/ppermute | solution.py:42
  5.1 6.0 %collective-permute-start.7 = (bf16[16,13824]{1,0:T(8,128)(2,1)}, bf16[16,13824]{1,0:T(8,128)(2,1)S(1)}, u32[]{:S(2)}, u32[]{:S(2)}) collective-permute-start(bf16[16,13824]{1,0:T(8,128)(2,1)} %bitcast.20), channel_id=1, source_target_pairs={{0,8},{1,25},{2,10},{3,27},{4,12},{5,29},{6,14},{7,31},{8,16},{9,1... | collective-permute-start | bytes 1327112 | tf_op jit(solution)/shard_map/ppermute | solution.py:38
  15.3 3.6 %collective-permute-done.1.refs_5_ = bf16[256,5120]{1,0:T(8,128)(2,1)S(1)} collective-permute-done((bf16[256,5120]{1,0:T(8,128)(2,1)}, bf16[256,5120]{1,0:T(8,128)(2,1)S(1)}, u32[]{:S(2)}, u32[]{:S(2)}) %collective-permute-start.1) | collective-permute-done | bytes 2621472 | tf_op jit(solution)/shard_map/ppermute | solution.py:42
  19.9 3.5 %collective-permute-done = bf16[16,5248]{1,0:T(8,128)(2,1)S(1)} collective-permute-done((bf16[16,5248]{1,0:T(8,128)(2,1)S(1)}, bf16[16,5248]{1,0:T(8,128)(2,1)S(1)}, u32[]{:S(2)}, u32[]{:S(2)}) %collective-permute-start) | collective-permute-done | bytes 167968 | tf_op jit(solution)/shard_map/ppermute | solution.py:38
  23.4 2.1 %collective-permute-start.4 = (bf16[16,5248]{1,0:T(8,128)(2,1)S(1)}, bf16[16,5248]{1,0:T(8,128)(2,1)S(1)}, u32[]{:S(2)}, u32[]{:S(2)}) collective-permute-start(bf16[16,5248]{1,0:T(8,128)(2,1)S(1)} %collective-permute-done), channel_id=1, source_target_pairs={{0,2},{1,7},{2,4},{3,1},{4,6},{5,3},{6,0},{7,5},{8,10},{9,15},{10,... | collective-permute-start | bytes 503816 | tf_op jit(solution)/shard_map/ppermute | solution.py:38
  25.4 2.7 %collective-permute-start.10 = (bf16[16,13824]{1,0:T(8,128)(2,1)S(1)}, bf16[16,13824]{1,0:T(8,128)(2,1)S(1)}, u32[]{:S(2)}, u32[]{:S(2)}) collective-permute-start(bf16[16,13824]{1,0:T(8,128)(2,1)S(1)} %collective-permute-done.2.refs_1_), channel_id=1, source_target_pairs={{0,2},{1,7},{2,4},{3,1},{4,6},{5,3},{6,0},{7,5},{8,10},{9,15},{10,... | collective-permute-start | bytes 1327112 | tf_op jit(solution)/shard_map/ppermute | solution.py:38
  28.1 6.3 %collective-permute-start.9 = (bf16[16,13824]{1,0:T(8,128)(2,1)S(1)}, bf16[16,13824]{1,0:T(8,128)(2,1)S(1)}, u32[]{:S(2)}, u32[]{:S(2)}) collective-permute-start(bf16[16,13824]{1,0:T(8,128)(2,1)S(1)} %collective-permute-done.7.refs_4_), channel_id=1, source_target_pairs={{0,8},{1,25},{2,10},{3,27},{4,12},{5,29},{6,14},{7,31},{8,16},{9,1... | collective-permute-start | bytes 1327112 | tf_op jit(solution)/shard_map/ppermute | solution.py:38
  34.4 2.9 %collective-permute-start.14 = (bf16[16,13824]{1,0:T(8,128)(2,1)S(1)}, bf16[16,13824]{1,0:T(8,128)(2,1)S(1)}, u32[]{:S(2)}, u32[]{:S(2)}) collective-permute-start(bf16[16,13824]{1,0:T(8,128)(2,1)S(1)} %collective-permute-done.12.refs_8_), channel_id=1, source_target_pairs={{0,2},{1,7},{2,4},{3,1},{4,6},{5,3},{6,0},{7,5},{8,10},{9,15},{10,... | collective-permute-start | bytes 1327112 | tf_op jit(solution)/shard_map/ppermute | solution.py:38
  37.4 2.0 %collective-permute-start.8 = (bf16[64,5248]{1,0:T(8,128)(2,1)S(1)}, bf16[64,5248]{1,0:T(8,128)(2,1)S(1)}, u32[]{:S(2)}, u32[]{:S(2)}) collective-permute-start(bf16[64,5248]{1,0:T(8,128)(2,1)S(1)} %pad_maximum_fusion.refs_0_), channel_id=1, source_target_pairs={{0,8},{1,25},{2,10},{3,27},{4,12},{5,29},{6,14},{7,31},{8,16},{9,1... | collective-permute-start | bytes 2015240 | tf_op jit(solution)/shard_map/ppermute | solution.py:38
  39.4 13.1 %collective-permute-done.9.refs_12_ = bf16[16,13824]{1,0:T(8,128)(2,1)S(1)} collective-permute-done((bf16[16,13824]{1,0:T(8,128)(2,1)S(1)}, bf16[16,13824]{1,0:T(8,128)(2,1)S(1)}, u32[]{:S(2)}, u32[]{:S(2)}) %collective-permute-start.9) | collective-permute-done | bytes 442400 | tf_op jit(solution)/shard_map/ppermute | solution.py:38
  52.5 3.5 %collective-permute-start.13 = (bf16[16,13824]{1,0:T(8,128)(2,1)S(1)}, bf16[16,13824]{1,0:T(8,128)(2,1)S(1)}, u32[]{:S(2)}, u32[]{:S(2)}) collective-permute-start(bf16[16,13824]{1,0:T(8,128)(2,1)S(1)} %collective-permute-done.9.refs_12_), channel_id=1, source_target_pairs={{0,2},{1,7},{2,4},{3,1},{4,6},{5,3},{6,0},{7,5},{8,10},{9,15},{10,... | collective-permute-start | bytes 1327112 | tf_op jit(solution)/shard_map/ppermute | solution.py:38
  57.4 8.5 %collective-permute-done.13.refs_13_ = bf16[16,13824]{1,0:T(8,128)(2,1)S(1)} collective-permute-done((bf16[16,13824]{1,0:T(8,128)(2,1)S(1)}, bf16[16,13824]{1,0:T(8,128)(2,1)S(1)}, u32[]{:S(2)}, u32[]{:S(2)}) %collective-permute-start.13) | collective-permute-done | bytes 442400 | tf_op jit(solution)/shard_map/ppermute | solution.py:38
  66.0 3.4 %collective-permute-start.16 = (bf16[16,13824]{1,0:T(8,128)(2,1)S(1)}, bf16[16,13824]{1,0:T(8,128)(2,1)S(1)}, u32[]{:S(2)}, u32[]{:S(2)}) collective-permute-start(bf16[16,13824]{1,0:T(8,128)(2,1)S(1)} %collective-permute-done.7.refs_4_), channel_id=1, source_target_pairs={{0,2},{1,7},{2,4},{3,1},{4,6},{5,3},{6,0},{7,5},{8,10},{9,15},{10,... | collective-permute-start | bytes 1327112 | tf_op jit(solution)/shard_map/ppermute | solution.py:38
  69.4 3.2 %collective-permute-start.15 = (bf16[64,5248]{1,0:T(8,128)(2,1)S(1)}, bf16[64,5248]{1,0:T(8,128)(2,1)S(1)}, u32[]{:S(2)}, u32[]{:S(2)}) collective-permute-start(bf16[64,5248]{1,0:T(8,128)(2,1)S(1)} %pad_maximum_fusion.refs_0_), channel_id=1, source_target_pairs={{0,24},{1,9},{2,26},{3,11},{4,28},{5,13},{6,30},{7,15},{8,0},{9,17... | collective-permute-start | bytes 2015240 | tf_op jit(solution)/shard_map/ppermute | solution.py:38
  72.6 4.0 %collective-permute-start.22 = (bf16[64,5248]{1,0:T(8,128)(2,1)S(1)}, bf16[64,5248]{1,0:T(8,128)(2,1)S(1)}, u32[]{:S(2)}, u32[]{:S(2)}) collective-permute-start(bf16[64,5248]{1,0:T(8,128)(2,1)S(1)} %collective-permute-done.8.refs_1_), channel_id=1, source_target_pairs={{0,8},{1,25},{2,10},{3,27},{4,12},{5,29},{6,14},{7,31},{8,16},{9,1... | collective-permute-start | bytes 2015240 | tf_op jit(solution)/shard_map/ppermute | solution.py:38
  77.1 3.3 %collective-permute-start.20 = (bf16[16,13824]{1,0:T(8,128)(2,1)S(1)}, bf16[16,13824]{1,0:T(8,128)(2,1)S(1)}, u32[]{:S(2)}, u32[]{:S(2)}) collective-permute-start(bf16[16,13824]{1,0:T(8,128)(2,1)S(1)} %collective-permute-done.16.refs_5_), channel_id=1, source_target_pairs={{0,2},{1,7},{2,4},{3,1},{4,6},{5,3},{6,0},{7,5},{8,10},{9,15},{10,... | collective-permute-start | bytes 1327112 | tf_op jit(solution)/shard_map/ppermute | solution.py:38
  80.9 4.7 %collective-permute-done.20.refs_7_ = bf16[16,13824]{1,0:T(8,128)(2,1)S(1)} collective-permute-done((bf16[16,13824]{1,0:T(8,128)(2,1)S(1)}, bf16[16,13824]{1,0:T(8,128)(2,1)S(1)}, u32[]{:S(2)}, u32[]{:S(2)}) %collective-permute-start.20) | collective-permute-done | bytes 442400 | tf_op jit(solution)/shard_map/ppermute | solution.py:38
  85.6 4.7 %collective-permute-done.21.refs_15_ = bf16[16,13824]{1,0:T(8,128)(2,1)S(1)} collective-permute-done((bf16[16,13824]{1,0:T(8,128)(2,1)S(1)}, bf16[16,13824]{1,0:T(8,128)(2,1)S(1)}, u32[]{:S(2)}, u32[]{:S(2)}) %collective-permute-start.21) | collective-permute-done | bytes 442400 | tf_op jit(solution)/shard_map/ppermute | solution.py:38
  90.3 3.0 %copy-done.1 = bf16[1,256,13824]{2,1,0:T(8,128)(2,1)S(1)} copy-done((bf16[1,256,13824]{2,1,0:T(8,128)(2,1)S(1)}, bf16[1,256,13824]{2,1,0:T(8,128)(2,1)}, u32[]{:S(2)}) %copy-start.1) | copy-done | bytes 7077912
  93.3 3.8 %grad_part.1 = (f32[256,256]{1,0:T(8,128)S(1)}, f32[256,256]{1,0:T(8,128)S(1)}) custom-call(bf16[16,13824]{1,0:T(8,128)(2,1)S(1)} %bitcast.23, bf16[16,13824]{1,0:T(8,128)(2,1)S(1)} %collective-permute-done.2.refs_1_, bf16[16,13824]{1,0:T(8,128)(2,1)S(1)} %collective-permute-done.6.refs_2_, bf16[16,13824]{1,0:T(8,128)(2,1)S(1)} %collective-permute-done.10.refs_3_, ...), custom_call_target="tpu_custom_call" | custom-call | tf_op jit(solution)/shard_map/grad_part/pallas_call | solution.py:80
  100.2 10.7 %all-to-all-start = ((f32[16,2,256]{2,1,0:T(2,128)}), f32[16,2,256]{2,1,0:T(2,128)S(1)}, u32[]{:S(2)}, u32[]{:S(2)}) async-start(f32[16,2,256]{2,1,0:T(2,128)} %bitcast.6), calls=%async_computation | async-start | bytes 65536 | tf_op jit(solution)/shard_map/all_to_all | solution.py:172
  111.1 5.6 %all-to-all-done = f32[16,2,256]{2,1,0:T(2,128)S(1)} async-done(((f32[16,2,256]{2,1,0:T(2,128)}), f32[16,2,256]{2,1,0:T(2,128)S(1)}, u32[]{:S(2)}, u32[]{:S(2)}) %all-to-all-start) | async-done | bytes 32800 | tf_op jit(solution)/shard_map/all_to_all | solution.py:172
  117.7 5.8 %all-to-all-start.1 = ((f32[32,4,128]{2,1,0:T(4,128)}), f32[32,4,128]{2,1,0:T(4,128)S(1)}, u32[]{:S(2)}, u32[]{:S(2)}) async-start(f32[32,4,128]{2,1,0:T(4,128)} %broadcast_in_dim.61), calls=%async_computation.1 | async-start | bytes 131072 | tf_op jit(solution)/shard_map/all_to_all | solution.py:181
  124.1 9.2 %all-to-all-done.1 = f32[32,4,128]{2,1,0:T(4,128)S(1)} async-done(((f32[32,4,128]{2,1,0:T(4,128)}), f32[32,4,128]{2,1,0:T(4,128)S(1)}, u32[]{:S(2)}, u32[]{:S(2)}) %all-to-all-start.1) | async-done | bytes 65568 | tf_op jit(solution)/shard_map/all_to_all | solution.py:181
  (69 shorter events, 14.4 us)
Async XLA Ops:
  0.7 27.4 %collective-permute-start.5 = (bf16[256,13824]{1,0:T(8,128)(2,1)}, bf16[256,13824]{1,0:T(8,128)(2,1)S(1)}, u32[]{:S(2)}, u32[]{:S(2)}) collective-permute-start(bf16[256,13824]{1,0:T(8,128)(2,1)} %bitcast.15), channel_id=1, source_target_pairs={{0,1},{1,0},{2,3},{3,2},{4,5},{5,4},{6,7},{7,6},{8,9},{9,8},{10,11... | collective-permute-start | bytes 21233672 | tf_op jit(solution)/shard_map/ppermute | solution.py:42
  4.0 14.9 %collective-permute-start.1 = (bf16[256,5120]{1,0:T(8,128)(2,1)}, bf16[256,5120]{1,0:T(8,128)(2,1)S(1)}, u32[]{:S(2)}, u32[]{:S(2)}) collective-permute-start(bf16[256,5120]{1,0:T(8,128)(2,1)} %bitcast.17), channel_id=1, source_target_pairs={{0,1},{1,0},{2,3},{3,2},{4,5},{5,4},{6,7},{7,6},{8,9},{9,8},{10,11... | collective-permute-start | bytes 7864328 | tf_op jit(solution)/shard_map/ppermute | solution.py:42
  4.1 8.4 %collective-permute-start.2 = (bf16[16,13824]{1,0:T(8,128)(2,1)}, bf16[16,13824]{1,0:T(8,128)(2,1)S(1)}, u32[]{:S(2)}, u32[]{:S(2)}) collective-permute-start(bf16[16,13824]{1,0:T(8,128)(2,1)} %bitcast.19), channel_id=1, source_target_pairs={{0,2},{1,7},{2,4},{3,1},{4,6},{5,3},{6,0},{7,5},{8,10},{9,15},{10,... | collective-permute-start | bytes 1327112 | tf_op jit(solution)/shard_map/ppermute | solution.py:38
  5.1 20.3 %collective-permute-start.7 = (bf16[16,13824]{1,0:T(8,128)(2,1)}, bf16[16,13824]{1,0:T(8,128)(2,1)S(1)}, u32[]{:S(2)}, u32[]{:S(2)}) collective-permute-start(bf16[16,13824]{1,0:T(8,128)(2,1)} %bitcast.20), channel_id=1, source_target_pairs={{0,8},{1,25},{2,10},{3,27},{4,12},{5,29},{6,14},{7,31},{8,16},{9,1... | collective-permute-start | bytes 1327112 | tf_op jit(solution)/shard_map/ppermute | solution.py:38
  11.1 14.3 %collective-permute-start.6 = (bf16[16,13824]{1,0:T(8,128)(2,1)}, bf16[16,13824]{1,0:T(8,128)(2,1)S(1)}, u32[]{:S(2)}, u32[]{:S(2)}) collective-permute-start(bf16[16,13824]{1,0:T(8,128)(2,1)} %bitcast.21), channel_id=1, source_target_pairs={{0,6},{1,3},{2,0},{3,5},{4,2},{5,7},{6,4},{7,1},{8,14},{9,11},{10,... | collective-permute-start | bytes 1327112 | tf_op jit(solution)/shard_map/ppermute | solution.py:38
  12.4 21.9 %collective-permute-start.12 = (bf16[16,13824]{1,0:T(8,128)(2,1)}, bf16[16,13824]{1,0:T(8,128)(2,1)S(1)}, u32[]{:S(2)}, u32[]{:S(2)}) collective-permute-start(bf16[16,13824]{1,0:T(8,128)(2,1)} %bitcast.22), channel_id=1, source_target_pairs={{0,24},{1,9},{2,26},{3,11},{4,28},{5,13},{6,30},{7,15},{8,0},{9,17... | collective-permute-start | bytes 1327112 | tf_op jit(solution)/shard_map/ppermute | solution.py:38
  23.4 4.7 %collective-permute-start.4 = (bf16[16,5248]{1,0:T(8,128)(2,1)S(1)}, bf16[16,5248]{1,0:T(8,128)(2,1)S(1)}, u32[]{:S(2)}, u32[]{:S(2)}) collective-permute-start(bf16[16,5248]{1,0:T(8,128)(2,1)S(1)} %collective-permute-done), channel_id=1, source_target_pairs={{0,2},{1,7},{2,4},{3,1},{4,6},{5,3},{6,0},{7,5},{8,10},{9,15},{10,... | collective-permute-start | bytes 503816 | tf_op jit(solution)/shard_map/ppermute | solution.py:38
  25.4 8.9 %collective-permute-start.3 = (bf16[16,5248]{1,0:T(8,128)(2,1)S(1)}, bf16[16,5248]{1,0:T(8,128)(2,1)S(1)}, u32[]{:S(2)}, u32[]{:S(2)}) collective-permute-start(bf16[16,5248]{1,0:T(8,128)(2,1)S(1)} %pack.1), channel_id=1, source_target_pairs={{0,6},{1,3},{2,0},{3,5},{4,2},{5,7},{6,4},{7,1},{8,14},{9,11},{10,... | collective-permute-start | bytes 503816 | tf_op jit(solution)/shard_map/ppermute | solution.py:38
  25.4 13.9 %collective-permute-start.10 = (bf16[16,13824]{1,0:T(8,128)(2,1)S(1)}, bf16[16,13824]{1,0:T(8,128)(2,1)S(1)}, u32[]{:S(2)}, u32[]{:S(2)}) collective-permute-start(bf16[16,13824]{1,0:T(8,128)(2,1)S(1)} %collective-permute-done.2.refs_1_), channel_id=1, source_target_pairs={{0,2},{1,7},{2,4},{3,1},{4,6},{5,3},{6,0},{7,5},{8,10},{9,15},{10,... | collective-permute-start | bytes 1327112 | tf_op jit(solution)/shard_map/ppermute | solution.py:38
  28.1 11.2 %collective-permute-start.11 = (bf16[16,13824]{1,0:T(8,128)(2,1)S(1)}, bf16[16,13824]{1,0:T(8,128)(2,1)S(1)}, u32[]{:S(2)}, u32[]{:S(2)}) collective-permute-start(bf16[16,13824]{1,0:T(8,128)(2,1)S(1)} %collective-permute-done.7.refs_4_), channel_id=1, source_target_pairs={{0,6},{1,3},{2,0},{3,5},{4,2},{5,7},{6,4},{7,1},{8,14},{9,11},{10,... | collective-permute-start | bytes 1327112 | tf_op jit(solution)/shard_map/ppermute | solution.py:38
  28.1 24.3 %collective-permute-start.9 = (bf16[16,13824]{1,0:T(8,128)(2,1)S(1)}, bf16[16,13824]{1,0:T(8,128)(2,1)S(1)}, u32[]{:S(2)}, u32[]{:S(2)}) collective-permute-start(bf16[16,13824]{1,0:T(8,128)(2,1)S(1)} %collective-permute-done.7.refs_4_), channel_id=1, source_target_pairs={{0,8},{1,25},{2,10},{3,27},{4,12},{5,29},{6,14},{7,31},{8,16},{9,1... | collective-permute-start | bytes 1327112 | tf_op jit(solution)/shard_map/ppermute | solution.py:38
  34.4 21.5 %collective-permute-start.14 = (bf16[16,13824]{1,0:T(8,128)(2,1)S(1)}, bf16[16,13824]{1,0:T(8,128)(2,1)S(1)}, u32[]{:S(2)}, u32[]{:S(2)}) collective-permute-start(bf16[16,13824]{1,0:T(8,128)(2,1)S(1)} %collective-permute-done.12.refs_8_), channel_id=1, source_target_pairs={{0,2},{1,7},{2,4},{3,1},{4,6},{5,3},{6,0},{7,5},{8,10},{9,15},{10,... | collective-permute-start | bytes 1327112 | tf_op jit(solution)/shard_map/ppermute | solution.py:38
  37.4 32.0 %collective-permute-start.8 = (bf16[64,5248]{1,0:T(8,128)(2,1)S(1)}, bf16[64,5248]{1,0:T(8,128)(2,1)S(1)}, u32[]{:S(2)}, u32[]{:S(2)}) collective-permute-start(bf16[64,5248]{1,0:T(8,128)(2,1)S(1)} %pad_maximum_fusion.refs_0_), channel_id=1, source_target_pairs={{0,8},{1,25},{2,10},{3,27},{4,12},{5,29},{6,14},{7,31},{8,16},{9,1... | collective-permute-start | bytes 2015240 | tf_op jit(solution)/shard_map/ppermute | solution.py:38
  52.5 13.5 %collective-permute-start.13 = (bf16[16,13824]{1,0:T(8,128)(2,1)S(1)}, bf16[16,13824]{1,0:T(8,128)(2,1)S(1)}, u32[]{:S(2)}, u32[]{:S(2)}) collective-permute-start(bf16[16,13824]{1,0:T(8,128)(2,1)S(1)} %collective-permute-done.9.refs_12_), channel_id=1, source_target_pairs={{0,2},{1,7},{2,4},{3,1},{4,6},{5,3},{6,0},{7,5},{8,10},{9,15},{10,... | collective-permute-start | bytes 1327112 | tf_op jit(solution)/shard_map/ppermute | solution.py:38
  55.9 16.7 %collective-permute-start.19 = (bf16[16,13824]{1,0:T(8,128)(2,1)S(1)}, bf16[16,13824]{1,0:T(8,128)(2,1)S(1)}, u32[]{:S(2)}, u32[]{:S(2)}) collective-permute-start(bf16[16,13824]{1,0:T(8,128)(2,1)S(1)} %collective-permute-done.14.refs_9_), channel_id=1, source_target_pairs={{0,2},{1,7},{2,4},{3,1},{4,6},{5,3},{6,0},{7,5},{8,10},{9,15},{10,... | collective-permute-start | bytes 1327112 | tf_op jit(solution)/shard_map/ppermute | solution.py:38
  56.0 20.7 %collective-permute-start.18 = (bf16[16,13824]{1,0:T(8,128)(2,1)S(1)}, bf16[16,13824]{1,0:T(8,128)(2,1)S(1)}, u32[]{:S(2)}, u32[]{:S(2)}) collective-permute-start(bf16[16,13824]{1,0:T(8,128)(2,1)S(1)} %collective-permute-done.9.refs_12_), channel_id=1, source_target_pairs={{0,6},{1,3},{2,0},{3,5},{4,2},{5,7},{6,4},{7,1},{8,14},{9,11},{10,... | collective-permute-start | bytes 1327112 | tf_op jit(solution)/shard_map/ppermute | solution.py:38
  57.4 19.7 %collective-permute-start.17 = (bf16[16,13824]{1,0:T(8,128)(2,1)S(1)}, bf16[16,13824]{1,0:T(8,128)(2,1)S(1)}, u32[]{:S(2)}, u32[]{:S(2)}) collective-permute-start(bf16[16,13824]{1,0:T(8,128)(2,1)S(1)} %collective-permute-done.12.refs_8_), channel_id=1, source_target_pairs={{0,6},{1,3},{2,0},{3,5},{4,2},{5,7},{6,4},{7,1},{8,14},{9,11},{10,... | collective-permute-start | bytes 1327112 | tf_op jit(solution)/shard_map/ppermute | solution.py:38
  66.0 11.1 %collective-permute-start.16 = (bf16[16,13824]{1,0:T(8,128)(2,1)S(1)}, bf16[16,13824]{1,0:T(8,128)(2,1)S(1)}, u32[]{:S(2)}, u32[]{:S(2)}) collective-permute-start(bf16[16,13824]{1,0:T(8,128)(2,1)S(1)} %collective-permute-done.7.refs_4_), channel_id=1, source_target_pairs={{0,2},{1,7},{2,4},{3,1},{4,6},{5,3},{6,0},{7,5},{8,10},{9,15},{10,... | collective-permute-start | bytes 1327112 | tf_op jit(solution)/shard_map/ppermute | solution.py:38
  69.4 27.8 %collective-permute-start.15 = (bf16[64,5248]{1,0:T(8,128)(2,1)S(1)}, bf16[64,5248]{1,0:T(8,128)(2,1)S(1)}, u32[]{:S(2)}, u32[]{:S(2)}) collective-permute-start(bf16[64,5248]{1,0:T(8,128)(2,1)S(1)} %pad_maximum_fusion.refs_0_), channel_id=1, source_target_pairs={{0,24},{1,9},{2,26},{3,11},{4,28},{5,13},{6,30},{7,15},{8,0},{9,17... | collective-permute-start | bytes 2015240 | tf_op jit(solution)/shard_map/ppermute | solution.py:38
  72.6 24.6 %collective-permute-start.22 = (bf16[64,5248]{1,0:T(8,128)(2,1)S(1)}, bf16[64,5248]{1,0:T(8,128)(2,1)S(1)}, u32[]{:S(2)}, u32[]{:S(2)}) collective-permute-start(bf16[64,5248]{1,0:T(8,128)(2,1)S(1)} %collective-permute-done.8.refs_1_), channel_id=1, source_target_pairs={{0,8},{1,25},{2,10},{3,27},{4,12},{5,29},{6,14},{7,31},{8,16},{9,1... | collective-permute-start | bytes 2015240 | tf_op jit(solution)/shard_map/ppermute | solution.py:38
  77.1 8.5 %collective-permute-start.20 = (bf16[16,13824]{1,0:T(8,128)(2,1)S(1)}, bf16[16,13824]{1,0:T(8,128)(2,1)S(1)}, u32[]{:S(2)}, u32[]{:S(2)}) collective-permute-start(bf16[16,13824]{1,0:T(8,128)(2,1)S(1)} %collective-permute-done.16.refs_5_), channel_id=1, source_target_pairs={{0,2},{1,7},{2,4},{3,1},{4,6},{5,3},{6,0},{7,5},{8,10},{9,15},{10,... | collective-permute-start | bytes 1327112 | tf_op jit(solution)/shard_map/ppermute | solution.py:38
  80.3 10.0 %collective-permute-start.21 = (bf16[16,13824]{1,0:T(8,128)(2,1)S(1)}, bf16[16,13824]{1,0:T(8,128)(2,1)S(1)}, u32[]{:S(2)}, u32[]{:S(2)}) collective-permute-start(bf16[16,13824]{1,0:T(8,128)(2,1)S(1)} %collective-permute-done.13.refs_13_), channel_id=1, source_target_pairs={{0,2},{1,7},{2,4},{3,1},{4,6},{5,3},{6,0},{7,5},{8,10},{9,15},{10,... | collective-permute-start | bytes 1327112 | tf_op jit(solution)/shard_map/ppermute | solution.py:38
  100.2 16.5 %all-to-all-start = ((f32[16,2,256]{2,1,0:T(2,128)}), f32[16,2,256]{2,1,0:T(2,128)S(1)}, u32[]{:S(2)}, u32[]{:S(2)}) async-start(f32[16,2,256]{2,1,0:T(2,128)} %bitcast.6), calls=%async_computation | async-start | bytes 65536 | tf_op jit(solution)/shard_map/all_to_all | solution.py:172
  117.7 15.6 %all-to-all-start.1 = ((f32[32,4,128]{2,1,0:T(4,128)}), f32[32,4,128]{2,1,0:T(4,128)S(1)}, u32[]{:S(2)}, u32[]{:S(2)}) async-start(f32[32,4,128]{2,1,0:T(4,128)} %broadcast_in_dim.61), calls=%async_computation.1 | async-start | bytes 131072 | tf_op jit(solution)/shard_map/all_to_all | solution.py:181
  (9 other events, 228.5 us)

commit v4 on v3

--- a/solution.py
+++ b/solution.py
@@ -13,8 +13,10 @@
 VMEM = 12 << 20
 PLAN = (
     "y01", "ga", "p1", "z1", "y02", "gg", "p3", "p2", "z2", "y12", "y03", "z3", "y21", "y31",
-    "b1", "y23", "y32", "y22", "y11", "y13", "y33", "C0", "b2", "b3", "C1",
+    "b1", "y23", "y32", "y22", "y11", "C0", "y13", "y33", "C1", "b2", "b3", "C2",
 )
+BLOCKS = tuple(f"y{i}{j}" for i in range(NZ) for j in range(NY))
+LATE = ("y13", "y33")
 STEPS = (0, 1, -1, 2)
 
 
@@ -73,44 +75,57 @@
             total = None
             for k in range(0, depth, step):
                 factors = jnp.concatenate([r[:, k : k + step] for r in block_refs], axis=0)
-                part = contract(rest[s][:, k : k + step], factors)
+                part = contract(factors, rest[s][:, k : k + step])
                 total = part if total is None else total + part
             out_ref[...] = total
 
     return pl.pallas_call(
         kernel,
-        out_shape=(jax.ShapeDtypeStruct((tokens, rows), jnp.float32),) * len(sources),
+        out_shape=(jax.ShapeDtypeStruct((rows, tokens), jnp.float32),) * len(sources),
         name="grad_part",
         compiler_params=pltpu.CompilerParams(vmem_limit_bytes=VMEM),
+        cost_estimate=pl.CostEstimate(
+            flops=1, bytes_accessed=1, transcendentals=0
+        ),
     )(*blocks, *sources)
 
 
-def score_part(bundles, sources, grad_parts, rank):
+def score_part(bundles, sources, early, late, rank):
     tokens, depth = sources[0].shape
     rows = sum(x.shape[0] for x in bundles)
     step = depth // 4
+    count = len(sources)
 
     def kernel(*refs):
         bundle_refs, rest = refs[: len(bundles)], refs[len(bundles) : -1]
         out_ref = refs[-1]
         weight = jnp.concatenate([r[:, depth:] for r in bundle_refs], axis=0)
         weight = weight.astype(jnp.float32)[:, :1]
-        for s in range(len(sources)):
+        for s in range(count):
             total = None
             for k in range(0, depth, step):
                 factors = jnp.concatenate([r[:, k : k + step] for r in bundle_refs], axis=0)
-                part = contract(rest[s][:, k : k + step], factors)
+                part = contract(factors, rest[s][:, k : k + step])
                 total = part if total is None else total + part
-            weighted = (total * rest[len(sources) + s][...]).T * weight
+            early_ref, late_ref = rest[count + s], rest[2 * count + s]
+            pieces, e, l = [], 0, 0
+            for key in BLOCKS:
+                if key in LATE:
+                    pieces.append(late_ref[l : l + rank, :])
+                    l += rank
+                else:
+                    pieces.append(early_ref[e : e + rank, :])
+                    e += rank
+            weighted = total * jnp.concatenate(pieces, axis=0) * weight
             mine = slice(s * tokens, (s + 1) * tokens)
             out_ref[:, mine] = weighted.reshape(rows // rank, rank, tokens).sum(axis=1)
 
     return pl.pallas_call(
         kernel,
-        out_shape=jax.ShapeDtypeStruct((rows // rank, len(sources) * tokens), jnp.float32),
+        out_shape=jax.ShapeDtypeStruct((rows // rank, count * tokens), jnp.float32),
         name="score_part",
         compiler_params=pltpu.CompilerParams(vmem_limit_bytes=VMEM),
-    )(*bundles, *sources, *grad_parts)
+    )(*bundles, *sources, *early, *late)
 
 
 def contract(a, b):
@@ -144,11 +159,12 @@
         return hop(held[from_task], task[0] in "zb", WAY[count])
 
     def compute(task):
-        if task == "C0":
-            blocks = [held[f"y{i}{j}"] for i in range(NZ) for j in range(NY)]
-            return grad_part(blocks, [grads, held["gg"]])
-        bundles = [held[f"b{i}"] for i in range(NZ)]
-        return score_part(bundles, [acts, held["ga"]], held["C0"], rank)
+        if task == "C2":
+            bundles = [held[f"b{i}"] for i in range(NZ)]
+            return score_part(bundles, [acts, held["ga"]], held["C0"], held["C1"], rank)
+        blocks = [held[key] for key in BLOCKS if (key in LATE) == (task == "C1")]
+        blocks[0] = after(blocks[0])
+        return grad_part(blocks, [grads, held["gg"]])
 
     def after(x):
         return x if last is None else lax.optimization_barrier((x, last))[0]
@@ -157,7 +173,7 @@
         held[task] = last = compute(task) if task[0] == "C" else after(start(task))
         if task[0] == "z":
             held[f"y{task[1]}0"] = last
-    scores, z0, y0, c0, layer_index = lax.optimization_barrier((held["C1"], *places))
+    scores, z0, y0, c0, layer_index = lax.optimization_barrier((held["C2"], *places))
     scores = scores.reshape(NZ, NY, -1)
 
     steps = jnp.array(STEPS, jnp.int32)

time: 134 us -> 132 us (0.985)
  waiting for transfers between devices: 54.9 us -> 50.3 us
  Pallas kernels: 5.62 us -> 10.1 us
  starting transfers between devices: 64.4 us -> 61.7 us
    ppermute x21, waiting for transfers between devices: 36.5 us -> 31.9 us  [hop(): return lax.ppermute(x, RING, pairs(along_z, way))]
    pallas_call x2 -> x3, Pallas kernels: 5.54 us -> 9.97 us  [the longest x2 8.38 us: grad_part(): pl.pallas_call(kernel, out_shape=(jax.ShapeDtypeStruct((rows, tokens), jn...]
    all_to_all x1, starting transfers between devices: 10.7 us -> 8.09 us  [local(): got = lax.all_to_all(sent, ('layer', 'c'), 0, 0, tiled=True)]
  transfers between devices with their start and end apart: 25 -> 25, of which waited for: 10 -> 10; matrix products, arithmetic and copies ran while one was open for 1% -> 1% of each run, Pallas kernels for 3% -> 6%
where the time goes in v4:
time: 132 us; the launch traced here: 131 us
  starting transfers between devices  61.7 us (47%)
  waiting for transfers between devices  50.3 us (38%)
  Pallas kernels  10.1 us (8%)
  local copies, waits for them, and re-layouts  7.14 us (5%)
    ppermute x21, starting transfers between devices, hop(): return lax.ppermute(x, RING, pairs(along_z, way))  44.5 us
    ppermute x21, waiting for transfers between devices, hop(): return lax.ppermute(x, RING, pairs(along_z, way))  31.9 us
    all_to_all x1, waiting for transfers between devices, local(): sums = lax.all_to_all(sums, RING, 0, 0, tiled=True)[:, :, 0]  9.19 us
    pallas_call x2, Pallas kernels, grad_part(): pl.pallas_call(kernel, out_shape=(jax.ShapeDtypeStruct((rows, tokens), jn...  8.38 us
    all_to_all x1, starting transfers between devices, local(): got = lax.all_to_all(sent, ('layer', 'c'), 0, 0, tiled=True)  8.09 us
    all_to_all x1, starting transfers between devices, local(): sums = lax.all_to_all(sums, RING, 0, 0, tiled=True)[:, :, 0]  5.76 us
    all_to_all x1, waiting for transfers between devices, local(): got = lax.all_to_all(sent, ('layer', 'c'), 0, 0, tiled=True)  5.63 us
    unnamed x16, local copies, waits for them, and re-layouts  4.61 us
  transfers between devices with their start and end apart: 25, of which 10 were waited for; matrix products, arithmetic and copies ran while one was open for 1% of the time, Pallas kernels for 6%

profile of v4, /device:TPU:1, one launch (start us, length us, event | category | flops | bytes accessed | tf_op | source)
XLA Modules:
  0.0 131.4 jit_solution(3934491601748495817)
XLA Ops:
  0.7 3.3 %collective-permute-start.5 = (bf16[256,13824]{1,0:T(8,128)(2,1)}, bf16[256,13824]{1,0:T(8,128)(2,1)S(1)}, u32[]{:S(2)}, u32[]{:S(2)}) collective-permute-start(bf16[256,13824]{1,0:T(8,128)(2,1)} %bitcast.15), channel_id=1, source_target_pairs={{0,1},{1,0},{2,3},{3,2},{4,5},{5,4},{6,7},{7,6},{8,9},{9,8},{10,11... | collective-permute-start | bytes 21233672 | tf_op jit(solution)/shard_map/ppermute | solution.py:44
  5.1 6.0 %collective-permute-start.7 = (bf16[16,13824]{1,0:T(8,128)(2,1)}, bf16[16,13824]{1,0:T(8,128)(2,1)S(1)}, u32[]{:S(2)}, u32[]{:S(2)}) collective-permute-start(bf16[16,13824]{1,0:T(8,128)(2,1)} %bitcast.21), channel_id=1, source_target_pairs={{0,8},{1,25},{2,10},{3,27},{4,12},{5,29},{6,14},{7,31},{8,16},{9,1... | collective-permute-start | bytes 1327112 | tf_op jit(solution)/shard_map/ppermute | solution.py:40
  15.3 3.6 %collective-permute-done.1.refs_5_ = bf16[256,5120]{1,0:T(8,128)(2,1)S(1)} collective-permute-done((bf16[256,5120]{1,0:T(8,128)(2,1)}, bf16[256,5120]{1,0:T(8,128)(2,1)S(1)}, u32[]{:S(2)}, u32[]{:S(2)}) %collective-permute-start.1) | collective-permute-done | bytes 2621472 | tf_op jit(solution)/shard_map/ppermute | solution.py:44
  19.9 3.5 %collective-permute-done = bf16[16,5248]{1,0:T(8,128)(2,1)S(1)} collective-permute-done((bf16[16,5248]{1,0:T(8,128)(2,1)S(1)}, bf16[16,5248]{1,0:T(8,128)(2,1)S(1)}, u32[]{:S(2)}, u32[]{:S(2)}) %collective-permute-start) | collective-permute-done | bytes 167968 | tf_op jit(solution)/shard_map/ppermute | solution.py:40
  23.4 2.1 %collective-permute-start.4 = (bf16[16,5248]{1,0:T(8,128)(2,1)S(1)}, bf16[16,5248]{1,0:T(8,128)(2,1)S(1)}, u32[]{:S(2)}, u32[]{:S(2)}) collective-permute-start(bf16[16,5248]{1,0:T(8,128)(2,1)S(1)} %collective-permute-done), channel_id=1, source_target_pairs={{0,2},{1,7},{2,4},{3,1},{4,6},{5,3},{6,0},{7,5},{8,10},{9,15},{10,... | collective-permute-start | bytes 503816 | tf_op jit(solution)/shard_map/ppermute | solution.py:40
  25.4 2.7 %collective-permute-start.10 = (bf16[16,13824]{1,0:T(8,128)(2,1)S(1)}, bf16[16,13824]{1,0:T(8,128)(2,1)S(1)}, u32[]{:S(2)}, u32[]{:S(2)}) collective-permute-start(bf16[16,13824]{1,0:T(8,128)(2,1)S(1)} %collective-permute-done.2.refs_1_), channel_id=1, source_target_pairs={{0,2},{1,7},{2,4},{3,1},{4,6},{5,3},{6,0},{7,5},{8,10},{9,15},{10,... | collective-permute-start | bytes 1327112 | tf_op jit(solution)/shard_map/ppermute | solution.py:40
  28.1 6.3 %collective-permute-start.9 = (bf16[16,13824]{1,0:T(8,128)(2,1)S(1)}, bf16[16,13824]{1,0:T(8,128)(2,1)S(1)}, u32[]{:S(2)}, u32[]{:S(2)}) collective-permute-start(bf16[16,13824]{1,0:T(8,128)(2,1)S(1)} %collective-permute-done.7.refs_4_), channel_id=1, source_target_pairs={{0,8},{1,25},{2,10},{3,27},{4,12},{5,29},{6,14},{7,31},{8,16},{9,1... | collective-permute-start | bytes 1327112 | tf_op jit(solution)/shard_map/ppermute | solution.py:40
  34.4 2.9 %collective-permute-start.14 = (bf16[16,13824]{1,0:T(8,128)(2,1)S(1)}, bf16[16,13824]{1,0:T(8,128)(2,1)S(1)}, u32[]{:S(2)}, u32[]{:S(2)}) collective-permute-start(bf16[16,13824]{1,0:T(8,128)(2,1)S(1)} %collective-permute-done.12.refs_7_), channel_id=1, source_target_pairs={{0,2},{1,7},{2,4},{3,1},{4,6},{5,3},{6,0},{7,5},{8,10},{9,15},{10,... | collective-permute-start | bytes 1327112 | tf_op jit(solution)/shard_map/ppermute | solution.py:40
  39.4 13.1 %collective-permute-done.9.refs_11_ = bf16[16,13824]{1,0:T(8,128)(2,1)S(1)} collective-permute-done((bf16[16,13824]{1,0:T(8,128)(2,1)S(1)}, bf16[16,13824]{1,0:T(8,128)(2,1)S(1)}, u32[]{:S(2)}, u32[]{:S(2)}) %collective-permute-start.9) | collective-permute-done | bytes 442400 | tf_op jit(solution)/shard_map/ppermute | solution.py:40
  52.5 3.5 %collective-permute-start.13 = (bf16[16,13824]{1,0:T(8,128)(2,1)S(1)}, bf16[16,13824]{1,0:T(8,128)(2,1)S(1)}, u32[]{:S(2)}, u32[]{:S(2)}) collective-permute-start(bf16[16,13824]{1,0:T(8,128)(2,1)S(1)} %collective-permute-done.9.refs_11_), channel_id=1, source_target_pairs={{0,2},{1,7},{2,4},{3,1},{4,6},{5,3},{6,0},{7,5},{8,10},{9,15},{10,... | collective-permute-start | bytes 1327112 | tf_op jit(solution)/shard_map/ppermute | solution.py:40
  57.4 8.5 %collective-permute-done.13.refs_12_ = bf16[16,13824]{1,0:T(8,128)(2,1)S(1)} collective-permute-done((bf16[16,13824]{1,0:T(8,128)(2,1)S(1)}, bf16[16,13824]{1,0:T(8,128)(2,1)S(1)}, u32[]{:S(2)}, u32[]{:S(2)}) %collective-permute-start.13) | collective-permute-done | bytes 442400 | tf_op jit(solution)/shard_map/ppermute | solution.py:40
  66.0 3.4 %collective-permute-start.16 = (bf16[16,13824]{1,0:T(8,128)(2,1)S(1)}, bf16[16,13824]{1,0:T(8,128)(2,1)S(1)}, u32[]{:S(2)}, u32[]{:S(2)}) collective-permute-start(bf16[16,13824]{1,0:T(8,128)(2,1)S(1)} %collective-permute-done.7.refs_4_), channel_id=1, source_target_pairs={{0,2},{1,7},{2,4},{3,1},{4,6},{5,3},{6,0},{7,5},{8,10},{9,15},{10,... | collective-permute-start | bytes 1327112 | tf_op jit(solution)/shard_map/ppermute | solution.py:40
  69.4 3.2 %collective-permute-start.15 = (bf16[64,5248]{1,0:T(8,128)(2,1)S(1)}, bf16[64,5248]{1,0:T(8,128)(2,1)S(1)}, u32[]{:S(2)}, u32[]{:S(2)}) collective-permute-start(bf16[64,5248]{1,0:T(8,128)(2,1)S(1)} %pad_maximum_fusion.refs_0_), channel_id=1, source_target_pairs={{0,24},{1,9},{2,26},{3,11},{4,28},{5,13},{6,30},{7,15},{8,0},{9,17... | collective-permute-start | bytes 2015240 | tf_op jit(solution)/shard_map/ppermute | solution.py:40
  72.6 4.0 %collective-permute-start.22 = (bf16[64,5248]{1,0:T(8,128)(2,1)S(1)}, bf16[64,5248]{1,0:T(8,128)(2,1)S(1)}, u32[]{:S(2)}, u32[]{:S(2)}) collective-permute-start(bf16[64,5248]{1,0:T(8,128)(2,1)S(1)} %collective-permute-done.8.refs_1_), channel_id=1, source_target_pairs={{0,8},{1,25},{2,10},{3,27},{4,12},{5,29},{6,14},{7,31},{8,16},{9,1... | collective-permute-start | bytes 2015240 | tf_op jit(solution)/shard_map/ppermute | solution.py:40
  77.1 3.3 %collective-permute-start.20 = (bf16[16,13824]{1,0:T(8,128)(2,1)S(1)}, bf16[16,13824]{1,0:T(8,128)(2,1)S(1)}, u32[]{:S(2)}, u32[]{:S(2)}) collective-permute-start(bf16[16,13824]{1,0:T(8,128)(2,1)S(1)} %collective-permute-done.16.refs_5_), channel_id=1, source_target_pairs={{0,2},{1,7},{2,4},{3,1},{4,6},{5,3},{6,0},{7,5},{8,10},{9,15},{10,... | collective-permute-start | bytes 1327112 | tf_op jit(solution)/shard_map/ppermute | solution.py:40
  80.9 3.0 %copy-done.1 = bf16[1,256,13824]{2,1,0:T(8,128)(2,1)S(1)} copy-done((bf16[1,256,13824]{2,1,0:T(8,128)(2,1)S(1)}, bf16[1,256,13824]{2,1,0:T(8,128)(2,1)}, u32[]{:S(2)}) %copy-start.1) | copy-done | bytes 7077912
  83.9 4.2 %grad_part.2 = (f32[224,256]{1,0:T(8,128)S(1)}, f32[224,256]{1,0:T(8,128)S(1)}) custom-call(bf16[16,13824]{1,0:T(8,128)(2,1)S(1)} %bitcast.24, bf16[16,13824]{1,0:T(8,128)(2,1)S(1)} %collective-permute-done.2.refs_1_, bf16[16,13824]{1,0:T(8,128)(2,1)S(1)} %collective-permute-done.6.refs_2_, bf16[16,13824]{1,0:T(8,128)(2,1)S(1)} %collective-permute-done.10.refs_3_, ...), custom_call_target="tpu_custom_call" | custom-call | flops 1 | bytes 1 | tf_op jit(solution)/shard_map/grad_part/pallas_call | solution.py:82
  88.1 2.3 %collective-permute-done.21.refs_1_ = bf16[16,13824]{1,0:T(8,128)(2,1)S(1)} collective-permute-done((bf16[16,13824]{1,0:T(8,128)(2,1)S(1)}, bf16[16,13824]{1,0:T(8,128)(2,1)S(1)}, u32[]{:S(2)}, u32[]{:S(2)}) %collective-permute-start.21) | collective-permute-done | bytes 442400 | tf_op jit(solution)/shard_map/ppermute | solution.py:40
  90.3 4.2 %grad_part.3 = (f32[32,256]{1,0:T(8,128)S(1)}, f32[32,256]{1,0:T(8,128)S(1)}) custom-call(bf16[16,13824]{1,0:T(8,128)(2,1)S(1)} %collective-permute-done.20.refs_0_, bf16[16,13824]{1,0:T(8,128)(2,1)S(1)} %collective-permute-done.21.refs_1_, bf16[256,13824]{1,0:T(8,128)(2,1)S(1)} %bitcast.17, bf16[256,13824]{1,0:T(8,128)(2,1)S(1)} %collective-permute-done.5.refs_15_.refs_3_), custom_call_target="tpu_custom_call" | custom-call | flops 1 | bytes 1 | tf_op jit(solution)/shard_map/grad_part/pallas_call | solution.py:82
  94.6 2.7 %collective-permute-done.22.refs_3_ = bf16[64,5248]{1,0:T(8,128)(2,1)S(1)} collective-permute-done((bf16[64,5248]{1,0:T(8,128)(2,1)S(1)}, bf16[64,5248]{1,0:T(8,128)(2,1)S(1)}, u32[]{:S(2)}, u32[]{:S(2)}) %collective-permute-start.22) | collective-permute-done | bytes 671776 | tf_op jit(solution)/shard_map/ppermute | solution.py:40
  100.0 8.1 %all-to-all-start = ((f32[16,2,256]{2,1,0:T(2,128)}), f32[16,2,256]{2,1,0:T(2,128)S(1)}, u32[]{:S(2)}, u32[]{:S(2)}) async-start(f32[16,2,256]{2,1,0:T(2,128)} %bitcast.6), calls=%async_computation | async-start | bytes 65536 | tf_op jit(solution)/shard_map/all_to_all | solution.py:188
  108.3 5.6 %all-to-all-done = f32[16,2,256]{2,1,0:T(2,128)S(1)} async-done(((f32[16,2,256]{2,1,0:T(2,128)}), f32[16,2,256]{2,1,0:T(2,128)S(1)}, u32[]{:S(2)}, u32[]{:S(2)}) %all-to-all-start) | async-done | bytes 32800 | tf_op jit(solution)/shard_map/all_to_all | solution.py:188
  115.0 5.8 %all-to-all-start.1 = ((f32[32,4,128]{2,1,0:T(4,128)}), f32[32,4,128]{2,1,0:T(4,128)S(1)}, u32[]{:S(2)}, u32[]{:S(2)}) async-start(f32[32,4,128]{2,1,0:T(4,128)} %broadcast_in_dim.61), calls=%async_computation.1 | async-start | bytes 131072 | tf_op jit(solution)/shard_map/all_to_all | solution.py:197
  121.3 9.2 %all-to-all-done.1 = f32[32,4,128]{2,1,0:T(4,128)S(1)} async-done(((f32[32,4,128]{2,1,0:T(4,128)}), f32[32,4,128]{2,1,0:T(4,128)S(1)}, u32[]{:S(2)}, u32[]{:S(2)}) %all-to-all-start.1) | async-done | bytes 65568 | tf_op jit(solution)/shard_map/all_to_all | solution.py:197
  (70 shorter events, 16.2 us)
Async XLA Ops:
  0.7 27.4 %collective-permute-start.5 = (bf16[256,13824]{1,0:T(8,128)(2,1)}, bf16[256,13824]{1,0:T(8,128)(2,1)S(1)}, u32[]{:S(2)}, u32[]{:S(2)}) collective-permute-start(bf16[256,13824]{1,0:T(8,128)(2,1)} %bitcast.15), channel_id=1, source_target_pairs={{0,1},{1,0},{2,3},{3,2},{4,5},{5,4},{6,7},{7,6},{8,9},{9,8},{10,11... | collective-permute-start | bytes 21233672 | tf_op jit(solution)/shard_map/ppermute | solution.py:44
  4.0 14.9 %collective-permute-start.1 = (bf16[256,5120]{1,0:T(8,128)(2,1)}, bf16[256,5120]{1,0:T(8,128)(2,1)S(1)}, u32[]{:S(2)}, u32[]{:S(2)}) collective-permute-start(bf16[256,5120]{1,0:T(8,128)(2,1)} %bitcast.18), channel_id=1, source_target_pairs={{0,1},{1,0},{2,3},{3,2},{4,5},{5,4},{6,7},{7,6},{8,9},{9,8},{10,11... | collective-permute-start | bytes 7864328 | tf_op jit(solution)/shard_map/ppermute | solution.py:44
  4.1 8.4 %collective-permute-start.2 = (bf16[16,13824]{1,0:T(8,128)(2,1)}, bf16[16,13824]{1,0:T(8,128)(2,1)S(1)}, u32[]{:S(2)}, u32[]{:S(2)}) collective-permute-start(bf16[16,13824]{1,0:T(8,128)(2,1)} %bitcast.20), channel_id=1, source_target_pairs={{0,2},{1,7},{2,4},{3,1},{4,6},{5,3},{6,0},{7,5},{8,10},{9,15},{10,... | collective-permute-start | bytes 1327112 | tf_op jit(solution)/shard_map/ppermute | solution.py:40
  5.1 20.3 %collective-permute-start.7 = (bf16[16,13824]{1,0:T(8,128)(2,1)}, bf16[16,13824]{1,0:T(8,128)(2,1)S(1)}, u32[]{:S(2)}, u32[]{:S(2)}) collective-permute-start(bf16[16,13824]{1,0:T(8,128)(2,1)} %bitcast.21), channel_id=1, source_target_pairs={{0,8},{1,25},{2,10},{3,27},{4,12},{5,29},{6,14},{7,31},{8,16},{9,1... | collective-permute-start | bytes 1327112 | tf_op jit(solution)/shard_map/ppermute | solution.py:40
  11.1 14.3 %collective-permute-start.6 = (bf16[16,13824]{1,0:T(8,128)(2,1)}, bf16[16,13824]{1,0:T(8,128)(2,1)S(1)}, u32[]{:S(2)}, u32[]{:S(2)}) collective-permute-start(bf16[16,13824]{1,0:T(8,128)(2,1)} %bitcast.22), channel_id=1, source_target_pairs={{0,6},{1,3},{2,0},{3,5},{4,2},{5,7},{6,4},{7,1},{8,14},{9,11},{10,... | collective-permute-start | bytes 1327112 | tf_op jit(solution)/shard_map/ppermute | solution.py:40
  12.4 21.9 %collective-permute-start.12 = (bf16[16,13824]{1,0:T(8,128)(2,1)}, bf16[16,13824]{1,0:T(8,128)(2,1)S(1)}, u32[]{:S(2)}, u32[]{:S(2)}) collective-permute-start(bf16[16,13824]{1,0:T(8,128)(2,1)} %bitcast.23), channel_id=1, source_target_pairs={{0,24},{1,9},{2,26},{3,11},{4,28},{5,13},{6,30},{7,15},{8,0},{9,17... | collective-permute-start | bytes 1327112 | tf_op jit(solution)/shard_map/ppermute | solution.py:40
  23.4 4.7 %collective-permute-start.4 = (bf16[16,5248]{1,0:T(8,128)(2,1)S(1)}, bf16[16,5248]{1,0:T(8,128)(2,1)S(1)}, u32[]{:S(2)}, u32[]{:S(2)}) collective-permute-start(bf16[16,5248]{1,0:T(8,128)(2,1)S(1)} %collective-permute-done), channel_id=1, source_target_pairs={{0,2},{1,7},{2,4},{3,1},{4,6},{5,3},{6,0},{7,5},{8,10},{9,15},{10,... | collective-permute-start | bytes 503816 | tf_op jit(solution)/shard_map/ppermute | solution.py:40
  25.4 8.9 %collective-permute-start.3 = (bf16[16,5248]{1,0:T(8,128)(2,1)S(1)}, bf16[16,5248]{1,0:T(8,128)(2,1)S(1)}, u32[]{:S(2)}, u32[]{:S(2)}) collective-permute-start(bf16[16,5248]{1,0:T(8,128)(2,1)S(1)} %pack.1), channel_id=1, source_target_pairs={{0,6},{1,3},{2,0},{3,5},{4,2},{5,7},{6,4},{7,1},{8,14},{9,11},{10,... | collective-permute-start | bytes 503816 | tf_op jit(solution)/shard_map/ppermute | solution.py:40
  25.4 13.9 %collective-permute-start.10 = (bf16[16,13824]{1,0:T(8,128)(2,1)S(1)}, bf16[16,13824]{1,0:T(8,128)(2,1)S(1)}, u32[]{:S(2)}, u32[]{:S(2)}) collective-permute-start(bf16[16,13824]{1,0:T(8,128)(2,1)S(1)} %collective-permute-done.2.refs_1_), channel_id=1, source_target_pairs={{0,2},{1,7},{2,4},{3,1},{4,6},{5,3},{6,0},{7,5},{8,10},{9,15},{10,... | collective-permute-start | bytes 1327112 | tf_op jit(solution)/shard_map/ppermute | solution.py:40
  28.1 11.2 %collective-permute-start.11 = (bf16[16,13824]{1,0:T(8,128)(2,1)S(1)}, bf16[16,13824]{1,0:T(8,128)(2,1)S(1)}, u32[]{:S(2)}, u32[]{:S(2)}) collective-permute-start(bf16[16,13824]{1,0:T(8,128)(2,1)S(1)} %collective-permute-done.7.refs_4_), channel_id=1, source_target_pairs={{0,6},{1,3},{2,0},{3,5},{4,2},{5,7},{6,4},{7,1},{8,14},{9,11},{10,... | collective-permute-start | bytes 1327112 | tf_op jit(solution)/shard_map/ppermute | solution.py:40
  28.1 24.3 %collective-permute-start.9 = (bf16[16,13824]{1,0:T(8,128)(2,1)S(1)}, bf16[16,13824]{1,0:T(8,128)(2,1)S(1)}, u32[]{:S(2)}, u32[]{:S(2)}) collective-permute-start(bf16[16,13824]{1,0:T(8,128)(2,1)S(1)} %collective-permute-done.7.refs_4_), channel_id=1, source_target_pairs={{0,8},{1,25},{2,10},{3,27},{4,12},{5,29},{6,14},{7,31},{8,16},{9,1... | collective-permute-start | bytes 1327112 | tf_op jit(solution)/shard_map/ppermute | solution.py:40
  34.4 21.5 %collective-permute-start.14 = (bf16[16,13824]{1,0:T(8,128)(2,1)S(1)}, bf16[16,13824]{1,0:T(8,128)(2,1)S(1)}, u32[]{:S(2)}, u32[]{:S(2)}) collective-permute-start(bf16[16,13824]{1,0:T(8,128)(2,1)S(1)} %collective-permute-done.12.refs_7_), channel_id=1, source_target_pairs={{0,2},{1,7},{2,4},{3,1},{4,6},{5,3},{6,0},{7,5},{8,10},{9,15},{10,... | collective-permute-start | bytes 1327112 | tf_op jit(solution)/shard_map/ppermute | solution.py:40
  37.4 32.0 %collective-permute-start.8 = (bf16[64,5248]{1,0:T(8,128)(2,1)S(1)}, bf16[64,5248]{1,0:T(8,128)(2,1)S(1)}, u32[]{:S(2)}, u32[]{:S(2)}) collective-permute-start(bf16[64,5248]{1,0:T(8,128)(2,1)S(1)} %pad_maximum_fusion.refs_0_), channel_id=1, source_target_pairs={{0,8},{1,25},{2,10},{3,27},{4,12},{5,29},{6,14},{7,31},{8,16},{9,1... | collective-permute-start | bytes 2015240 | tf_op jit(solution)/shard_map/ppermute | solution.py:40
  52.5 13.5 %collective-permute-start.13 = (bf16[16,13824]{1,0:T(8,128)(2,1)S(1)}, bf16[16,13824]{1,0:T(8,128)(2,1)S(1)}, u32[]{:S(2)}, u32[]{:S(2)}) collective-permute-start(bf16[16,13824]{1,0:T(8,128)(2,1)S(1)} %collective-permute-done.9.refs_11_), channel_id=1, source_target_pairs={{0,2},{1,7},{2,4},{3,1},{4,6},{5,3},{6,0},{7,5},{8,10},{9,15},{10,... | collective-permute-start | bytes 1327112 | tf_op jit(solution)/shard_map/ppermute | solution.py:40
  55.9 16.7 %collective-permute-start.19 = (bf16[16,13824]{1,0:T(8,128)(2,1)S(1)}, bf16[16,13824]{1,0:T(8,128)(2,1)S(1)}, u32[]{:S(2)}, u32[]{:S(2)}) collective-permute-start(bf16[16,13824]{1,0:T(8,128)(2,1)S(1)} %collective-permute-done.14.refs_8_), channel_id=1, source_target_pairs={{0,2},{1,7},{2,4},{3,1},{4,6},{5,3},{6,0},{7,5},{8,10},{9,15},{10,... | collective-permute-start | bytes 1327112 | tf_op jit(solution)/shard_map/ppermute | solution.py:40
  56.0 20.7 %collective-permute-start.18 = (bf16[16,13824]{1,0:T(8,128)(2,1)S(1)}, bf16[16,13824]{1,0:T(8,128)(2,1)S(1)}, u32[]{:S(2)}, u32[]{:S(2)}) collective-permute-start(bf16[16,13824]{1,0:T(8,128)(2,1)S(1)} %collective-permute-done.9.refs_11_), channel_id=1, source_target_pairs={{0,6},{1,3},{2,0},{3,5},{4,2},{5,7},{6,4},{7,1},{8,14},{9,11},{10,... | collective-permute-start | bytes 1327112 | tf_op jit(solution)/shard_map/ppermute | solution.py:40
  57.4 19.7 %collective-permute-start.17 = (bf16[16,13824]{1,0:T(8,128)(2,1)S(1)}, bf16[16,13824]{1,0:T(8,128)(2,1)S(1)}, u32[]{:S(2)}, u32[]{:S(2)}) collective-permute-start(bf16[16,13824]{1,0:T(8,128)(2,1)S(1)} %collective-permute-done.12.refs_7_), channel_id=1, source_target_pairs={{0,6},{1,3},{2,0},{3,5},{4,2},{5,7},{6,4},{7,1},{8,14},{9,11},{10,... | collective-permute-start | bytes 1327112 | tf_op jit(solution)/shard_map/ppermute | solution.py:40
  66.0 11.1 %collective-permute-start.16 = (bf16[16,13824]{1,0:T(8,128)(2,1)S(1)}, bf16[16,13824]{1,0:T(8,128)(2,1)S(1)}, u32[]{:S(2)}, u32[]{:S(2)}) collective-permute-start(bf16[16,13824]{1,0:T(8,128)(2,1)S(1)} %collective-permute-done.7.refs_4_), channel_id=1, source_target_pairs={{0,2},{1,7},{2,4},{3,1},{4,6},{5,3},{6,0},{7,5},{8,10},{9,15},{10,... | collective-permute-start | bytes 1327112 | tf_op jit(solution)/shard_map/ppermute | solution.py:40
  69.4 25.1 %collective-permute-start.15 = (bf16[64,5248]{1,0:T(8,128)(2,1)S(1)}, bf16[64,5248]{1,0:T(8,128)(2,1)S(1)}, u32[]{:S(2)}, u32[]{:S(2)}) collective-permute-start(bf16[64,5248]{1,0:T(8,128)(2,1)S(1)} %pad_maximum_fusion.refs_0_), channel_id=1, source_target_pairs={{0,24},{1,9},{2,26},{3,11},{4,28},{5,13},{6,30},{7,15},{8,0},{9,17... | collective-permute-start | bytes 2015240 | tf_op jit(solution)/shard_map/ppermute | solution.py:40
  72.6 24.6 %collective-permute-start.22 = (bf16[64,5248]{1,0:T(8,128)(2,1)S(1)}, bf16[64,5248]{1,0:T(8,128)(2,1)S(1)}, u32[]{:S(2)}, u32[]{:S(2)}) collective-permute-start(bf16[64,5248]{1,0:T(8,128)(2,1)S(1)} %collective-permute-done.8.refs_1_), channel_id=1, source_target_pairs={{0,8},{1,25},{2,10},{3,27},{4,12},{5,29},{6,14},{7,31},{8,16},{9,1... | collective-permute-start | bytes 2015240 | tf_op jit(solution)/shard_map/ppermute | solution.py:40
  77.1 11.0 %collective-permute-start.20 = (bf16[16,13824]{1,0:T(8,128)(2,1)S(1)}, bf16[16,13824]{1,0:T(8,128)(2,1)S(1)}, u32[]{:S(2)}, u32[]{:S(2)}) collective-permute-start(bf16[16,13824]{1,0:T(8,128)(2,1)S(1)} %collective-permute-done.16.refs_5_), channel_id=1, source_target_pairs={{0,2},{1,7},{2,4},{3,1},{4,6},{5,3},{6,0},{7,5},{8,10},{9,15},{10,... | collective-permute-start | bytes 1327112 | tf_op jit(solution)/shard_map/ppermute | solution.py:40
  80.3 10.0 %collective-permute-start.21 = (bf16[16,13824]{1,0:T(8,128)(2,1)S(1)}, bf16[16,13824]{1,0:T(8,128)(2,1)S(1)}, u32[]{:S(2)}, u32[]{:S(2)}) collective-permute-start(bf16[16,13824]{1,0:T(8,128)(2,1)S(1)} %collective-permute-done.13.refs_12_), channel_id=1, source_target_pairs={{0,2},{1,7},{2,4},{3,1},{4,6},{5,3},{6,0},{7,5},{8,10},{9,15},{10,... | collective-permute-start | bytes 1327112 | tf_op jit(solution)/shard_map/ppermute | solution.py:40
  100.0 13.9 %all-to-all-start = ((f32[16,2,256]{2,1,0:T(2,128)}), f32[16,2,256]{2,1,0:T(2,128)S(1)}, u32[]{:S(2)}, u32[]{:S(2)}) async-start(f32[16,2,256]{2,1,0:T(2,128)} %bitcast.6), calls=%async_computation | async-start | bytes 65536 | tf_op jit(solution)/shard_map/all_to_all | solution.py:188
  115.0 15.6 %all-to-all-start.1 = ((f32[32,4,128]{2,1,0:T(4,128)}), f32[32,4,128]{2,1,0:T(4,128)S(1)}, u32[]{:S(2)}, u32[]{:S(2)}) async-start(f32[32,4,128]{2,1,0:T(4,128)} %broadcast_in_dim.61), calls=%async_computation.1 | async-start | bytes 131072 | tf_op jit(solution)/shard_map/all_to_all | solution.py:197
  (9 other events, 221.7 us)

commit v5 on v4

--- a/solution.py
+++ b/solution.py
@@ -12,7 +12,7 @@
 RING = ("z", "y", "c")
 VMEM = 12 << 20
 PLAN = (
-    "y01", "ga", "p1", "z1", "y02", "gg", "p3", "p2", "z2", "y12", "y03", "z3", "y21", "y31",
+    "p1", "y01", "ga", "z1", "y02", "gg", "p3", "p2", "z2", "y12", "y03", "z3", "y21", "y31",
     "b1", "y23", "y32", "y22", "y11", "C0", "y13", "y33", "C1", "b2", "b3", "C2",
 )
 BLOCKS = tuple(f"y{i}{j}" for i in range(NZ) for j in range(NY))

time: 132 us -> 130 us (0.985)
  waiting for transfers between devices: 50.3 us -> 43.8 us
  starting transfers between devices: 61.7 us -> 66.9 us
    all_to_all x1, starting transfers between devices: 8.09 us -> 19.3 us  [local(): got = lax.all_to_all(sent, ('layer', 'c'), 0, 0, tiled=True)]
    ppermute x21, starting transfers between devices: 44.5 us -> 37.9 us  [hop(): return lax.ppermute(x, RING, pairs(along_z, way))]
    ppermute x2, waiting for transfers between devices: 3.56 us -> 0.01 us  [swap(): return lax.ppermute(x, 'c', [(0, 1), (1, 0)])]
    ppermute x21, waiting for transfers between devices: 31.9 us -> 28.9 us  [hop(): return lax.ppermute(x, RING, pairs(along_z, way))]
  transfers between devices with their start and end apart: 25 -> 25, of which waited for: 10 -> 12; matrix products, arithmetic and copies ran while one was open for 1% -> 1% of each run, Pallas kernels for 6% -> 7%
where the time goes in v5:
time: 130 us
  starting transfers between devices  66.9 us (51%)
  waiting for transfers between devices  43.8 us (34%)
  Pallas kernels  10 us (8%)
  local copies, waits for them, and re-layouts  7.13 us (5%)
    ppermute x21, starting transfers between devices, hop(): return lax.ppermute(x, RING, pairs(along_z, way))  37.9 us
    ppermute x21, waiting for transfers between devices, hop(): return lax.ppermute(x, RING, pairs(along_z, way))  28.9 us
    all_to_all x1, starting transfers between devices, local(): got = lax.all_to_all(sent, ('layer', 'c'), 0, 0, tiled=True)  19.3 us
    all_to_all x1, waiting for transfers between devices, local(): sums = lax.all_to_all(sums, RING, 0, 0, tiled=True)[:, :, 0]  9.19 us
    pallas_call x2, Pallas kernels, grad_part(): pl.pallas_call(kernel, out_shape=(jax.ShapeDtypeStruct((rows, tokens), jn...  8.38 us
    all_to_all x1, starting transfers between devices, local(): sums = lax.all_to_all(sums, RING, 0, 0, tiled=True)[:, :, 0]  6.32 us
    all_to_all x1, waiting for transfers between devices, local(): got = lax.all_to_all(sent, ('layer', 'c'), 0, 0, tiled=True)  5.63 us
    unnamed x16, local copies, waits for them, and re-layouts  4.61 us
  transfers between devices with their start and end apart: 25, of which 12 were waited for; matrix products, arithmetic and copies ran while one was open for 1% of the time, Pallas kernels for 7%

profile of v5, /device:TPU:1, one launch (start us, length us, event | category | flops | bytes accessed | tf_op | source)
XLA Modules:
  0.0 130.0 jit_solution(7454201350377996293)
XLA Ops:
  0.7 3.3 %collective-permute-start.3 = (bf16[256,13824]{1,0:T(8,128)(2,1)}, bf16[256,13824]{1,0:T(8,128)(2,1)S(1)}, u32[]{:S(2)}, u32[]{:S(2)}) collective-permute-start(bf16[256,13824]{1,0:T(8,128)(2,1)} %bitcast.15), channel_id=1, source_target_pairs={{0,1},{1,0},{2,3},{3,2},{4,5},{5,4},{6,7},{7,6},{8,9},{9,8},{10,11... | collective-permute-start | bytes 21233672 | tf_op jit(solution)/shard_map/ppermute | solution.py:44
  7.2 6.0 %collective-permute-start.5 = (bf16[16,13824]{1,0:T(8,128)(2,1)}, bf16[16,13824]{1,0:T(8,128)(2,1)S(1)}, u32[]{:S(2)}, u32[]{:S(2)}) collective-permute-start(bf16[16,13824]{1,0:T(8,128)(2,1)} %bitcast.21), channel_id=1, source_target_pairs={{0,8},{1,25},{2,10},{3,27},{4,12},{5,29},{6,14},{7,31},{8,16},{9,1... | collective-permute-start | bytes 1327112 | tf_op jit(solution)/shard_map/ppermute | solution.py:40
  14.3 1.9 %collective-permute-start.12 = (bf16[16,13824]{1,0:T(8,128)(2,1)}, bf16[16,13824]{1,0:T(8,128)(2,1)S(1)}, u32[]{:S(2)}, u32[]{:S(2)}) collective-permute-start(bf16[16,13824]{1,0:T(8,128)(2,1)} %bitcast.23), channel_id=1, source_target_pairs={{0,24},{1,9},{2,26},{3,11},{4,28},{5,13},{6,30},{7,15},{8,0},{9,17... | collective-permute-start | bytes 1327112 | tf_op jit(solution)/shard_map/ppermute | solution.py:40
  16.1 5.5 %collective-permute-done.5.refs_4_ = bf16[16,13824]{1,0:T(8,128)(2,1)S(1)} collective-permute-done((bf16[16,13824]{1,0:T(8,128)(2,1)}, bf16[16,13824]{1,0:T(8,128)(2,1)S(1)}, u32[]{:S(2)}, u32[]{:S(2)}) %collective-permute-start.5) | collective-permute-done | bytes 442400 | tf_op jit(solution)/shard_map/ppermute | solution.py:40
  21.6 2.4 %collective-permute-start.1 = (bf16[16,5248]{1,0:T(8,128)(2,1)S(1)}, bf16[16,5248]{1,0:T(8,128)(2,1)S(1)}, u32[]{:S(2)}, u32[]{:S(2)}) collective-permute-start(bf16[16,5248]{1,0:T(8,128)(2,1)S(1)} %pack.1), channel_id=1, source_target_pairs={{0,6},{1,3},{2,0},{3,5},{4,2},{5,7},{6,4},{7,1},{8,14},{9,11},{10,... | collective-permute-start | bytes 503816 | tf_op jit(solution)/shard_map/ppermute | solution.py:40
  25.5 1.5 %collective-permute-done.2 = bf16[16,5248]{1,0:T(8,128)(2,1)S(1)} collective-permute-done((bf16[16,5248]{1,0:T(8,128)(2,1)S(1)}, bf16[16,5248]{1,0:T(8,128)(2,1)S(1)}, u32[]{:S(2)}, u32[]{:S(2)}) %collective-permute-start.2) | collective-permute-done | bytes 167968 | tf_op jit(solution)/shard_map/ppermute | solution.py:40
  27.0 4.8 %collective-permute-start.9 = (bf16[16,13824]{1,0:T(8,128)(2,1)S(1)}, bf16[16,13824]{1,0:T(8,128)(2,1)S(1)}, u32[]{:S(2)}, u32[]{:S(2)}) collective-permute-start(bf16[16,13824]{1,0:T(8,128)(2,1)S(1)} %collective-permute-done.5.refs_4_), channel_id=1, source_target_pairs={{0,8},{1,25},{2,10},{3,27},{4,12},{5,29},{6,14},{7,31},{8,16},{9,1... | collective-permute-start | bytes 1327112 | tf_op jit(solution)/shard_map/ppermute | solution.py:40
  33.0 5.4 %collective-permute-start.8 = (bf16[64,5248]{1,0:T(8,128)(2,1)S(1)}, bf16[64,5248]{1,0:T(8,128)(2,1)S(1)}, u32[]{:S(2)}, u32[]{:S(2)}) collective-permute-start(bf16[64,5248]{1,0:T(8,128)(2,1)S(1)} %pad_maximum_fusion.refs_0_), channel_id=1, source_target_pairs={{0,8},{1,25},{2,10},{3,27},{4,12},{5,29},{6,14},{7,31},{8,16},{9,1... | collective-permute-start | bytes 2015240 | tf_op jit(solution)/shard_map/ppermute | solution.py:40
  38.9 2.2 %collective-permute-start.13 = (bf16[16,13824]{1,0:T(8,128)(2,1)S(1)}, bf16[16,13824]{1,0:T(8,128)(2,1)S(1)}, u32[]{:S(2)}, u32[]{:S(2)}) collective-permute-start(bf16[16,13824]{1,0:T(8,128)(2,1)S(1)} %collective-permute-done.9.refs_11_), channel_id=1, source_target_pairs={{0,2},{1,7},{2,4},{3,1},{4,6},{5,3},{6,0},{7,5},{8,10},{9,15},{10,... | collective-permute-start | bytes 1327112 | tf_op jit(solution)/shard_map/ppermute | solution.py:40
  41.1 1.9 %collective-permute-done.14.refs_8_ = bf16[16,13824]{1,0:T(8,128)(2,1)S(1)} collective-permute-done((bf16[16,13824]{1,0:T(8,128)(2,1)S(1)}, bf16[16,13824]{1,0:T(8,128)(2,1)S(1)}, u32[]{:S(2)}, u32[]{:S(2)}) %collective-permute-start.14) | collective-permute-done | bytes 442400 | tf_op jit(solution)/shard_map/ppermute | solution.py:40
  45.9 1.8 %collective-permute-done.13.refs_12_ = bf16[16,13824]{1,0:T(8,128)(2,1)S(1)} collective-permute-done((bf16[16,13824]{1,0:T(8,128)(2,1)S(1)}, bf16[16,13824]{1,0:T(8,128)(2,1)S(1)}, u32[]{:S(2)}, u32[]{:S(2)}) %collective-permute-start.13) | collective-permute-done | bytes 442400 | tf_op jit(solution)/shard_map/ppermute | solution.py:40
  47.8 2.0 %collective-permute-start.16 = (bf16[16,13824]{1,0:T(8,128)(2,1)S(1)}, bf16[16,13824]{1,0:T(8,128)(2,1)S(1)}, u32[]{:S(2)}, u32[]{:S(2)}) collective-permute-start(bf16[16,13824]{1,0:T(8,128)(2,1)S(1)} %collective-permute-done.5.refs_4_), channel_id=1, source_target_pairs={{0,2},{1,7},{2,4},{3,1},{4,6},{5,3},{6,0},{7,5},{8,10},{9,15},{10,... | collective-permute-start | bytes 1327112 | tf_op jit(solution)/shard_map/ppermute | solution.py:40
  49.8 8.8 %collective-permute-done.8.refs_1_ = bf16[64,5248]{1,0:T(8,128)(2,1)S(1)} collective-permute-done((bf16[64,5248]{1,0:T(8,128)(2,1)S(1)}, bf16[64,5248]{1,0:T(8,128)(2,1)S(1)}, u32[]{:S(2)}, u32[]{:S(2)}) %collective-permute-start.8) | collective-permute-done | bytes 671776 | tf_op jit(solution)/shard_map/ppermute | solution.py:40
  58.6 4.3 %collective-permute-start.22 = (bf16[64,5248]{1,0:T(8,128)(2,1)S(1)}, bf16[64,5248]{1,0:T(8,128)(2,1)S(1)}, u32[]{:S(2)}, u32[]{:S(2)}) collective-permute-start(bf16[64,5248]{1,0:T(8,128)(2,1)S(1)} %collective-permute-done.8.refs_1_), channel_id=1, source_target_pairs={{0,8},{1,25},{2,10},{3,27},{4,12},{5,29},{6,14},{7,31},{8,16},{9,1... | collective-permute-start | bytes 2015240 | tf_op jit(solution)/shard_map/ppermute | solution.py:40
  62.9 4.3 %collective-permute-done.17.refs_9_ = bf16[16,13824]{1,0:T(8,128)(2,1)S(1)} collective-permute-done((bf16[16,13824]{1,0:T(8,128)(2,1)S(1)}, bf16[16,13824]{1,0:T(8,128)(2,1)S(1)}, u32[]{:S(2)}, u32[]{:S(2)}) %collective-permute-start.17) | collective-permute-done | bytes 442400 | tf_op jit(solution)/shard_map/ppermute | solution.py:40
  68.3 3.0 %copy-done.1 = bf16[1,256,13824]{2,1,0:T(8,128)(2,1)S(1)} copy-done((bf16[1,256,13824]{2,1,0:T(8,128)(2,1)S(1)}, bf16[1,256,13824]{2,1,0:T(8,128)(2,1)}, u32[]{:S(2)}) %copy-start.1) | copy-done | bytes 7077912
  71.3 4.2 %grad_part.2 = (f32[224,256]{1,0:T(8,128)S(1)}, f32[224,256]{1,0:T(8,128)S(1)}) custom-call(bf16[16,13824]{1,0:T(8,128)(2,1)S(1)} %bitcast.24, bf16[16,13824]{1,0:T(8,128)(2,1)S(1)} %collective-permute-done.7.refs_1_, bf16[16,13824]{1,0:T(8,128)(2,1)S(1)} %collective-permute-done.4.refs_2_, bf16[16,13824]{1,0:T(8,128)(2,1)S(1)} %collective-permute-done.10.refs_3_, ...), custom_call_target="tpu_custom_call" | custom-call | flops 1 | bytes 1 | tf_op jit(solution)/shard_map/grad_part/pallas_call | solution.py:82
  75.5 3.9 %collective-permute-done.21.refs_1_ = bf16[16,13824]{1,0:T(8,128)(2,1)S(1)} collective-permute-done((bf16[16,13824]{1,0:T(8,128)(2,1)S(1)}, bf16[16,13824]{1,0:T(8,128)(2,1)S(1)}, u32[]{:S(2)}, u32[]{:S(2)}) %collective-permute-start.21) | collective-permute-done | bytes 442400 | tf_op jit(solution)/shard_map/ppermute | solution.py:40
  79.4 4.2 %grad_part.3 = (f32[32,256]{1,0:T(8,128)S(1)}, f32[32,256]{1,0:T(8,128)S(1)}) custom-call(bf16[16,13824]{1,0:T(8,128)(2,1)S(1)} %collective-permute-done.20.refs_0_, bf16[16,13824]{1,0:T(8,128)(2,1)S(1)} %collective-permute-done.21.refs_1_, bf16[256,13824]{1,0:T(8,128)(2,1)S(1)} %bitcast.17, bf16[256,13824]{1,0:T(8,128)(2,1)S(1)} %collective-permute-done.3.refs_15_.refs_3_), custom_call_target="tpu_custom_call" | custom-call | flops 1 | bytes 1 | tf_op jit(solution)/shard_map/grad_part/pallas_call | solution.py:82
  84.1 1.6 %score_part.1 = f32[16,512]{1,0:T(8,128)S(1)} custom-call(bf16[64,5248]{1,0:T(8,128)(2,1)S(1)} %pad_maximum_fusion.refs_0_, bf16[64,5248]{1,0:T(8,128)(2,1)S(1)} %collective-permute-done.8.refs_1_, bf16[64,5248]{1,0:T(8,128)(2,1)S(1)} %collective-permute-done.15.refs_2_, bf16[64,5248]{1,0:T(8,128)(2,1)S(1)} %collective-permute-done.22.refs_3_, ...), custom_call_target="tpu_custom_call" | custom-call | tf_op jit(solution)/shard_map/score_part/pallas_call | solution.py:123
  86.9 19.3 %all-to-all-start = ((f32[16,2,256]{2,1,0:T(2,128)}), f32[16,2,256]{2,1,0:T(2,128)S(1)}, u32[]{:S(2)}, u32[]{:S(2)}) async-start(f32[16,2,256]{2,1,0:T(2,128)} %bitcast.6), calls=%async_computation | async-start | bytes 65536 | tf_op jit(solution)/shard_map/all_to_all | solution.py:188
  106.4 5.6 %all-to-all-done = f32[16,2,256]{2,1,0:T(2,128)S(1)} async-done(((f32[16,2,256]{2,1,0:T(2,128)}), f32[16,2,256]{2,1,0:T(2,128)S(1)}, u32[]{:S(2)}, u32[]{:S(2)}) %all-to-all-start) | async-done | bytes 32800 | tf_op jit(solution)/shard_map/all_to_all | solution.py:188
  113.0 6.3 %all-to-all-start.1 = ((f32[32,4,128]{2,1,0:T(4,128)}), f32[32,4,128]{2,1,0:T(4,128)S(1)}, u32[]{:S(2)}, u32[]{:S(2)}) async-start(f32[32,4,128]{2,1,0:T(4,128)} %broadcast_in_dim.61), calls=%async_computation.1 | async-start | bytes 131072 | tf_op jit(solution)/shard_map/all_to_all | solution.py:197
  120.0 9.2 %all-to-all-done.1 = f32[32,4,128]{2,1,0:T(4,128)S(1)} async-done(((f32[32,4,128]{2,1,0:T(4,128)}), f32[32,4,128]{2,1,0:T(4,128)S(1)}, u32[]{:S(2)}, u32[]{:S(2)}) %all-to-all-start.1) | async-done | bytes 65568 | tf_op jit(solution)/shard_map/all_to_all | solution.py:197
  (70 shorter events, 15.8 us)
Async XLA Ops:
  0.7 23.9 %collective-permute-start.3 = (bf16[256,13824]{1,0:T(8,128)(2,1)}, bf16[256,13824]{1,0:T(8,128)(2,1)S(1)}, u32[]{:S(2)}, u32[]{:S(2)}) collective-permute-start(bf16[256,13824]{1,0:T(8,128)(2,1)} %bitcast.15), channel_id=1, source_target_pairs={{0,1},{1,0},{2,3},{3,2},{4,5},{5,4},{6,7},{7,6},{8,9},{9,8},{10,11... | collective-permute-start | bytes 21233672 | tf_op jit(solution)/shard_map/ppermute | solution.py:44
  4.0 17.6 %collective-permute-start.6 = (bf16[256,5120]{1,0:T(8,128)(2,1)}, bf16[256,5120]{1,0:T(8,128)(2,1)S(1)}, u32[]{:S(2)}, u32[]{:S(2)}) collective-permute-start(bf16[256,5120]{1,0:T(8,128)(2,1)} %bitcast.18), channel_id=1, source_target_pairs={{0,1},{1,0},{2,3},{3,2},{4,5},{5,4},{6,7},{7,6},{8,9},{9,8},{10,11... | collective-permute-start | bytes 7864328 | tf_op jit(solution)/shard_map/ppermute | solution.py:44
  4.1 10.2 %collective-permute-start.7 = (bf16[16,13824]{1,0:T(8,128)(2,1)}, bf16[16,13824]{1,0:T(8,128)(2,1)S(1)}, u32[]{:S(2)}, u32[]{:S(2)}) collective-permute-start(bf16[16,13824]{1,0:T(8,128)(2,1)} %bitcast.20), channel_id=1, source_target_pairs={{0,2},{1,7},{2,4},{3,1},{4,6},{5,3},{6,0},{7,5},{8,10},{9,15},{10,... | collective-permute-start | bytes 1327112 | tf_op jit(solution)/shard_map/ppermute | solution.py:40
  6.7 6.8 %collective-permute-start = (bf16[16,5248]{1,0:T(8,128)(2,1)S(1)}, bf16[16,5248]{1,0:T(8,128)(2,1)S(1)}, u32[]{:S(2)}, u32[]{:S(2)}) collective-permute-start(bf16[16,5248]{1,0:T(8,128)(2,1)S(1)} %pack.1), channel_id=1, source_target_pairs={{0,2},{1,7},{2,4},{3,1},{4,6},{5,3},{6,0},{7,5},{8,10},{9,15},{10,... | collective-permute-start | bytes 503816 | tf_op jit(solution)/shard_map/ppermute | solution.py:40
  7.2 14.3 %collective-permute-start.5 = (bf16[16,13824]{1,0:T(8,128)(2,1)}, bf16[16,13824]{1,0:T(8,128)(2,1)S(1)}, u32[]{:S(2)}, u32[]{:S(2)}) collective-permute-start(bf16[16,13824]{1,0:T(8,128)(2,1)} %bitcast.21), channel_id=1, source_target_pairs={{0,8},{1,25},{2,10},{3,27},{4,12},{5,29},{6,14},{7,31},{8,16},{9,1... | collective-permute-start | bytes 1327112 | tf_op jit(solution)/shard_map/ppermute | solution.py:40
  13.6 10.4 %collective-permute-start.4 = (bf16[16,13824]{1,0:T(8,128)(2,1)}, bf16[16,13824]{1,0:T(8,128)(2,1)S(1)}, u32[]{:S(2)}, u32[]{:S(2)}) collective-permute-start(bf16[16,13824]{1,0:T(8,128)(2,1)} %bitcast.22), channel_id=1, source_target_pairs={{0,6},{1,3},{2,0},{3,5},{4,2},{5,7},{6,4},{7,1},{8,14},{9,11},{10,... | collective-permute-start | bytes 1327112 | tf_op jit(solution)/shard_map/ppermute | solution.py:40
  14.3 17.6 %collective-permute-start.12 = (bf16[16,13824]{1,0:T(8,128)(2,1)}, bf16[16,13824]{1,0:T(8,128)(2,1)S(1)}, u32[]{:S(2)}, u32[]{:S(2)}) collective-permute-start(bf16[16,13824]{1,0:T(8,128)(2,1)} %bitcast.23), channel_id=1, source_target_pairs={{0,24},{1,9},{2,26},{3,11},{4,28},{5,13},{6,30},{7,15},{8,0},{9,17... | collective-permute-start | bytes 1327112 | tf_op jit(solution)/shard_map/ppermute | solution.py:40
  21.6 10.3 %collective-permute-start.1 = (bf16[16,5248]{1,0:T(8,128)(2,1)S(1)}, bf16[16,5248]{1,0:T(8,128)(2,1)S(1)}, u32[]{:S(2)}, u32[]{:S(2)}) collective-permute-start(bf16[16,5248]{1,0:T(8,128)(2,1)S(1)} %pack.1), channel_id=1, source_target_pairs={{0,6},{1,3},{2,0},{3,5},{4,2},{5,7},{6,4},{7,1},{8,14},{9,11},{10,... | collective-permute-start | bytes 503816 | tf_op jit(solution)/shard_map/ppermute | solution.py:40
  24.0 14.4 %collective-permute-start.10 = (bf16[16,13824]{1,0:T(8,128)(2,1)S(1)}, bf16[16,13824]{1,0:T(8,128)(2,1)S(1)}, u32[]{:S(2)}, u32[]{:S(2)}) collective-permute-start(bf16[16,13824]{1,0:T(8,128)(2,1)S(1)} %collective-permute-done.7.refs_1_), channel_id=1, source_target_pairs={{0,2},{1,7},{2,4},{3,1},{4,6},{5,3},{6,0},{7,5},{8,10},{9,15},{10,... | collective-permute-start | bytes 1327112 | tf_op jit(solution)/shard_map/ppermute | solution.py:40
  24.6 13.8 %collective-permute-start.11 = (bf16[16,13824]{1,0:T(8,128)(2,1)S(1)}, bf16[16,13824]{1,0:T(8,128)(2,1)S(1)}, u32[]{:S(2)}, u32[]{:S(2)}) collective-permute-start(bf16[16,13824]{1,0:T(8,128)(2,1)S(1)} %collective-permute-done.5.refs_4_), channel_id=1, source_target_pairs={{0,6},{1,3},{2,0},{3,5},{4,2},{5,7},{6,4},{7,1},{8,14},{9,11},{10,... | collective-permute-start | bytes 1327112 | tf_op jit(solution)/shard_map/ppermute | solution.py:40
  27.0 11.9 %collective-permute-start.9 = (bf16[16,13824]{1,0:T(8,128)(2,1)S(1)}, bf16[16,13824]{1,0:T(8,128)(2,1)S(1)}, u32[]{:S(2)}, u32[]{:S(2)}) collective-permute-start(bf16[16,13824]{1,0:T(8,128)(2,1)S(1)} %collective-permute-done.5.refs_4_), channel_id=1, source_target_pairs={{0,8},{1,25},{2,10},{3,27},{4,12},{5,29},{6,14},{7,31},{8,16},{9,1... | collective-permute-start | bytes 1327112 | tf_op jit(solution)/shard_map/ppermute | solution.py:40
  31.9 11.2 %collective-permute-start.14 = (bf16[16,13824]{1,0:T(8,128)(2,1)S(1)}, bf16[16,13824]{1,0:T(8,128)(2,1)S(1)}, u32[]{:S(2)}, u32[]{:S(2)}) collective-permute-start(bf16[16,13824]{1,0:T(8,128)(2,1)S(1)} %collective-permute-done.12.refs_7_), channel_id=1, source_target_pairs={{0,2},{1,7},{2,4},{3,1},{4,6},{5,3},{6,0},{7,5},{8,10},{9,15},{10,... | collective-permute-start | bytes 1327112 | tf_op jit(solution)/shard_map/ppermute | solution.py:40
  33.0 25.6 %collective-permute-start.8 = (bf16[64,5248]{1,0:T(8,128)(2,1)S(1)}, bf16[64,5248]{1,0:T(8,128)(2,1)S(1)}, u32[]{:S(2)}, u32[]{:S(2)}) collective-permute-start(bf16[64,5248]{1,0:T(8,128)(2,1)S(1)} %pad_maximum_fusion.refs_0_), channel_id=1, source_target_pairs={{0,8},{1,25},{2,10},{3,27},{4,12},{5,29},{6,14},{7,31},{8,16},{9,1... | collective-permute-start | bytes 2015240 | tf_op jit(solution)/shard_map/ppermute | solution.py:40
  38.9 8.8 %collective-permute-start.13 = (bf16[16,13824]{1,0:T(8,128)(2,1)S(1)}, bf16[16,13824]{1,0:T(8,128)(2,1)S(1)}, u32[]{:S(2)}, u32[]{:S(2)}) collective-permute-start(bf16[16,13824]{1,0:T(8,128)(2,1)S(1)} %collective-permute-done.9.refs_11_), channel_id=1, source_target_pairs={{0,2},{1,7},{2,4},{3,1},{4,6},{5,3},{6,0},{7,5},{8,10},{9,15},{10,... | collective-permute-start | bytes 1327112 | tf_op jit(solution)/shard_map/ppermute | solution.py:40
  43.0 15.6 %collective-permute-start.19 = (bf16[16,13824]{1,0:T(8,128)(2,1)S(1)}, bf16[16,13824]{1,0:T(8,128)(2,1)S(1)}, u32[]{:S(2)}, u32[]{:S(2)}) collective-permute-start(bf16[16,13824]{1,0:T(8,128)(2,1)S(1)} %collective-permute-done.14.refs_8_), channel_id=1, source_target_pairs={{0,2},{1,7},{2,4},{3,1},{4,6},{5,3},{6,0},{7,5},{8,10},{9,15},{10,... | collective-permute-start | bytes 1327112 | tf_op jit(solution)/shard_map/ppermute | solution.py:40
  44.3 18.7 %collective-permute-start.18 = (bf16[16,13824]{1,0:T(8,128)(2,1)S(1)}, bf16[16,13824]{1,0:T(8,128)(2,1)S(1)}, u32[]{:S(2)}, u32[]{:S(2)}) collective-permute-start(bf16[16,13824]{1,0:T(8,128)(2,1)S(1)} %collective-permute-done.9.refs_11_), channel_id=1, source_target_pairs={{0,6},{1,3},{2,0},{3,5},{4,2},{5,7},{6,4},{7,1},{8,14},{9,11},{10,... | collective-permute-start | bytes 1327112 | tf_op jit(solution)/shard_map/ppermute | solution.py:40
  44.5 22.7 %collective-permute-start.17 = (bf16[16,13824]{1,0:T(8,128)(2,1)S(1)}, bf16[16,13824]{1,0:T(8,128)(2,1)S(1)}, u32[]{:S(2)}, u32[]{:S(2)}) collective-permute-start(bf16[16,13824]{1,0:T(8,128)(2,1)S(1)} %collective-permute-done.12.refs_7_), channel_id=1, source_target_pairs={{0,6},{1,3},{2,0},{3,5},{4,2},{5,7},{6,4},{7,1},{8,14},{9,11},{10,... | collective-permute-start | bytes 1327112 | tf_op jit(solution)/shard_map/ppermute | solution.py:40
  47.8 19.4 %collective-permute-start.16 = (bf16[16,13824]{1,0:T(8,128)(2,1)S(1)}, bf16[16,13824]{1,0:T(8,128)(2,1)S(1)}, u32[]{:S(2)}, u32[]{:S(2)}) collective-permute-start(bf16[16,13824]{1,0:T(8,128)(2,1)S(1)} %collective-permute-done.5.refs_4_), channel_id=1, source_target_pairs={{0,2},{1,7},{2,4},{3,1},{4,6},{5,3},{6,0},{7,5},{8,10},{9,15},{10,... | collective-permute-start | bytes 1327112 | tf_op jit(solution)/shard_map/ppermute | solution.py:40
  58.6 25.5 %collective-permute-start.15 = (bf16[64,5248]{1,0:T(8,128)(2,1)S(1)}, bf16[64,5248]{1,0:T(8,128)(2,1)S(1)}, u32[]{:S(2)}, u32[]{:S(2)}) collective-permute-start(bf16[64,5248]{1,0:T(8,128)(2,1)S(1)} %pad_maximum_fusion.refs_0_), channel_id=1, source_target_pairs={{0,24},{1,9},{2,26},{3,11},{4,28},{5,13},{6,30},{7,15},{8,0},{9,17... | collective-permute-start | bytes 2015240 | tf_op jit(solution)/shard_map/ppermute | solution.py:40
  58.6 25.5 %collective-permute-start.22 = (bf16[64,5248]{1,0:T(8,128)(2,1)S(1)}, bf16[64,5248]{1,0:T(8,128)(2,1)S(1)}, u32[]{:S(2)}, u32[]{:S(2)}) collective-permute-start(bf16[64,5248]{1,0:T(8,128)(2,1)S(1)} %collective-permute-done.8.refs_1_), channel_id=1, source_target_pairs={{0,8},{1,25},{2,10},{3,27},{4,12},{5,29},{6,14},{7,31},{8,16},{9,1... | collective-permute-start | bytes 2015240 | tf_op jit(solution)/shard_map/ppermute | solution.py:40
  67.2 8.3 %collective-permute-start.20 = (bf16[16,13824]{1,0:T(8,128)(2,1)S(1)}, bf16[16,13824]{1,0:T(8,128)(2,1)S(1)}, u32[]{:S(2)}, u32[]{:S(2)}) collective-permute-start(bf16[16,13824]{1,0:T(8,128)(2,1)S(1)} %collective-permute-done.16.refs_5_), channel_id=1, source_target_pairs={{0,2},{1,7},{2,4},{3,1},{4,6},{5,3},{6,0},{7,5},{8,10},{9,15},{10,... | collective-permute-start | bytes 1327112 | tf_op jit(solution)/shard_map/ppermute | solution.py:40
  67.2 12.2 %collective-permute-start.21 = (bf16[16,13824]{1,0:T(8,128)(2,1)S(1)}, bf16[16,13824]{1,0:T(8,128)(2,1)S(1)}, u32[]{:S(2)}, u32[]{:S(2)}) collective-permute-start(bf16[16,13824]{1,0:T(8,128)(2,1)S(1)} %collective-permute-done.13.refs_12_), channel_id=1, source_target_pairs={{0,2},{1,7},{2,4},{3,1},{4,6},{5,3},{6,0},{7,5},{8,10},{9,15},{10,... | collective-permute-start | bytes 1327112 | tf_op jit(solution)/shard_map/ppermute | solution.py:40
  86.9 25.1 %all-to-all-start = ((f32[16,2,256]{2,1,0:T(2,128)}), f32[16,2,256]{2,1,0:T(2,128)S(1)}, u32[]{:S(2)}, u32[]{:S(2)}) async-start(f32[16,2,256]{2,1,0:T(2,128)} %bitcast.6), calls=%async_computation | async-start | bytes 65536 | tf_op jit(solution)/shard_map/all_to_all | solution.py:188
  113.0 16.1 %all-to-all-start.1 = ((f32[32,4,128]{2,1,0:T(4,128)}), f32[32,4,128]{2,1,0:T(4,128)S(1)}, u32[]{:S(2)}, u32[]{:S(2)}) async-start(f32[32,4,128]{2,1,0:T(4,128)} %broadcast_in_dim.61), calls=%async_computation.1 | async-start | bytes 131072 | tf_op jit(solution)/shard_map/all_to_all | solution.py:197
  (9 other events, 211.8 us)

commit v6 on v5

--- a/solution.py
+++ b/solution.py
@@ -193,8 +193,8 @@
     own_ids = lax.dynamic_slice_in_dim(query_ids, layer_index * own_rows, own_rows, 0)
     matches = jnp.any(own_ids[:, :, None] == train_ids[None, None, :], axis=1).astype(jnp.float32)
     seq_part = jnp.sum(own_scores * matches, axis=1) * (1.0 / math.sqrt(SEQ_LEN))
-    sums = jnp.broadcast_to(seq_part[None, :, None], (NZ * NY * NC, own_rows, 128))
-    sums = lax.all_to_all(sums, RING, 0, 0, tiled=True)[:, :, 0]
+    sums = jnp.broadcast_to(seq_part[None, None, :], (NZ * NY * NC, 1, own_rows))
+    sums = lax.all_to_all(sums, RING, 0, 0, tiled=True)[:, 0]
     intersection = sums.reshape(NZ, NY * NC, own_rows).sum(axis=1).T
     return (own_scores, intersection)
 

time: 130 us -> 130 us (level)
    unnamed x16 -> x17, local copies, waits for them, and re-layouts: 4.61 us -> 5.27 us
where the time goes in v6:
time: 130 us; the launch traced here: 129 us
  starting transfers between devices  67 us (52%)
  waiting for transfers between devices  43.3 us (33%)
  Pallas kernels  10 us (8%)
  local copies, waits for them, and re-layouts  7.53 us (6%)
    ppermute x21, starting transfers between devices, hop(): return lax.ppermute(x, RING, pairs(along_z, way))  37.9 us
    ppermute x21, waiting for transfers between devices, hop(): return lax.ppermute(x, RING, pairs(along_z, way))  28.9 us
    all_to_all x1, starting transfers between devices, local(): got = lax.all_to_all(sent, ('layer', 'c'), 0, 0, tiled=True)  19.3 us
    all_to_all x1, waiting for transfers between devices, local(): sums = lax.all_to_all(sums, RING, 0, 0, tiled=True)[:, 0]  8.73 us
    pallas_call x2, Pallas kernels, grad_part(): pl.pallas_call(kernel, out_shape=(jax.ShapeDtypeStruct((rows, tokens), jn...  8.38 us
    all_to_all x1, starting transfers between devices, local(): sums = lax.all_to_all(sums, RING, 0, 0, tiled=True)[:, 0]  6.32 us
    all_to_all x1, waiting for transfers between devices, local(): got = lax.all_to_all(sent, ('layer', 'c'), 0, 0, tiled=True)  5.63 us
    unnamed x17, local copies, waits for them, and re-layouts  5.27 us
  transfers between devices with their start and end apart: 25, of which 12 were waited for; matrix products, arithmetic and copies ran while one was open for 1% of the time, Pallas kernels for 7%

profile of v6, /device:TPU:1, one launch (start us, length us, event | category | flops | bytes accessed | tf_op | source)
XLA Modules:
  0.0 129.3 jit_solution(1332192475260491805)
XLA Ops:
  0.7 3.3 %collective-permute-start.3 = (bf16[256,13824]{1,0:T(8,128)(2,1)}, bf16[256,13824]{1,0:T(8,128)(2,1)S(1)}, u32[]{:S(2)}, u32[]{:S(2)}) collective-permute-start(bf16[256,13824]{1,0:T(8,128)(2,1)} %bitcast.15), channel_id=1, source_target_pairs={{0,1},{1,0},{2,3},{3,2},{4,5},{5,4},{6,7},{7,6},{8,9},{9,8},{10,11... | collective-permute-start | bytes 21233672 | tf_op jit(solution)/shard_map/ppermute | solution.py:44
  7.2 6.0 %collective-permute-start.5 = (bf16[16,13824]{1,0:T(8,128)(2,1)}, bf16[16,13824]{1,0:T(8,128)(2,1)S(1)}, u32[]{:S(2)}, u32[]{:S(2)}) collective-permute-start(bf16[16,13824]{1,0:T(8,128)(2,1)} %bitcast.21), channel_id=1, source_target_pairs={{0,8},{1,25},{2,10},{3,27},{4,12},{5,29},{6,14},{7,31},{8,16},{9,1... | collective-permute-start | bytes 1327112 | tf_op jit(solution)/shard_map/ppermute | solution.py:40
  14.3 1.9 %collective-permute-start.12 = (bf16[16,13824]{1,0:T(8,128)(2,1)}, bf16[16,13824]{1,0:T(8,128)(2,1)S(1)}, u32[]{:S(2)}, u32[]{:S(2)}) collective-permute-start(bf16[16,13824]{1,0:T(8,128)(2,1)} %bitcast.23), channel_id=1, source_target_pairs={{0,24},{1,9},{2,26},{3,11},{4,28},{5,13},{6,30},{7,15},{8,0},{9,17... | collective-permute-start | bytes 1327112 | tf_op jit(solution)/shard_map/ppermute | solution.py:40
  16.1 5.5 %collective-permute-done.5.refs_4_ = bf16[16,13824]{1,0:T(8,128)(2,1)S(1)} collective-permute-done((bf16[16,13824]{1,0:T(8,128)(2,1)}, bf16[16,13824]{1,0:T(8,128)(2,1)S(1)}, u32[]{:S(2)}, u32[]{:S(2)}) %collective-permute-start.5) | collective-permute-done | bytes 442400 | tf_op jit(solution)/shard_map/ppermute | solution.py:40
  21.6 2.4 %collective-permute-start.1 = (bf16[16,5248]{1,0:T(8,128)(2,1)S(1)}, bf16[16,5248]{1,0:T(8,128)(2,1)S(1)}, u32[]{:S(2)}, u32[]{:S(2)}) collective-permute-start(bf16[16,5248]{1,0:T(8,128)(2,1)S(1)} %pack.1), channel_id=1, source_target_pairs={{0,6},{1,3},{2,0},{3,5},{4,2},{5,7},{6,4},{7,1},{8,14},{9,11},{10,... | collective-permute-start | bytes 503816 | tf_op jit(solution)/shard_map/ppermute | solution.py:40
  25.5 1.5 %collective-permute-done.2 = bf16[16,5248]{1,0:T(8,128)(2,1)S(1)} collective-permute-done((bf16[16,5248]{1,0:T(8,128)(2,1)S(1)}, bf16[16,5248]{1,0:T(8,128)(2,1)S(1)}, u32[]{:S(2)}, u32[]{:S(2)}) %collective-permute-start.2) | collective-permute-done | bytes 167968 | tf_op jit(solution)/shard_map/ppermute | solution.py:40
  27.0 4.8 %collective-permute-start.9 = (bf16[16,13824]{1,0:T(8,128)(2,1)S(1)}, bf16[16,13824]{1,0:T(8,128)(2,1)S(1)}, u32[]{:S(2)}, u32[]{:S(2)}) collective-permute-start(bf16[16,13824]{1,0:T(8,128)(2,1)S(1)} %collective-permute-done.5.refs_4_), channel_id=1, source_target_pairs={{0,8},{1,25},{2,10},{3,27},{4,12},{5,29},{6,14},{7,31},{8,16},{9,1... | collective-permute-start | bytes 1327112 | tf_op jit(solution)/shard_map/ppermute | solution.py:40
  33.0 5.4 %collective-permute-start.8 = (bf16[64,5248]{1,0:T(8,128)(2,1)S(1)}, bf16[64,5248]{1,0:T(8,128)(2,1)S(1)}, u32[]{:S(2)}, u32[]{:S(2)}) collective-permute-start(bf16[64,5248]{1,0:T(8,128)(2,1)S(1)} %pad_maximum_fusion.refs_0_), channel_id=1, source_target_pairs={{0,8},{1,25},{2,10},{3,27},{4,12},{5,29},{6,14},{7,31},{8,16},{9,1... | collective-permute-start | bytes 2015240 | tf_op jit(solution)/shard_map/ppermute | solution.py:40
  38.9 2.2 %collective-permute-start.13 = (bf16[16,13824]{1,0:T(8,128)(2,1)S(1)}, bf16[16,13824]{1,0:T(8,128)(2,1)S(1)}, u32[]{:S(2)}, u32[]{:S(2)}) collective-permute-start(bf16[16,13824]{1,0:T(8,128)(2,1)S(1)} %collective-permute-done.9.refs_11_), channel_id=1, source_target_pairs={{0,2},{1,7},{2,4},{3,1},{4,6},{5,3},{6,0},{7,5},{8,10},{9,15},{10,... | collective-permute-start | bytes 1327112 | tf_op jit(solution)/shard_map/ppermute | solution.py:40
  41.1 1.9 %collective-permute-done.14.refs_8_ = bf16[16,13824]{1,0:T(8,128)(2,1)S(1)} collective-permute-done((bf16[16,13824]{1,0:T(8,128)(2,1)S(1)}, bf16[16,13824]{1,0:T(8,128)(2,1)S(1)}, u32[]{:S(2)}, u32[]{:S(2)}) %collective-permute-start.14) | collective-permute-done | bytes 442400 | tf_op jit(solution)/shard_map/ppermute | solution.py:40
  45.9 1.8 %collective-permute-done.13.refs_12_ = bf16[16,13824]{1,0:T(8,128)(2,1)S(1)} collective-permute-done((bf16[16,13824]{1,0:T(8,128)(2,1)S(1)}, bf16[16,13824]{1,0:T(8,128)(2,1)S(1)}, u32[]{:S(2)}, u32[]{:S(2)}) %collective-permute-start.13) | collective-permute-done | bytes 442400 | tf_op jit(solution)/shard_map/ppermute | solution.py:40
  47.8 2.0 %collective-permute-start.16 = (bf16[16,13824]{1,0:T(8,128)(2,1)S(1)}, bf16[16,13824]{1,0:T(8,128)(2,1)S(1)}, u32[]{:S(2)}, u32[]{:S(2)}) collective-permute-start(bf16[16,13824]{1,0:T(8,128)(2,1)S(1)} %collective-permute-done.5.refs_4_), channel_id=1, source_target_pairs={{0,2},{1,7},{2,4},{3,1},{4,6},{5,3},{6,0},{7,5},{8,10},{9,15},{10,... | collective-permute-start | bytes 1327112 | tf_op jit(solution)/shard_map/ppermute | solution.py:40
  49.8 8.8 %collective-permute-done.8.refs_1_ = bf16[64,5248]{1,0:T(8,128)(2,1)S(1)} collective-permute-done((bf16[64,5248]{1,0:T(8,128)(2,1)S(1)}, bf16[64,5248]{1,0:T(8,128)(2,1)S(1)}, u32[]{:S(2)}, u32[]{:S(2)}) %collective-permute-start.8) | collective-permute-done | bytes 671776 | tf_op jit(solution)/shard_map/ppermute | solution.py:40
  58.6 4.3 %collective-permute-start.22 = (bf16[64,5248]{1,0:T(8,128)(2,1)S(1)}, bf16[64,5248]{1,0:T(8,128)(2,1)S(1)}, u32[]{:S(2)}, u32[]{:S(2)}) collective-permute-start(bf16[64,5248]{1,0:T(8,128)(2,1)S(1)} %collective-permute-done.8.refs_1_), channel_id=1, source_target_pairs={{0,8},{1,25},{2,10},{3,27},{4,12},{5,29},{6,14},{7,31},{8,16},{9,1... | collective-permute-start | bytes 2015240 | tf_op jit(solution)/shard_map/ppermute | solution.py:40
  62.9 4.3 %collective-permute-done.17.refs_9_ = bf16[16,13824]{1,0:T(8,128)(2,1)S(1)} collective-permute-done((bf16[16,13824]{1,0:T(8,128)(2,1)S(1)}, bf16[16,13824]{1,0:T(8,128)(2,1)S(1)}, u32[]{:S(2)}, u32[]{:S(2)}) %collective-permute-start.17) | collective-permute-done | bytes 442400 | tf_op jit(solution)/shard_map/ppermute | solution.py:40
  68.3 3.0 %copy-done.1 = bf16[1,256,13824]{2,1,0:T(8,128)(2,1)S(1)} copy-done((bf16[1,256,13824]{2,1,0:T(8,128)(2,1)S(1)}, bf16[1,256,13824]{2,1,0:T(8,128)(2,1)}, u32[]{:S(2)}) %copy-start.1) | copy-done | bytes 7077912
  71.3 4.2 %grad_part.2 = (f32[224,256]{1,0:T(8,128)S(1)}, f32[224,256]{1,0:T(8,128)S(1)}) custom-call(bf16[16,13824]{1,0:T(8,128)(2,1)S(1)} %bitcast.24, bf16[16,13824]{1,0:T(8,128)(2,1)S(1)} %collective-permute-done.7.refs_1_, bf16[16,13824]{1,0:T(8,128)(2,1)S(1)} %collective-permute-done.4.refs_2_, bf16[16,13824]{1,0:T(8,128)(2,1)S(1)} %collective-permute-done.10.refs_3_, ...), custom_call_target="tpu_custom_call" | custom-call | flops 1 | bytes 1 | tf_op jit(solution)/shard_map/grad_part/pallas_call | solution.py:82
  75.5 3.9 %collective-permute-done.21.refs_1_ = bf16[16,13824]{1,0:T(8,128)(2,1)S(1)} collective-permute-done((bf16[16,13824]{1,0:T(8,128)(2,1)S(1)}, bf16[16,13824]{1,0:T(8,128)(2,1)S(1)}, u32[]{:S(2)}, u32[]{:S(2)}) %collective-permute-start.21) | collective-permute-done | bytes 442400 | tf_op jit(solution)/shard_map/ppermute | solution.py:40
  79.4 4.2 %grad_part.3 = (f32[32,256]{1,0:T(8,128)S(1)}, f32[32,256]{1,0:T(8,128)S(1)}) custom-call(bf16[16,13824]{1,0:T(8,128)(2,1)S(1)} %collective-permute-done.20.refs_0_, bf16[16,13824]{1,0:T(8,128)(2,1)S(1)} %collective-permute-done.21.refs_1_, bf16[256,13824]{1,0:T(8,128)(2,1)S(1)} %bitcast.17, bf16[256,13824]{1,0:T(8,128)(2,1)S(1)} %collective-permute-done.3.refs_15_.refs_3_), custom_call_target="tpu_custom_call" | custom-call | flops 1 | bytes 1 | tf_op jit(solution)/shard_map/grad_part/pallas_call | solution.py:82
  84.1 1.6 %score_part.1 = f32[16,512]{1,0:T(8,128)S(1)} custom-call(bf16[64,5248]{1,0:T(8,128)(2,1)S(1)} %pad_maximum_fusion.refs_0_, bf16[64,5248]{1,0:T(8,128)(2,1)S(1)} %collective-permute-done.8.refs_1_, bf16[64,5248]{1,0:T(8,128)(2,1)S(1)} %collective-permute-done.15.refs_2_, bf16[64,5248]{1,0:T(8,128)(2,1)S(1)} %collective-permute-done.22.refs_3_, ...), custom_call_target="tpu_custom_call" | custom-call | tf_op jit(solution)/shard_map/score_part/pallas_call | solution.py:123
  86.9 19.3 %all-to-all-start = ((f32[16,2,256]{2,1,0:T(2,128)}), f32[16,2,256]{2,1,0:T(2,128)S(1)}, u32[]{:S(2)}, u32[]{:S(2)}) async-start(f32[16,2,256]{2,1,0:T(2,128)} %bitcast.6), calls=%async_computation | async-start | bytes 65536 | tf_op jit(solution)/shard_map/all_to_all | solution.py:188
  106.4 5.6 %all-to-all-done = f32[16,2,256]{2,1,0:T(2,128)S(1)} async-done(((f32[16,2,256]{2,1,0:T(2,128)}), f32[16,2,256]{2,1,0:T(2,128)S(1)}, u32[]{:S(2)}, u32[]{:S(2)}) %all-to-all-start) | async-done | bytes 32800 | tf_op jit(solution)/shard_map/all_to_all | solution.py:188
  112.9 6.3 %all-to-all-start.1 = ((f32[32,1,4]{2,1,0:T(1,128)}), f32[32,1,4]{2,1,0:T(1,128)S(1)}, u32[]{:S(2)}, u32[]{:S(2)}) async-start(f32[32,1,4]{2,1,0:T(1,128)} %broadcast_in_dim.61), calls=%async_computation.1 | async-start | bytes 32768 | tf_op jit(solution)/shard_map/all_to_all | solution.py:197
  119.9 8.7 %all-to-all-done.1 = f32[32,1,4]{2,1,0:T(1,128)S(1)} async-done(((f32[32,1,4]{2,1,0:T(1,128)}), f32[32,1,4]{2,1,0:T(1,128)S(1)}, u32[]{:S(2)}, u32[]{:S(2)}) %all-to-all-start.1) | async-done | bytes 544 | tf_op jit(solution)/shard_map/all_to_all | solution.py:197
  (69 shorter events, 15.5 us)
Async XLA Ops:
  0.7 23.9 %collective-permute-start.3 = (bf16[256,13824]{1,0:T(8,128)(2,1)}, bf16[256,13824]{1,0:T(8,128)(2,1)S(1)}, u32[]{:S(2)}, u32[]{:S(2)}) collective-permute-start(bf16[256,13824]{1,0:T(8,128)(2,1)} %bitcast.15), channel_id=1, source_target_pairs={{0,1},{1,0},{2,3},{3,2},{4,5},{5,4},{6,7},{7,6},{8,9},{9,8},{10,11... | collective-permute-start | bytes 21233672 | tf_op jit(solution)/shard_map/ppermute | solution.py:44
  4.0 17.6 %collective-permute-start.6 = (bf16[256,5120]{1,0:T(8,128)(2,1)}, bf16[256,5120]{1,0:T(8,128)(2,1)S(1)}, u32[]{:S(2)}, u32[]{:S(2)}) collective-permute-start(bf16[256,5120]{1,0:T(8,128)(2,1)} %bitcast.18), channel_id=1, source_target_pairs={{0,1},{1,0},{2,3},{3,2},{4,5},{5,4},{6,7},{7,6},{8,9},{9,8},{10,11... | collective-permute-start | bytes 7864328 | tf_op jit(solution)/shard_map/ppermute | solution.py:44
  4.1 10.2 %collective-permute-start.7 = (bf16[16,13824]{1,0:T(8,128)(2,1)}, bf16[16,13824]{1,0:T(8,128)(2,1)S(1)}, u32[]{:S(2)}, u32[]{:S(2)}) collective-permute-start(bf16[16,13824]{1,0:T(8,128)(2,1)} %bitcast.20), channel_id=1, source_target_pairs={{0,2},{1,7},{2,4},{3,1},{4,6},{5,3},{6,0},{7,5},{8,10},{9,15},{10,... | collective-permute-start | bytes 1327112 | tf_op jit(solution)/shard_map/ppermute | solution.py:40
  6.7 6.8 %collective-permute-start = (bf16[16,5248]{1,0:T(8,128)(2,1)S(1)}, bf16[16,5248]{1,0:T(8,128)(2,1)S(1)}, u32[]{:S(2)}, u32[]{:S(2)}) collective-permute-start(bf16[16,5248]{1,0:T(8,128)(2,1)S(1)} %pack.1), channel_id=1, source_target_pairs={{0,2},{1,7},{2,4},{3,1},{4,6},{5,3},{6,0},{7,5},{8,10},{9,15},{10,... | collective-permute-start | bytes 503816 | tf_op jit(solution)/shard_map/ppermute | solution.py:40
  7.2 14.3 %collective-permute-start.5 = (bf16[16,13824]{1,0:T(8,128)(2,1)}, bf16[16,13824]{1,0:T(8,128)(2,1)S(1)}, u32[]{:S(2)}, u32[]{:S(2)}) collective-permute-start(bf16[16,13824]{1,0:T(8,128)(2,1)} %bitcast.21), channel_id=1, source_target_pairs={{0,8},{1,25},{2,10},{3,27},{4,12},{5,29},{6,14},{7,31},{8,16},{9,1... | collective-permute-start | bytes 1327112 | tf_op jit(solution)/shard_map/ppermute | solution.py:40
  13.6 10.4 %collective-permute-start.4 = (bf16[16,13824]{1,0:T(8,128)(2,1)}, bf16[16,13824]{1,0:T(8,128)(2,1)S(1)}, u32[]{:S(2)}, u32[]{:S(2)}) collective-permute-start(bf16[16,13824]{1,0:T(8,128)(2,1)} %bitcast.22), channel_id=1, source_target_pairs={{0,6},{1,3},{2,0},{3,5},{4,2},{5,7},{6,4},{7,1},{8,14},{9,11},{10,... | collective-permute-start | bytes 1327112 | tf_op jit(solution)/shard_map/ppermute | solution.py:40
  14.3 17.6 %collective-permute-start.12 = (bf16[16,13824]{1,0:T(8,128)(2,1)}, bf16[16,13824]{1,0:T(8,128)(2,1)S(1)}, u32[]{:S(2)}, u32[]{:S(2)}) collective-permute-start(bf16[16,13824]{1,0:T(8,128)(2,1)} %bitcast.23), channel_id=1, source_target_pairs={{0,24},{1,9},{2,26},{3,11},{4,28},{5,13},{6,30},{7,15},{8,0},{9,17... | collective-permute-start | bytes 1327112 | tf_op jit(solution)/shard_map/ppermute | solution.py:40
  21.6 10.3 %collective-permute-start.1 = (bf16[16,5248]{1,0:T(8,128)(2,1)S(1)}, bf16[16,5248]{1,0:T(8,128)(2,1)S(1)}, u32[]{:S(2)}, u32[]{:S(2)}) collective-permute-start(bf16[16,5248]{1,0:T(8,128)(2,1)S(1)} %pack.1), channel_id=1, source_target_pairs={{0,6},{1,3},{2,0},{3,5},{4,2},{5,7},{6,4},{7,1},{8,14},{9,11},{10,... | collective-permute-start | bytes 503816 | tf_op jit(solution)/shard_map/ppermute | solution.py:40
  24.0 14.4 %collective-permute-start.10 = (bf16[16,13824]{1,0:T(8,128)(2,1)S(1)}, bf16[16,13824]{1,0:T(8,128)(2,1)S(1)}, u32[]{:S(2)}, u32[]{:S(2)}) collective-permute-start(bf16[16,13824]{1,0:T(8,128)(2,1)S(1)} %collective-permute-done.7.refs_1_), channel_id=1, source_target_pairs={{0,2},{1,7},{2,4},{3,1},{4,6},{5,3},{6,0},{7,5},{8,10},{9,15},{10,... | collective-permute-start | bytes 1327112 | tf_op jit(solution)/shard_map/ppermute | solution.py:40
  24.6 13.8 %collective-permute-start.11 = (bf16[16,13824]{1,0:T(8,128)(2,1)S(1)}, bf16[16,13824]{1,0:T(8,128)(2,1)S(1)}, u32[]{:S(2)}, u32[]{:S(2)}) collective-permute-start(bf16[16,13824]{1,0:T(8,128)(2,1)S(1)} %collective-permute-done.5.refs_4_), channel_id=1, source_target_pairs={{0,6},{1,3},{2,0},{3,5},{4,2},{5,7},{6,4},{7,1},{8,14},{9,11},{10,... | collective-permute-start | bytes 1327112 | tf_op jit(solution)/shard_map/ppermute | solution.py:40
  27.0 11.9 %collective-permute-start.9 = (bf16[16,13824]{1,0:T(8,128)(2,1)S(1)}, bf16[16,13824]{1,0:T(8,128)(2,1)S(1)}, u32[]{:S(2)}, u32[]{:S(2)}) collective-permute-start(bf16[16,13824]{1,0:T(8,128)(2,1)S(1)} %collective-permute-done.5.refs_4_), channel_id=1, source_target_pairs={{0,8},{1,25},{2,10},{3,27},{4,12},{5,29},{6,14},{7,31},{8,16},{9,1... | collective-permute-start | bytes 1327112 | tf_op jit(solution)/shard_map/ppermute | solution.py:40
  31.9 11.2 %collective-permute-start.14 = (bf16[16,13824]{1,0:T(8,128)(2,1)S(1)}, bf16[16,13824]{1,0:T(8,128)(2,1)S(1)}, u32[]{:S(2)}, u32[]{:S(2)}) collective-permute-start(bf16[16,13824]{1,0:T(8,128)(2,1)S(1)} %collective-permute-done.12.refs_7_), channel_id=1, source_target_pairs={{0,2},{1,7},{2,4},{3,1},{4,6},{5,3},{6,0},{7,5},{8,10},{9,15},{10,... | collective-permute-start | bytes 1327112 | tf_op jit(solution)/shard_map/ppermute | solution.py:40
  33.0 25.6 %collective-permute-start.8 = (bf16[64,5248]{1,0:T(8,128)(2,1)S(1)}, bf16[64,5248]{1,0:T(8,128)(2,1)S(1)}, u32[]{:S(2)}, u32[]{:S(2)}) collective-permute-start(bf16[64,5248]{1,0:T(8,128)(2,1)S(1)} %pad_maximum_fusion.refs_0_), channel_id=1, source_target_pairs={{0,8},{1,25},{2,10},{3,27},{4,12},{5,29},{6,14},{7,31},{8,16},{9,1... | collective-permute-start | bytes 2015240 | tf_op jit(solution)/shard_map/ppermute | solution.py:40
  38.9 8.8 %collective-permute-start.13 = (bf16[16,13824]{1,0:T(8,128)(2,1)S(1)}, bf16[16,13824]{1,0:T(8,128)(2,1)S(1)}, u32[]{:S(2)}, u32[]{:S(2)}) collective-permute-start(bf16[16,13824]{1,0:T(8,128)(2,1)S(1)} %collective-permute-done.9.refs_11_), channel_id=1, source_target_pairs={{0,2},{1,7},{2,4},{3,1},{4,6},{5,3},{6,0},{7,5},{8,10},{9,15},{10,... | collective-permute-start | bytes 1327112 | tf_op jit(solution)/shard_map/ppermute | solution.py:40
  43.0 15.6 %collective-permute-start.19 = (bf16[16,13824]{1,0:T(8,128)(2,1)S(1)}, bf16[16,13824]{1,0:T(8,128)(2,1)S(1)}, u32[]{:S(2)}, u32[]{:S(2)}) collective-permute-start(bf16[16,13824]{1,0:T(8,128)(2,1)S(1)} %collective-permute-done.14.refs_8_), channel_id=1, source_target_pairs={{0,2},{1,7},{2,4},{3,1},{4,6},{5,3},{6,0},{7,5},{8,10},{9,15},{10,... | collective-permute-start | bytes 1327112 | tf_op jit(solution)/shard_map/ppermute | solution.py:40
  44.3 18.7 %collective-permute-start.18 = (bf16[16,13824]{1,0:T(8,128)(2,1)S(1)}, bf16[16,13824]{1,0:T(8,128)(2,1)S(1)}, u32[]{:S(2)}, u32[]{:S(2)}) collective-permute-start(bf16[16,13824]{1,0:T(8,128)(2,1)S(1)} %collective-permute-done.9.refs_11_), channel_id=1, source_target_pairs={{0,6},{1,3},{2,0},{3,5},{4,2},{5,7},{6,4},{7,1},{8,14},{9,11},{10,... | collective-permute-start | bytes 1327112 | tf_op jit(solution)/shard_map/ppermute | solution.py:40
  44.5 22.7 %collective-permute-start.17 = (bf16[16,13824]{1,0:T(8,128)(2,1)S(1)}, bf16[16,13824]{1,0:T(8,128)(2,1)S(1)}, u32[]{:S(2)}, u32[]{:S(2)}) collective-permute-start(bf16[16,13824]{1,0:T(8,128)(2,1)S(1)} %collective-permute-done.12.refs_7_), channel_id=1, source_target_pairs={{0,6},{1,3},{2,0},{3,5},{4,2},{5,7},{6,4},{7,1},{8,14},{9,11},{10,... | collective-permute-start | bytes 1327112 | tf_op jit(solution)/shard_map/ppermute | solution.py:40
  47.8 19.4 %collective-permute-start.16 = (bf16[16,13824]{1,0:T(8,128)(2,1)S(1)}, bf16[16,13824]{1,0:T(8,128)(2,1)S(1)}, u32[]{:S(2)}, u32[]{:S(2)}) collective-permute-start(bf16[16,13824]{1,0:T(8,128)(2,1)S(1)} %collective-permute-done.5.refs_4_), channel_id=1, source_target_pairs={{0,2},{1,7},{2,4},{3,1},{4,6},{5,3},{6,0},{7,5},{8,10},{9,15},{10,... | collective-permute-start | bytes 1327112 | tf_op jit(solution)/shard_map/ppermute | solution.py:40
  58.6 25.5 %collective-permute-start.15 = (bf16[64,5248]{1,0:T(8,128)(2,1)S(1)}, bf16[64,5248]{1,0:T(8,128)(2,1)S(1)}, u32[]{:S(2)}, u32[]{:S(2)}) collective-permute-start(bf16[64,5248]{1,0:T(8,128)(2,1)S(1)} %pad_maximum_fusion.refs_0_), channel_id=1, source_target_pairs={{0,24},{1,9},{2,26},{3,11},{4,28},{5,13},{6,30},{7,15},{8,0},{9,17... | collective-permute-start | bytes 2015240 | tf_op jit(solution)/shard_map/ppermute | solution.py:40
  58.6 25.5 %collective-permute-start.22 = (bf16[64,5248]{1,0:T(8,128)(2,1)S(1)}, bf16[64,5248]{1,0:T(8,128)(2,1)S(1)}, u32[]{:S(2)}, u32[]{:S(2)}) collective-permute-start(bf16[64,5248]{1,0:T(8,128)(2,1)S(1)} %collective-permute-done.8.refs_1_), channel_id=1, source_target_pairs={{0,8},{1,25},{2,10},{3,27},{4,12},{5,29},{6,14},{7,31},{8,16},{9,1... | collective-permute-start | bytes 2015240 | tf_op jit(solution)/shard_map/ppermute | solution.py:40
  67.2 8.3 %collective-permute-start.20 = (bf16[16,13824]{1,0:T(8,128)(2,1)S(1)}, bf16[16,13824]{1,0:T(8,128)(2,1)S(1)}, u32[]{:S(2)}, u32[]{:S(2)}) collective-permute-start(bf16[16,13824]{1,0:T(8,128)(2,1)S(1)} %collective-permute-done.16.refs_5_), channel_id=1, source_target_pairs={{0,2},{1,7},{2,4},{3,1},{4,6},{5,3},{6,0},{7,5},{8,10},{9,15},{10,... | collective-permute-start | bytes 1327112 | tf_op jit(solution)/shard_map/ppermute | solution.py:40
  67.2 12.2 %collective-permute-start.21 = (bf16[16,13824]{1,0:T(8,128)(2,1)S(1)}, bf16[16,13824]{1,0:T(8,128)(2,1)S(1)}, u32[]{:S(2)}, u32[]{:S(2)}) collective-permute-start(bf16[16,13824]{1,0:T(8,128)(2,1)S(1)} %collective-permute-done.13.refs_12_), channel_id=1, source_target_pairs={{0,2},{1,7},{2,4},{3,1},{4,6},{5,3},{6,0},{7,5},{8,10},{9,15},{10,... | collective-permute-start | bytes 1327112 | tf_op jit(solution)/shard_map/ppermute | solution.py:40
  86.9 25.1 %all-to-all-start = ((f32[16,2,256]{2,1,0:T(2,128)}), f32[16,2,256]{2,1,0:T(2,128)S(1)}, u32[]{:S(2)}, u32[]{:S(2)}) async-start(f32[16,2,256]{2,1,0:T(2,128)} %bitcast.6), calls=%async_computation | async-start | bytes 65536 | tf_op jit(solution)/shard_map/all_to_all | solution.py:188
  112.9 15.7 %all-to-all-start.1 = ((f32[32,1,4]{2,1,0:T(1,128)}), f32[32,1,4]{2,1,0:T(1,128)S(1)}, u32[]{:S(2)}, u32[]{:S(2)}) async-start(f32[32,1,4]{2,1,0:T(1,128)} %broadcast_in_dim.61), calls=%async_computation.1 | async-start | bytes 32768 | tf_op jit(solution)/shard_map/all_to_all | solution.py:197
  (9 other events, 211.8 us)
